TPU v7x, 256 devices: a whole 4x4x8 slice. The times are simulated.
256 devices in a mesh: section: 4 (over x), dp: 8 (over z), mp: 8 (over y, core).
Axes of the slice: x: 4, y: 4, z: 8, core: 2. Of those that a mesh axis runs over, the one named last changes fastest.
Arguments:
- query_inputs: bfloat16 [1024, 4096], P('dp', 'mp'), may hold values from -12 to 12
- section_weights: bfloat16 [16384, 4096], P('section', 'mp'), may hold values from -0.09375 to 0.09375
- head_weight: bfloat16 [4096, 4096], P(None, 'mp'), may hold values from -0.09375 to 0.09375
- passages: bfloat16 [4096, 4096], P(('section', 'dp', 'mp')), may hold values from -32 to 32
- query_cells: int32 [1024], P('dp'), may hold values from 0 to 15
- passage_cells: int32 [4096], P(('section', 'dp', 'mp')), may hold values from 0 to 15
- positives: int32 [1024], P('dp'), may hold values from 0 to 4095
- master: float32 [4096, 4096], P(('section', 'dp'), 'mp'), may hold values from -0.09375 to 0.09375
- moment_one: float32 [4096, 4096], P(('section', 'dp'), 'mp'), may hold values from -3 to 3
- moment_two: float32 [4096, 4096], P(('section', 'dp'), 'mp'), may hold values from 0.1 to 10
Outputs:
- loss: float32 [1024], P('dp')
- passage_grads: float32 [4096, 4096], P(('section', 'dp', 'mp'))
- new_master: float32 [4096, 4096], P(('section', 'dp'), 'mp')
- new_moment_one: float32 [4096, 4096], P(('section', 'dp'), 'mp')
- new_moment_two: float32 [4096, 4096], P(('section', 'dp'), 'mp')
Inputs may be any that keep to these rules, and one draw needn't show every extreme that they name: `query_cells`: cell ids. `passage_cells`: cell ids. `positives`: passage indices.
All inputs are finite; a program needn't handle non-finite values.
Results may differ from a plain program's by a relative error of at most 0.0095.
Values may be sent and summed in bfloat16 or wider, within the bound.
No kernel may reach another device: no remote copies, remote signals or barrier semaphores. Data moves between devices by JAX's collectives and lax.ppermute only.
A program may use at most 64 MiB of HBM per device.

v0:
```python
import jax
import jax.numpy as jnp
from jax import lax
from jax.sharding import PartitionSpec as P

D = 4096
MICRO = 4


correct_one = 0.9999734386011124
correct_two = 0.994079470779666


def shifted(block, axis, distance):
    devices = range(lax.axis_size(axis))
    route = [(i - distance, i) for i in devices if i - distance in devices]
    return lax.ppermute(block, axis, route)


def from_root(value, axis, source):
    kept = jnp.where(lax.axis_index(axis) == source, value, 0).astype(value.dtype)
    return lax.psum(kept, axis)


def from_behind(value, axis, steps):
    count = lax.axis_size(axis)
    pairs = [(source, (source + steps) % count) for source in range(count)]
    return lax.ppermute(value, axis, pairs)


def merged(part, axis, combine):
    gathered = jax.tree.map(lambda a: lax.all_gather(a, axis), part)

    def take(source):
        return jax.tree.map(lambda a: lax.dynamic_index_in_dim(a, source, 0, False), gathered)

    return lax.fori_loop(
        1, lax.axis_size(axis), lambda source, state: combine(state, take(source)), take(0)
    )


def rms_rows(values):
    wide = values.astype(jnp.float32)
    return (wide * lax.rsqrt(jnp.mean(wide * wide, axis=1, keepdims=True) + 1e-06)).astype(
        jnp.bfloat16
    )


def silu_slope(values):
    sig = jax.nn.sigmoid(values)
    return sig * (1.0 + values * (1.0 - sig))


def shards(
    query_inputs,
    section_weights,
    head_weight,
    passages,
    query_cells,
    passage_cells,
    positives,
    master,
    moment_one,
    moment_two,
):
    sections = lax.axis_size("section")
    cycle = lax.axis_size("dp")
    width = lax.axis_size("mp")
    section_at = lax.axis_index("section")
    cycle_at = lax.axis_index("dp")
    part_at = lax.axis_index("mp")
    query_rows = query_inputs.shape[0]
    micro_rows = query_rows // MICRO
    columns = section_weights.shape[1]
    ticks = MICRO + sections - 1
    leading = section_at == 0
    received = jnp.zeros((micro_rows, columns), jnp.bfloat16)
    finished = []
    for tick in range(ticks):
        slot = min(tick, MICRO - 1)
        fresh = query_inputs[slot * micro_rows : (slot + 1) * micro_rows]
        shard = jnp.where(leading, fresh, received)
        whole = lax.all_gather(shard, "mp", axis=1, tiled=True)
        mixed = jnp.dot(rms_rows(whole), section_weights, preferred_element_type=jnp.float32)
        output = (shard.astype(jnp.float32) + jax.nn.silu(mixed)).astype(jnp.bfloat16)
        if tick >= sections - 1:
            finished.append(output)
        if tick + 1 < ticks:
            received = shifted(output, "section", 1)
    final = from_root(jnp.concatenate(finished, axis=0), "section", sections - 1)
    tower_out = lax.all_gather(final, "mp", axis=1, tiled=True)
    normed = rms_rows(tower_out)
    head = jnp.dot(normed, head_weight, preferred_element_type=jnp.float32)
    query_cols = (final.astype(jnp.float32) + jax.nn.silu(head)).astype(jnp.bfloat16)
    query_emb = lax.all_gather(query_cols, "mp", axis=1, tiled=True)
    block_rows = passages.shape[0]
    scale = D ** (-0.5)
    local_rows = lax.iota(jnp.int32, block_rows)

    def score_block(rows_in, cells_in, owner):
        score = (
            jnp.einsum("pd,qd->pq", rows_in, query_emb, preferred_element_type=jnp.float32) * scale
        )
        index = ((section_at * cycle + owner) * width + part_at) * block_rows + local_rows
        hit = index[:, None] == positives[None, :]
        allowed = jnp.logical_or(hit, cells_in[:, None] == query_cells[None, :])
        return (score, allowed, hit)

    top = jnp.full((query_rows,), -1e30, jnp.float32)
    total = jnp.zeros((query_rows,), jnp.float32)
    positive = jnp.zeros((query_rows,), jnp.float32)
    held = (passages, passage_cells)
    kept = []
    for step in range(cycle):
        owner = (cycle_at - step) % cycle
        score, allowed, hit = score_block(held[0], held[1], owner)
        masked = jnp.where(allowed, score, -1e30)
        newtop = jnp.maximum(top, jnp.max(masked, axis=0))
        total = total * jnp.exp(top - newtop) + jnp.sum(jnp.exp(masked - newtop[None, :]), axis=0)
        positive = positive + jnp.sum(jnp.where(hit, score, 0.0), axis=0)
        top = newtop
        kept.append(held)
        if step + 1 < cycle:
            held = from_behind((held[0], held[1]), "dp", 1)

    def combine(first, second):
        upper = jnp.maximum(first[0], second[0])
        summed = first[1] * jnp.exp(first[0] - upper) + second[1] * jnp.exp(second[0] - upper)
        return (upper, summed, first[2] + second[2])

    top, total, positive = merged((top, total, positive), ("section", "mp"), combine)
    lse = top + jnp.log(total)
    loss = lse - positive
    partial_value = jnp.zeros((query_rows, passages.shape[1]), jnp.float32)
    carried = jnp.zeros((block_rows, query_emb.shape[1]), jnp.float32)
    for step in range(cycle):
        owner = (cycle_at - step) % cycle
        rows_in, cells_in = kept[step]
        score, allowed, hit = score_block(rows_in, cells_in, owner)
        masked = jnp.where(allowed, score, -1e30)
        prob = (jnp.exp(masked - lse[None, :]) - jnp.where(hit, 1.0, 0.0)).astype(jnp.bfloat16)
        partial_value = partial_value + jnp.einsum(
            "pq,pd->qd", prob, rows_in, preferred_element_type=jnp.float32
        )
        carried = carried + jnp.dot(prob, query_emb, preferred_element_type=jnp.float32) * scale
        carried = from_behind(carried.astype(jnp.bfloat16), "dp", 1).astype(carried.dtype)
    query_grad = lax.psum_scatter(
        (partial_value * scale).astype(jnp.bfloat16), "mp", scatter_dimension=1, tiled=True
    ).astype(jnp.float32)
    head_grad = (query_grad * silu_slope(head)).astype(jnp.bfloat16)
    weight_part = jnp.einsum("qd,qc->dc", normed, head_grad, preferred_element_type=jnp.float32)
    weight_grad = lax.psum_scatter(
        weight_part.astype(jnp.bfloat16), ("section", "dp"), scatter_dimension=0, tiled=True
    ).astype(jnp.float32)
    new_moment_one = 0.9 * moment_one + 0.1 * weight_grad
    new_moment_two = 0.95 * moment_two + 0.05 * weight_grad * weight_grad
    update = new_moment_one / correct_one / (jnp.sqrt(new_moment_two / correct_two) + 1e-08)
    new_master = master - 0.001 * (update + 0.1 * master)
    return (loss, carried, new_master, new_moment_one, new_moment_two)


def solution(mesh):
    return jax.shard_map(
        shards,
        mesh=mesh,
        in_specs=(
            P("dp", "mp"),
            P("section", "mp"),
            P(None, "mp"),
            P(("section", "dp", "mp"), None),
            P("dp"),
            P(("section", "dp", "mp")),
            P("dp"),
            P(("section", "dp"), "mp"),
            P(("section", "dp"), "mp"),
            P(("section", "dp"), "mp"),
        ),
        out_specs=(
            P("dp"),
            P(("section", "dp", "mp"), None),
            P(("section", "dp"), "mp"),
            P(("section", "dp"), "mp"),
            P(("section", "dp"), "mp"),
        ),
        check_vma=False,
    )
```

profile of v0, /device:TPU:8, one launch (start us, length us, event | category | flops | bytes accessed | tf_op | source)
XLA Modules:
  0.0 630.2 jit_solution(3651752434942053775)
XLA Ops:
  8.0 13.0 %all_gather.39 = bf16[32,4096]{1,0:T(8,128)(2,1)S(1)} all-gather(bf16[32,512]{1,0:T(8,128)(2,1)S(1)} %slice_select_fusion), channel_id=1, replica_groups=mesh['section'=4,'dp'=8,'mp'=8] {'mp'}, dimensions={1}, use_global_device_ids=true | all-gather | bytes 294912 | tf_op jit(solution)/shard_map/all_gather | solution.py:83
  29.5 12.8 %all_gather.40 = bf16[32,4096]{1,0:T(8,128)(2,1)S(1)} all-gather(bf16[32,512]{1,0:T(8,128)(2,1)S(1)} %slice_select_fusion.1), channel_id=1, replica_groups=mesh['section'=4,'dp'=8,'mp'=8] {'mp'}, dimensions={1}, use_global_device_ids=true | all-gather | bytes 294912 | tf_op jit(solution)/shard_map/all_gather | solution.py:83
  49.2 12.8 %all_gather.41 = bf16[32,4096]{1,0:T(8,128)(2,1)S(1)} all-gather(bf16[32,512]{1,0:T(8,128)(2,1)S(1)} %slice_select_fusion.2), channel_id=1, replica_groups=mesh['section'=4,'dp'=8,'mp'=8] {'mp'}, dimensions={1}, use_global_device_ids=true | all-gather | bytes 294912 | tf_op jit(solution)/shard_map/all_gather | solution.py:83
  68.9 12.8 %all_gather.42 = bf16[32,4096]{1,0:T(8,128)(2,1)S(1)} all-gather(bf16[32,512]{1,0:T(8,128)(2,1)S(1)} %broadcast_select_fusion.3), channel_id=1, replica_groups=mesh['section'=4,'dp'=8,'mp'=8] {'mp'}, dimensions={1}, use_global_device_ids=true | all-gather | bytes 294912 | tf_op jit(solution)/shard_map/all_gather | solution.py:83
  88.7 12.8 %all_gather.43 = bf16[32,4096]{1,0:T(8,128)(2,1)S(1)} all-gather(bf16[32,512]{1,0:T(8,128)(2,1)S(1)} %broadcast_select_fusion.2), channel_id=1, replica_groups=mesh['section'=4,'dp'=8,'mp'=8] {'mp'}, dimensions={1}, use_global_device_ids=true | all-gather | bytes 294912 | tf_op jit(solution)/shard_map/all_gather | solution.py:83
  108.4 12.8 %all_gather.44 = bf16[32,4096]{1,0:T(8,128)(2,1)S(1)} all-gather(bf16[32,512]{1,0:T(8,128)(2,1)S(1)} %broadcast_select_fusion.1), channel_id=1, replica_groups=mesh['section'=4,'dp'=8,'mp'=8] {'mp'}, dimensions={1}, use_global_device_ids=true | all-gather | bytes 294912 | tf_op jit(solution)/shard_map/all_gather | solution.py:83
  128.2 12.8 %all_gather.45 = bf16[32,4096]{1,0:T(8,128)(2,1)S(1)} all-gather(bf16[32,512]{1,0:T(8,128)(2,1)S(1)} %broadcast_select_fusion), channel_id=1, replica_groups=mesh['section'=4,'dp'=8,'mp'=8] {'mp'}, dimensions={1}, use_global_device_ids=true | all-gather | bytes 294912 | tf_op jit(solution)/shard_map/all_gather | solution.py:83
  145.0 49.7 %all-reduce.2.cloned.1.call-done = bf16[128,512]{1,0:T(8,128)(2,1)} async-done(((bf16[128,512]{1,0:T(8,128)(2,1)}), bf16[128,512]{1,0:T(8,128)(2,1)}) %all-reduce.2.cloned.1.call-update) | async-done | bytes 131088 | tf_op jit(solution)/shard_map/psum | solution.py:22
  194.7 26.7 %all-gather.7.cloned.1.call-done = bf16[128,4096]{1,0:T(8,128)(2,1)} async-done(((bf16[128,512]{1,0:T(8,128)(2,1)}), bf16[128,4096]{1,0:T(8,128)(2,1)}) %all-gather.7.cloned.1.call-update) | async-done | bytes 1048592 | tf_op jit(solution)/shard_map/all_gather | solution.py:91
  228.7 5.7 collective-permute-done.7
  234.5 6.4 %collective-permute-done.9 = bf16[16,4096]{1,0:T(8,128)(2,1)S(1)} collective-permute-done((bf16[16,4096]{1,0:T(8,128)(2,1)S(1)}, bf16[16,4096]{1,0:T(8,128)(2,1)S(1)}, u32[]{:S(2)}, u32[]{:S(2)}) %collective-permute-start.9) | collective-permute-done | bytes 131104 | tf_op jit(solution)/shard_map/ppermute | solution.py:28
  241.0 6.1 collective-permute-done.11
  247.1 6.2 collective-permute-done.13
  253.3 7.0 %collective-permute-done.15 = bf16[16,4096]{1,0:T(8,128)(2,1)S(1)} collective-permute-done((bf16[16,4096]{1,0:T(8,128)(2,1)S(1)}, bf16[16,4096]{1,0:T(8,128)(2,1)S(1)}, u32[]{:S(2)}, u32[]{:S(2)}) %collective-permute-start.15) | collective-permute-done | bytes 131104 | tf_op jit(solution)/shard_map/ppermute | solution.py:28
  260.3 6.1 collective-permute-done.8
  266.5 4.7 collective-permute-done.10
  271.2 4.7 collective-permute-done.12
  276.0 4.7 collective-permute-done.14
  280.7 4.7 collective-permute-done.16
  293.2 21.3 %all-gather.2 = f32[32,1,128]{2,1,0:T(1,128)S(1)} all-gather(f32[1,1,128]{2,1,0:T(1,128)S(1)} %get-tuple-element.251), channel_id=1, replica_groups=mesh['section'=4,'dp'=8,'mp'=8] {'section','mp'}, dimensions={0}, use_global_device_ids=true | all-gather | bytes 16896 | tf_op jit(solution)/shard_map/all_gather | solution.py:32
  314.5 20.9 %all-gather.3 = f32[32,1,128]{2,1,0:T(1,128)S(1)} all-gather(f32[1,1,128]{2,1,0:T(1,128)S(1)} %add_bitcast_fusion), channel_id=2, replica_groups=mesh['section'=4,'dp'=8,'mp'=8] {'section','mp'}, dimensions={0}, use_global_device_ids=true | all-gather | bytes 16896 | tf_op jit(solution)/shard_map/all_gather | solution.py:32
  335.5 20.3 %all-gather.1 = f32[32,1,128]{2,1,0:T(1,128)S(1)} all-gather(f32[1,1,128]{2,1,0:T(1,128)S(1)} %get-tuple-element.252), channel_id=1, replica_groups=mesh['section'=4,'dp'=8,'mp'=8] {'section','mp'}, dimensions={0}, use_global_device_ids=true | all-gather | bytes 16896 | tf_op jit(solution)/shard_map/all_gather | solution.py:32
  363.2 30.6 %reduce-scatter.3.cloned.1.call-done = bf16[128,512]{1,0:T(8,128)(2,1)} async-done(((bf16[128,4096]{1,0:T(8,128)(2,1)}), bf16[128,512]{1,0:T(8,128)(2,1)}) %reduce-scatter.3.cloned.1.call-update) | async-done | bytes 131088 | tf_op jit(solution)/shard_map/reduce_scatter | solution.py:147
  400.0 4.7 collective-permute-done.20
  405.3 5.9 collective-permute-done.21
  411.6 6.2 collective-permute-done.22
  418.2 8.0 %collective-permute-done.23 = bf16[16,4096]{1,0:T(8,128)(2,1)S(1)} collective-permute-done((bf16[16,4096]{1,0:T(8,128)(2,1)S(1)}, bf16[16,4096]{1,0:T(8,128)(2,1)S(1)}, u32[]{:S(2)}, u32[]{:S(2)}) %collective-permute-start.23) | collective-permute-done | bytes 131104 | tf_op jit(solution)/shard_map/ppermute | solution.py:28
  426.6 7.6 %collective-permute-done.24 = bf16[16,4096]{1,0:T(8,128)(2,1)S(1)} collective-permute-done((bf16[16,4096]{1,0:T(8,128)(2,1)S(1)}, bf16[16,4096]{1,0:T(8,128)(2,1)S(1)}, u32[]{:S(2)}, u32[]{:S(2)}) %collective-permute-start.24) | collective-permute-done | bytes 131104 | tf_op jit(solution)/shard_map/ppermute | solution.py:28
  434.6 6.8 %collective-permute-done.25 = bf16[16,4096]{1,0:T(8,128)(2,1)S(1)} collective-permute-done((bf16[16,4096]{1,0:T(8,128)(2,1)S(1)}, bf16[16,4096]{1,0:T(8,128)(2,1)S(1)}, u32[]{:S(2)}, u32[]{:S(2)}) %collective-permute-start.25) | collective-permute-done | bytes 131104 | tf_op jit(solution)/shard_map/ppermute | solution.py:28
  441.8 6.6 %collective-permute-done.26 = bf16[16,4096]{1,0:T(8,128)(2,1)S(1)} collective-permute-done((bf16[16,4096]{1,0:T(8,128)(2,1)S(1)}, bf16[16,4096]{1,0:T(8,128)(2,1)S(1)}, u32[]{:S(2)}, u32[]{:S(2)}) %collective-permute-start.26) | collective-permute-done | bytes 131104 | tf_op jit(solution)/shard_map/ppermute | solution.py:28
  448.8 6.7 %collective-permute-done.27 = bf16[16,4096]{1,0:T(8,128)(2,1)S(1)} collective-permute-done((bf16[16,4096]{1,0:T(8,128)(2,1)S(1)}, bf16[16,4096]{1,0:T(8,128)(2,1)S(1)}, u32[]{:S(2)}, u32[]{:S(2)}) %collective-permute-start.27) | collective-permute-done | bytes 131104 | tf_op jit(solution)/shard_map/ppermute | solution.py:28
  456.2 165.2 %reduce-scatter.5.cloned.1.call-done = bf16[128,512]{1,0:T(8,128)(2,1)} async-done(((bf16[4096,512]{1,0:T(8,128)(2,1)}), bf16[128,512]{1,0:T(8,128)(2,1)}) %reduce-scatter.5.cloned.1.call-update) | async-done | bytes 131088 | tf_op jit(solution)/shard_map/reduce_scatter | solution.py:152
  (177 shorter events, 83.1 us)
Async XLA Ops:
  7.2 187.5 %all-reduce.2.cloned.1.call-start = ((), (), s32[]{:S(2)}) async-start(), calls=%async_computation.2 | async-start | bytes 262144 | tf_op jit(solution)/shard_map/psum | solution.py:22
  24.5 5.0 collective-permute-start
  43.4 5.8 collective-permute-start.1
  63.1 5.8 collective-permute-start.2
  82.9 5.8 collective-permute-start.3
  102.6 5.8 collective-permute-start.4
  122.3 5.8 collective-permute-start.5
  144.9 76.5 %all-gather.7.cloned.1.call-start = ((), (), s32[]{:S(2)}) async-start(), calls=%async_computation.3 | async-start | bytes 1179648 | tf_op jit(solution)/shard_map/all_gather | solution.py:91
  194.7 91.4 %all-gather.9.cloned.1.call-start = ((), (), s32[]{:S(2)}) async-start(), calls=%async_computation.4 | async-start | bytes 1179648 | tf_op jit(solution)/shard_map/all_gather | solution.py:95
  227.0 166.8 %reduce-scatter.3.cloned.1.call-start = ((), (), s32[]{:S(2)}) async-start(), calls=%async_computation.5 | async-start | bytes 1179648 | tf_op jit(solution)/shard_map/reduce_scatter | solution.py:147
  227.0 7.3 %collective-permute-start.7 = (bf16[16,4096]{1,0:T(8,128)(2,1)S(1)}, bf16[16,4096]{1,0:T(8,128)(2,1)S(1)}, u32[]{:S(2)}, u32[]{:S(2)}) collective-permute-start(bf16[16,4096]{1,0:T(8,128)(2,1)S(1)} %copy-done.9), channel_id=1, source_target_pairs={{0,8},{8,16},{16,24},{24,32},{32,40},{40,48},{48,56},{56,0},{1,9},... | collective-permute-start | bytes 393224 | tf_op jit(solution)/shard_map/ppermute | solution.py:28
  234.3 6.5 %collective-permute-start.9 = (bf16[16,4096]{1,0:T(8,128)(2,1)S(1)}, bf16[16,4096]{1,0:T(8,128)(2,1)S(1)}, u32[]{:S(2)}, u32[]{:S(2)}) collective-permute-start(bf16[16,4096]{1,0:T(8,128)(2,1)S(1)} %collective-permute-done.7), channel_id=1, source_target_pairs={{0,8},{8,16},{16,24},{24,32},{32,40},{40,48},{48,56},{56,0},{1,9},... | collective-permute-start | bytes 393224 | tf_op jit(solution)/shard_map/ppermute | solution.py:28
  240.9 6.2 collective-permute-start.11
  240.9 19.3 %collective-permute-start.6 = (s32[16]{0:T(128)S(1)}, s32[16]{0:T(128)S(1)}, u32[]{:S(2)}, u32[]{:S(2)}) collective-permute-start(s32[16]{0:T(128)S(1)} %copy-done.10), channel_id=1, source_target_pairs={{0,8},{8,16},{16,24},{24,32},{32,40},{40,48},{48,56},{56,0},{1,9},... | collective-permute-start | bytes 200 | tf_op jit(solution)/shard_map/ppermute | solution.py:28
  247.1 6.2 collective-permute-start.13
  253.2 7.0 %collective-permute-start.15 = (bf16[16,4096]{1,0:T(8,128)(2,1)S(1)}, bf16[16,4096]{1,0:T(8,128)(2,1)S(1)}, u32[]{:S(2)}, u32[]{:S(2)}) collective-permute-start(bf16[16,4096]{1,0:T(8,128)(2,1)S(1)} %collective-permute-done.13), channel_id=1, source_target_pairs={{0,8},{8,16},{16,24},{24,32},{32,40},{40,48},{48,56},{56,0},{1,9},... | collective-permute-start | bytes 393224 | tf_op jit(solution)/shard_map/ppermute | solution.py:28
  260.2 25.3 %collective-permute-start.17 = (bf16[16,4096]{1,0:T(8,128)(2,1)S(1)}, bf16[16,4096]{1,0:T(8,128)(2,1)S(1)}, u32[]{:S(2)}, u32[]{:S(2)}) collective-permute-start(bf16[16,4096]{1,0:T(8,128)(2,1)S(1)} %collective-permute-done.15), channel_id=1, source_target_pairs={{0,8},{8,16},{16,24},{24,32},{32,40},{40,48},{48,56},{56,0},{1,9},... | collective-permute-start | bytes 393224 | tf_op jit(solution)/shard_map/ppermute | solution.py:28
  260.2 6.2 collective-permute-start.8
  266.5 4.8 collective-permute-start.10
  276.0 4.8 collective-permute-start.14
  280.7 4.8 collective-permute-start.16
  285.5 6.6 %collective-permute-start.18 = (s32[16]{0:T(128)S(1)}, s32[16]{0:T(128)S(1)}, u32[]{:S(2)}, u32[]{:S(2)}) collective-permute-start(s32[16]{0:T(128)S(1)} %collective-permute-done.16), channel_id=1, source_target_pairs={{0,8},{8,16},{16,24},{24,32},{32,40},{40,48},{48,56},{56,0},{1,9},... | collective-permute-start | bytes 200 | tf_op jit(solution)/shard_map/ppermute | solution.py:28
  285.5 6.2 collective-permute-start.19
  363.2 258.2 %reduce-scatter.5.cloned.1.call-start = ((), (), s32[]{:S(2)}) async-start(), calls=%async_computation.6 | async-start | bytes 4325376 | tf_op jit(solution)/shard_map/reduce_scatter | solution.py:152
  398.4 6.3 collective-permute-start.20
  405.0 6.3 collective-permute-start.21
  411.5 6.3 collective-permute-start.22
  418.1 8.0 %collective-permute-start.23 = (bf16[16,4096]{1,0:T(8,128)(2,1)S(1)}, bf16[16,4096]{1,0:T(8,128)(2,1)S(1)}, u32[]{:S(2)}, u32[]{:S(2)}) collective-permute-start(bf16[16,4096]{1,0:T(8,128)(2,1)S(1)} %add_convert_fusion.4), channel_id=1, source_target_pairs={{0,8},{8,16},{16,24},{24,32},{32,40},{40,48},{48,56},{56,0},{1,9},... | collective-permute-start | bytes 393224 | tf_op jit(solution)/shard_map/ppermute | solution.py:28
  426.5 7.7 %collective-permute-start.24 = (bf16[16,4096]{1,0:T(8,128)(2,1)S(1)}, bf16[16,4096]{1,0:T(8,128)(2,1)S(1)}, u32[]{:S(2)}, u32[]{:S(2)}) collective-permute-start(bf16[16,4096]{1,0:T(8,128)(2,1)S(1)} %add_convert_fusion.3), channel_id=1, source_target_pairs={{0,8},{8,16},{16,24},{24,32},{32,40},{40,48},{48,56},{56,0},{1,9},... | collective-permute-start | bytes 393224 | tf_op jit(solution)/shard_map/ppermute | solution.py:28
  434.5 6.9 %collective-permute-start.25 = (bf16[16,4096]{1,0:T(8,128)(2,1)S(1)}, bf16[16,4096]{1,0:T(8,128)(2,1)S(1)}, u32[]{:S(2)}, u32[]{:S(2)}) collective-permute-start(bf16[16,4096]{1,0:T(8,128)(2,1)S(1)} %add_convert_fusion.2), channel_id=1, source_target_pairs={{0,8},{8,16},{16,24},{24,32},{32,40},{40,48},{48,56},{56,0},{1,9},... | collective-permute-start | bytes 393224 | tf_op jit(solution)/shard_map/ppermute | solution.py:28
  441.7 6.7 %collective-permute-start.26 = (bf16[16,4096]{1,0:T(8,128)(2,1)S(1)}, bf16[16,4096]{1,0:T(8,128)(2,1)S(1)}, u32[]{:S(2)}, u32[]{:S(2)}) collective-permute-start(bf16[16,4096]{1,0:T(8,128)(2,1)S(1)} %add_convert_fusion.1), channel_id=1, source_target_pairs={{0,8},{8,16},{16,24},{24,32},{32,40},{40,48},{48,56},{56,0},{1,9},... | collective-permute-start | bytes 393224 | tf_op jit(solution)/shard_map/ppermute | solution.py:28
  448.7 6.8 %collective-permute-start.27 = (bf16[16,4096]{1,0:T(8,128)(2,1)S(1)}, bf16[16,4096]{1,0:T(8,128)(2,1)S(1)}, u32[]{:S(2)}, u32[]{:S(2)}) collective-permute-start(bf16[16,4096]{1,0:T(8,128)(2,1)S(1)} %add_convert_fusion), channel_id=1, source_target_pairs={{0,8},{8,16},{16,24},{24,32},{32,40},{40,48},{48,56},{56,0},{1,9},... | collective-permute-start | bytes 393224 | tf_op jit(solution)/shard_map/ppermute | solution.py:28
  (12 other events, 681.8 us)
Sparse Core Ops, SparseCore 0:
  145.1 49.5 all-reduce.1
  196.6 24.7 all-gather.6
  227.1 25.8 all-gather.8
  363.3 30.4 reduce-scatter.2
  398.2 223.1 reduce-scatter.4
where the time goes:
time: 639 us; the launch traced here: 630 us
  waiting for transfers between devices  391 us (61%)
  blocking collectives  153 us (24%)
  matrix products  32.5 us (5%)
  starting transfers between devices  29.8 us (5%)
  between operations  14.6 us (2%)
  other arithmetic  8.59 us (1%)
    reduce_scatter x1, waiting for transfers between devices, shards(): lax.psum_scatter(weight_part.astype(jnp.bfloat16), ('section', 'dp'), sca...  165 us
    ppermute x22, waiting for transfers between devices, from_behind(): return lax.ppermute(value, axis, pairs)  110 us
    all_gather x7, blocking collectives, shards(): whole = lax.all_gather(shard, 'mp', axis=1, tiled=True)  90 us
    all_gather x3, blocking collectives, merged(): gathered = jax.tree.map(lambda a: lax.all_gather(a, axis), part)  62.6 us
    psum x1, waiting for transfers between devices, from_root(): return lax.psum(kept, axis)  49.7 us
    reduce_scatter x1, waiting for transfers between devices, shards(): lax.psum_scatter((partial_value * scale).astype(jnp.bfloat16), 'mp', scat...  30.6 us
    all_gather x1, waiting for transfers between devices, shards(): tower_out = lax.all_gather(final, 'mp', axis=1, tiled=True)  26.7 us
    ppermute x6, starting transfers between devices, shifted(): return lax.ppermute(block, axis, route)  24.6 us
  transfers between devices with their start and end apart: 33, of which 29 were waited for; matrix products, arithmetic and copies ran while one was open for 1% of the time, Pallas kernels for 0%

commit v1 on v0

v1 whole, which is shorter than its diff:
```python
import functools
import math

import jax
import jax.numpy as jnp
from jax import lax
from jax.experimental import pallas as pl
from jax.experimental.pallas import tpu as pltpu
from jax.sharding import Mesh, PartitionSpec as P

correct_one = 0.9999734386011124
correct_two = 0.994079470779666
FAR = -1e30
F32 = jnp.float32
BF16 = jnp.bfloat16
VMEM = pl.BlockSpec(memory_space=pltpu.VMEM)
SMEM = pl.BlockSpec(memory_space=pltpu.SMEM)
PARAMS = pltpu.CompilerParams(vmem_limit_bytes=48 * 1024 * 1024)


def turned(block, axis, steps):
    count = lax.axis_size(axis)
    return lax.ppermute(block, axis, [(i, (i + steps) % count) for i in range(count)])


def spread(block):
    count = lax.axis_size("y")
    near = jnp.stack([block] + [turned(block, "y", k) for k in range(1, count)])
    return near, turned(near, "core", 1)


def silu(u):
    return u * jax.nn.sigmoid(u)


def row_scale(near, far):
    square = 0.0
    for ref in (near, far):
        for k in range(ref.shape[0]):
            wide = ref[k].astype(F32)
            square = square + jnp.sum(wide * wide, axis=1, keepdims=True)
    width = 2 * near.shape[0] * near.shape[2]
    return lax.rsqrt(square / width + 1e-06)


def owners(place, near, far):
    count = near.shape[0]
    y, core = place[2], place[3]
    for k in range(count):
        for ref, c in ((near, core), (far, 1 - core)):
            yield ref, k, lax.rem(y - k + count, count) * 2 + c


def mixed_rows(place, near, far, weight, normed=None):
    scale = row_scale(near, far)
    wide = near.shape[2]
    total = 0.0
    for ref, k, owner in owners(place, near, far):
        rows = (ref[k].astype(F32) * scale).astype(BF16)
        at = pl.ds(pl.multiple_of(owner * wide, wide), wide)
        if normed is not None:
            normed[:, at] = rows
        total = total + jnp.dot(rows, weight[at, :], preferred_element_type=F32)
    return total


def layer_kernel(place, near, far, weight, out):
    mixed = mixed_rows(place, near, far, weight)
    out[...] = (near[0].astype(F32) + silu(mixed)).astype(BF16)


def head_kernel(place, near, far, weight, emb, slope, normed):
    head = mixed_rows(place, near, far, weight, normed)
    sig = jax.nn.sigmoid(head)
    emb[...] = (near[0].astype(F32) + head * sig).astype(BF16)
    slope[...] = sig * (1.0 + head * (1.0 - sig))


def masks(place, passages, query_cells, positives, sizes):
    width, cycle, parts, block = sizes
    rows, queries = passages.shape[0], positives.shape[1]
    at = lax.broadcasted_iota(jnp.int32, (rows, queries), 0)
    owner, inner = at // block, at % block
    part = place[2] * 2 + place[3]
    index = ((place[0] * cycle + owner) * parts + part) * block + inner
    hit = index == positives[...]
    cells = passages[:, width : width + queries].astype(F32)
    allowed = jnp.logical_or(hit, cells == query_cells[...].astype(F32))
    return hit, allowed


def score_kernel(sizes, place, near, far, passages, query_cells, positives, score, stats, full):
    wide = near.shape[2]
    total = 0.0
    for ref, k, owner in owners(place, near, far):
        at = pl.ds(pl.multiple_of(owner * wide, wide), wide)
        full[:, at] = ref[k]
        total = total + lax.dot_general(
            passages[:, at], ref[k], (((1,), (1,)), ((), ())), preferred_element_type=F32
        )
    total = total * sizes[0] ** -0.5
    score[...] = total
    hit, allowed = masks(place, passages, query_cells, positives, sizes)
    masked = jnp.where(allowed, total, FAR)
    top = jnp.max(masked, axis=0, keepdims=True)
    summed = jnp.sum(jnp.exp(masked - top), axis=0, keepdims=True)
    positive = jnp.sum(jnp.where(hit, total, 0.0), axis=0, keepdims=True)
    rest = jnp.zeros((5,) + top.shape[1:], F32)
    packed = jnp.concatenate([top, summed, positive, rest], axis=0)
    stats[...] = jnp.broadcast_to(packed[None], stats.shape)


def grad_kernel(
    sizes, place, stats, score, full, passages, query_cells, positives, loss, send, keep, grads
):
    width = sizes[0]
    top, summed, positive = stats[:, 0, :], stats[:, 1, :], stats[:, 2, :]
    upper = jnp.max(top, axis=0, keepdims=True)
    total = jnp.sum(summed * jnp.exp(top - upper), axis=0, keepdims=True)
    lse = upper + jnp.log(total)
    loss[...] = lse - jnp.sum(positive, axis=0, keepdims=True)
    hit, allowed = masks(place, passages, query_cells, positives, sizes)
    masked = jnp.where(allowed, score[...], FAR)
    prob = jnp.exp(masked - lse) - jnp.where(hit, 1.0, 0.0)
    turned_prob = prob.T.astype(BF16)
    prob = prob.astype(BF16)
    factor = width**-0.5
    sections, count, rows, wide = keep.shape
    core = place[3]
    for j in range(count):
        for ref, c in ((keep, core), (send, 1 - core)):
            at = pl.ds(pl.multiple_of((2 * j + c) * wide, wide), wide)
            part = jnp.dot(turned_prob, passages[:, at], preferred_element_type=F32) * factor
            part = part.astype(BF16)
            for s in range(sections):
                ref[s, j] = part[s * rows : (s + 1) * rows]
    for j in range(0, width, wide):
        part = jnp.dot(prob, full[:, j : j + wide], preferred_element_type=F32) * factor
        part = part.astype(BF16)
        cycle, block = grads.shape[:2]
        for d in range(cycle):
            grads[d, :, j : j + wide] = part[d * block : (d + 1) * block]


def call(kernel, outs, *args):
    return pl.pallas_call(
        kernel,
        out_shape=[jax.ShapeDtypeStruct(shape, dtype) for shape, dtype in outs],
        in_specs=[SMEM] + [VMEM] * (len(args) - 1),
        out_specs=[VMEM] * len(outs),
        compiler_params=PARAMS,
    )(*args)


def shards(
    query_inputs,
    section_weights,
    head_weight,
    passages,
    query_cells,
    passage_cells,
    positives,
    master,
    moment_one,
    moment_two,
):
    sections = lax.axis_size("section")
    cycle = lax.axis_size("dp")
    count = lax.axis_size("y")
    section_at = lax.axis_index("section")
    place = jnp.stack(
        [section_at, lax.axis_index("dp"), lax.axis_index("y"), lax.axis_index("core")]
    ).astype(jnp.int32)
    queries, wide = query_inputs.shape
    block, width = passages.shape
    sizes = (width, cycle, 2 * count, block)
    with jax.named_scope("passages"):
        cells = jnp.broadcast_to(passage_cells.astype(BF16)[:, None], (block, queries))
        held = lax.all_gather(
            jnp.concatenate([passages, cells], axis=1), "dp", axis=0, tiled=True
        )
    local = query_inputs
    for layer in range(sections):
        with jax.named_scope("tower"):
            near, far = spread(local)
            (local,) = call(
                layer_kernel, [((queries, wide), BF16)], place, near, far, section_weights
            )
            if layer + 1 < sections:
                local = turned(local, "section", 1)
    with jax.named_scope("to_sections"):
        last = sections - 1
        final = jnp.where(section_at == last, local, 0).astype(BF16)
        for other in range(last):
            final = final + lax.ppermute(local, "section", [(last, other)])
    with jax.named_scope("head"):
        near, far = spread(final)
        query_cols, slope, normed = call(
            head_kernel,
            [((queries, wide), BF16), ((queries, wide), F32), ((queries, width), BF16)],
            place, near, far, head_weight,
        )
    rows = queries // sections
    with jax.named_scope("normed_home"):
        mine = lax.dynamic_slice_in_dim(normed, section_at * rows, rows, 0)
        mine = mine.reshape(rows, sections, cycle, width // (sections * cycle))
        mine = mine.transpose(2, 0, 1, 3).reshape(cycle, rows, width // cycle)
        normed_all = lax.all_to_all(mine, "dp", 0, 0).reshape(cycle * rows, width // cycle)
    with jax.named_scope("score"):
        near, far = spread(query_cols)
        row_cells, row_positives = query_cells[None, :], positives[None, :]
        group = sections * count * 2
        score, stats, full = call(
            functools.partial(score_kernel, sizes),
            [
                ((cycle * block, queries), F32),
                ((group, 8, queries), F32),
                ((queries, width), BF16),
            ],
            place, near, far, held, row_cells, row_positives,
        )
    with jax.named_scope("stats"):
        stats = lax.all_to_all(stats, ("section", "y", "core"), 0, 0)
    with jax.named_scope("grad"):
        half = (sections, count, rows, wide)
        loss, send, keep, grads = call(
            functools.partial(grad_kernel, sizes),
            [((1, queries), F32), (half, BF16), (half, BF16), ((cycle, block, width), BF16)],
            place, stats, score, full, held, row_cells, row_positives,
        )
    with jax.named_scope("passage_grads"):
        grads = lax.all_to_all(grads, "dp", 0, 0)
        passage_grads = jnp.sum(grads.astype(F32), axis=0)
    with jax.named_scope("query_grad"):
        keep = (keep.astype(F32) + turned(send, "core", 1).astype(F32)).astype(BF16)
        parts = lax.all_to_all(keep.reshape(sections * count, rows, wide), ("section", "y"), 0, 0)
        query_grad = jnp.sum(parts.astype(F32), axis=0)
        head_grad = query_grad * lax.dynamic_slice_in_dim(slope, section_at * rows, rows, 0)
        head_grad = jnp.broadcast_to(head_grad.astype(BF16)[None], (cycle, rows, wide))
        head_grad = lax.all_to_all(head_grad, "dp", 0, 0).reshape(cycle * rows, wide)
    with jax.named_scope("weight_grad"):
        part = jnp.einsum("qd,qc->dc", normed_all, head_grad, preferred_element_type=F32)
        part = part.astype(BF16).reshape(sections, width // (sections * cycle), wide)
        part = lax.all_to_all(part, "section", 0, 0)
        weight_grad = jnp.sum(part.astype(F32), axis=0)
    new_moment_one = 0.9 * moment_one + 0.1 * weight_grad
    new_moment_two = 0.95 * moment_two + 0.05 * weight_grad * weight_grad
    update = new_moment_one / correct_one / (jnp.sqrt(new_moment_two / correct_two) + 1e-08)
    new_master = master - 0.001 * (update + 0.1 * master)
    return (loss[0], passage_grads, new_master, new_moment_one, new_moment_two)


def solution(mesh):
    sections, cycle, parts = (mesh.shape[axis] for axis in ("section", "dp", "mp"))
    split = Mesh(
        mesh.devices.reshape(sections, cycle, parts // 2, 2), ("section", "dp", "y", "core")
    )
    mp = ("y", "core")
    everything = ("section", "dp") + mp
    tile = P(("section", "dp"), mp)
    return jax.shard_map(
        shards,
        mesh=split,
        in_specs=(
            P("dp", mp),
            P("section", mp),
            P(None, mp),
            P(everything, None),
            P("dp"),
            P(everything),
            P("dp"),
            tile,
            tile,
            tile,
        ),
        out_specs=(P("dp"), P(everything, None), tile, tile, tile),
        check_vma=False,
    )
```

time: 639 us -> 245 us (0.38); the launches traced: 630 us -> 244 us
  waiting for transfers between devices: 391 us -> 126 us
  blocking collectives: 153 us -> 26.8 us
  matrix products: 32.5 us -> 1.15 us
  starting transfers between devices: 29.8 us -> 52.5 us
  Pallas kernels: 0 us -> 12.9 us
    reduce_scatter x2 -> x0, waiting for transfers between devices: 196 us -> none  [the longest x1 165 us: shards(): lax.psum_scatter(weight_part.astype(jnp.bfloat16), ('section', 'dp'), sca...]
    all_gather x10 -> x0, blocking collectives: 153 us -> none  [the longest x7 90 us: shards(): whole = lax.all_gather(shard, 'mp', axis=1, tiled=True)]
    ppermute x28 -> x31, waiting for transfers between devices: 119 us -> 64 us  [the longest x28 57.4 us: turned(): lax.ppermute(block, axis, [(i, (i + steps) % count) for i in range(count)])]
    all_to_all x0 -> x4, waiting for transfers between devices: none -> 51.6 us  [the longest x1 24.1 us: shards(): grads = lax.all_to_all(grads, 'dp', 0, 0)]
    psum x1 -> x0, waiting for transfers between devices: 49.7 us -> none  [from_root(): return lax.psum(kept, axis)]
    dot_general x33 -> x1, matrix products: 32.5 us -> 1.15 us  [shards(): jnp.einsum('qd,qc->dc', normed_all, head_grad, preferred_element_type=F32)]
    all_to_all x0 -> x2, blocking collectives: none -> 26.8 us  [the longest x1 14 us: shards(): stats = lax.all_to_all(stats, ('section', 'y', 'core'), 0, 0)]
    all_gather x2 -> x1, waiting for transfers between devices: 26.7 us -> 10.1 us  [shards(): lax.all_gather(jnp.concatenate([passages, cells], axis=1), 'dp', axis=0,...]
  transfers between devices with their start and end apart: 33 -> 36, of which waited for: 29 -> 30; matrix products, arithmetic and copies ran while one was open for 1% -> 2% of each run, Pallas kernels for 0% -> 1%
where the time goes in v1:
time: 245 us; the launch traced here: 244 us
  waiting for transfers between devices  126 us (51%)
  starting transfers between devices  52.5 us (21%)
  blocking collectives  26.8 us (11%)
  between operations  14.4 us (6%)
  Pallas kernels  12.9 us (5%)
  local copies, waits for them, and re-layouts  5.75 us (2%)
  other arithmetic  5.09 us (2%)
    ppermute x28, waiting for transfers between devices, turned(): lax.ppermute(block, axis, [(i, (i + steps) % count) for i in range(count)])  57.4 us
    ppermute x28, starting transfers between devices, turned(): lax.ppermute(block, axis, [(i, (i + steps) % count) for i in range(count)])  33.4 us
    all_to_all x1, waiting for transfers between devices, shards(): grads = lax.all_to_all(grads, 'dp', 0, 0)  24.1 us
    all_to_all x1, blocking collectives, shards(): stats = lax.all_to_all(stats, ('section', 'y', 'core'), 0, 0)  14 us
    pallas_call x7, Pallas kernels, call(): pl.pallas_call(kernel, out_shape=[jax.ShapeDtypeStruct(shape, dtype) for...  12.9 us
    all_to_all x1, blocking collectives, shards(): lax.all_to_all(head_grad, 'dp', 0, 0).reshape(cycle * rows, wide)  12.9 us
    all_to_all x1, waiting for transfers between devices, shards(): lax.all_to_all(mine, 'dp', 0, 0).reshape(cycle * rows, width // cycle)  10.5 us
    all_gather x1, waiting for transfers between devices, shards(): lax.all_gather(jnp.concatenate([passages, cells], axis=1), 'dp', axis=0,...  10.1 us
  transfers between devices with their start and end apart: 36, of which 30 were waited for; matrix products, arithmetic and copies ran while one was open for 2% of the time, Pallas kernels for 1%

profile of v1, /device:TPU:8, one launch (start us, length us, event | category | flops | bytes accessed | tf_op | source)
XLA Modules:
  0.0 244.3 jit_solution(8484409851932140307)
XLA Ops:
  14.8 2.8 %collective-permute-done.1 = bf16[128,512]{1,0:T(8,128)(2,1)S(1)} collective-permute-done((bf16[128,512]{1,0:T(8,128)(2,1)}, bf16[128,512]{1,0:T(8,128)(2,1)S(1)}, u32[]{:S(2)}, u32[]{:S(2)}) %collective-permute-start.1) | collective-permute-done | bytes 131104 | tf_op jit(solution)/shard_map/tower/ppermute | solution.py:23
  25.9 5.3 %collective-permute-done.4 = bf16[128,512]{1,0:T(8,128)(2,1)S(1)} collective-permute-done((bf16[128,512]{1,0:T(8,128)(2,1)S(1)}, bf16[128,512]{1,0:T(8,128)(2,1)S(1)}, u32[]{:S(2)}, u32[]{:S(2)}) %collective-permute-start.4) | collective-permute-done | bytes 131104 | tf_op jit(solution)/shard_map/tower/ppermute | solution.py:23
  33.6 2.6 %collective-permute-start.5 = (bf16[128,512]{1,0:T(8,128)(2,1)S(1)}, bf16[128,512]{1,0:T(8,128)(2,1)S(1)}, u32[]{:S(2)}, u32[]{:S(2)}) collective-permute-start(bf16[128,512]{1,0:T(8,128)(2,1)S(1)} %collective-permute-done.4), channel_id=1, source_target_pairs={{0,2},{2,4},{4,6},{6,0},{1,3},{3,5},{5,7},{7,1},{8,10},{10,12},{12... | collective-permute-start | bytes 393224 | tf_op jit(solution)/shard_map/tower/ppermute | solution.py:23
  36.6 2.8 %collective-permute-done.6 = bf16[128,512]{1,0:T(8,128)(2,1)S(1)} collective-permute-done((bf16[128,512]{1,0:T(8,128)(2,1)S(1)}, bf16[128,512]{1,0:T(8,128)(2,1)S(1)}, u32[]{:S(2)}, u32[]{:S(2)}) %collective-permute-start.6) | collective-permute-done | bytes 131104 | tf_op jit(solution)/shard_map/tower/ppermute | solution.py:23
  44.4 6.5 %collective-permute-done.9 = bf16[128,512]{1,0:T(8,128)(2,1)S(1)} collective-permute-done((bf16[128,512]{1,0:T(8,128)(2,1)S(1)}, bf16[128,512]{1,0:T(8,128)(2,1)S(1)}, u32[]{:S(2)}, u32[]{:S(2)}) %collective-permute-start.9) | collective-permute-done | bytes 131104 | tf_op jit(solution)/shard_map/tower/ppermute | solution.py:23
  50.9 3.0 %collective-permute-start.12 = (bf16[128,512]{1,0:T(8,128)(2,1)S(1)}, bf16[128,512]{1,0:T(8,128)(2,1)S(1)}, u32[]{:S(2)}, u32[]{:S(2)}) collective-permute-start(bf16[128,512]{1,0:T(8,128)(2,1)S(1)} %collective-permute-done.9), channel_id=1, source_target_pairs={{0,6},{2,0},{4,2},{6,4},{1,7},{3,1},{5,3},{7,5},{8,14},{10,8},{12,... | collective-permute-start | bytes 393224 | tf_op jit(solution)/shard_map/tower/ppermute | solution.py:23
  53.8 2.2 collective-permute-start.10
  57.5 2.8 %collective-permute-done.11 = bf16[128,512]{1,0:T(8,128)(2,1)S(1)} collective-permute-done((bf16[128,512]{1,0:T(8,128)(2,1)S(1)}, bf16[128,512]{1,0:T(8,128)(2,1)S(1)}, u32[]{:S(2)}, u32[]{:S(2)}) %collective-permute-start.11) | collective-permute-done | bytes 131104 | tf_op jit(solution)/shard_map/tower/ppermute | solution.py:23
  64.2 6.7 %collective-permute-done.14 = bf16[128,512]{1,0:T(8,128)(2,1)S(1)} collective-permute-done((bf16[128,512]{1,0:T(8,128)(2,1)S(1)}, bf16[128,512]{1,0:T(8,128)(2,1)S(1)}, u32[]{:S(2)}, u32[]{:S(2)}) %collective-permute-start.14) | collective-permute-done | bytes 131104 | tf_op jit(solution)/shard_map/tower/ppermute | solution.py:23
  71.0 3.0 %collective-permute-start.17 = (bf16[128,512]{1,0:T(8,128)(2,1)S(1)}, bf16[128,512]{1,0:T(8,128)(2,1)S(1)}, u32[]{:S(2)}, u32[]{:S(2)}) collective-permute-start(bf16[128,512]{1,0:T(8,128)(2,1)S(1)} %collective-permute-done.14), channel_id=1, source_target_pairs={{0,6},{2,0},{4,2},{6,4},{1,7},{3,1},{5,3},{7,5},{8,14},{10,8},{12,... | collective-permute-start | bytes 393224 | tf_op jit(solution)/shard_map/tower/ppermute | solution.py:23
  74.0 2.2 collective-permute-start.15
  77.6 2.8 %collective-permute-done.16 = bf16[128,512]{1,0:T(8,128)(2,1)S(1)} collective-permute-done((bf16[128,512]{1,0:T(8,128)(2,1)S(1)}, bf16[128,512]{1,0:T(8,128)(2,1)S(1)}, u32[]{:S(2)}, u32[]{:S(2)}) %collective-permute-start.16) | collective-permute-done | bytes 131104 | tf_op jit(solution)/shard_map/tower/ppermute | solution.py:23
  87.6 6.5 %collective-permute-done.19 = bf16[128,512]{1,0:T(8,128)(2,1)S(1)} collective-permute-done((bf16[128,512]{1,0:T(8,128)(2,1)S(1)}, bf16[128,512]{1,0:T(8,128)(2,1)S(1)}, u32[]{:S(2)}, u32[]{:S(2)}) %collective-permute-start.19) | collective-permute-done | bytes 131104 | tf_op jit(solution)/shard_map/to_sections/ppermute | solution.py:195
  94.1 3.1 %collective-permute-start.24 = (bf16[128,512]{1,0:T(8,128)(2,1)S(1)}, bf16[128,512]{1,0:T(8,128)(2,1)S(1)}, u32[]{:S(2)}, u32[]{:S(2)}) collective-permute-start(bf16[128,512]{1,0:T(8,128)(2,1)S(1)} %add_add_fusion), channel_id=1, source_target_pairs={{0,6},{2,0},{4,2},{6,4},{1,7},{3,1},{5,3},{7,5},{8,14},{10,8},{12,... | collective-permute-start | bytes 393224 | tf_op jit(solution)/shard_map/head/ppermute | solution.py:23
  97.2 2.2 collective-permute-start.22
  100.9 2.8 %collective-permute-done.23 = bf16[128,512]{1,0:T(8,128)(2,1)S(1)} collective-permute-done((bf16[128,512]{1,0:T(8,128)(2,1)S(1)}, bf16[128,512]{1,0:T(8,128)(2,1)S(1)}, u32[]{:S(2)}, u32[]{:S(2)}) %collective-permute-start.23) | collective-permute-done | bytes 131104 | tf_op jit(solution)/shard_map/head/ppermute | solution.py:23
  105.8 3.3 %head.1 = (bf16[128,512]{1,0:T(8,128)(2,1)S(1)}, f32[128,512]{1,0:T(8,128)S(1)}, bf16[128,4096]{1,0:T(8,128)(2,1)S(1)}) custom-call(s32[4]{0:T(128)S(1)} %pad_add_fusion.place, bf16[4,128,512]{2,1,0:T(8,128)(2,1)S(1)} %pad_maximum_fusion.4.near, bf16[4,128,512]{2,1,0:T(8,128)(2,1)S(1)} %collective-permute-done.25.far, bf16[4096,512]{1,0:T(8,128)(2,1)} %weight.9), custom_call_target="tpu_custom_call" | custom-call | tf_op jit(solution)/shard_map/head/pallas_call | solution.py:146
  109.1 3.1 %collective-permute-start.28 = (bf16[128,512]{1,0:T(8,128)(2,1)S(1)}, bf16[128,512]{1,0:T(8,128)(2,1)S(1)}, u32[]{:S(2)}, u32[]{:S(2)}) collective-permute-start(bf16[128,512]{1,0:T(8,128)(2,1)S(1)} %get-tuple-element.15), channel_id=1, source_target_pairs={{0,6},{2,0},{4,2},{6,4},{1,7},{3,1},{5,3},{7,5},{8,14},{10,8},{12,... | collective-permute-start | bytes 393224 | tf_op jit(solution)/shard_map/score/ppermute | solution.py:23
  112.2 2.2 collective-permute-start.26
  116.0 2.9 %collective-permute-done.27 = bf16[128,512]{1,0:T(8,128)(2,1)S(1)} collective-permute-done((bf16[128,512]{1,0:T(8,128)(2,1)S(1)}, bf16[128,512]{1,0:T(8,128)(2,1)S(1)}, u32[]{:S(2)}, u32[]{:S(2)}) %collective-permute-start.27) | collective-permute-done | bytes 131104 | tf_op jit(solution)/shard_map/score/ppermute | solution.py:23
  119.5 10.1 %all-gather.2.cloned.1.call-done.passages = bf16[128,4224]{1,0:T(8,128)(2,1)} async-done(((bf16[16,4224]{1,0:T(8,128)(2,1)}), bf16[128,4224]{1,0:T(8,128)(2,1)}) %all-gather.2.cloned.1.call-update) | async-done | bytes 1081360 | tf_op jit(solution)/shard_map/passages/all_gather | solution.py:179
  131.9 14.0 %all_to_all.30.stats = f32[32,8,128]{2,1,0:T(8,128)S(1)} all-to-all(f32[32,8,128]{2,1,0:T(8,128)S(1)} %get-tuple-element.16), channel_id=1, replica_groups=mesh['section'=4,'dp'=8,'y'=4,'core'=2] {'section','y','core'}, dimensions={0} | all-to-all | bytes 262144 | tf_op jit(solution)/shard_map/stats/all_to_all | solution.py:223
  147.1 2.3 grad.1
  152.4 4.9 %all-to-all-start.3 = ((bf16[16,32,512]{2,1,0:T(8,128)(2,1)}), bf16[16,32,512]{2,1,0:T(8,128)(2,1)S(1)}, u32[]{:S(2)}, u32[]{:S(2)}) async-start(bf16[16,32,512]{2,1,0:T(8,128)(2,1)} %bitcast.32), calls=%async_computation.3 | async-start | bytes 1048576 | tf_op jit(solution)/shard_map/query_grad/all_to_all | solution.py:236
  158.2 9.8 %all-to-all-done.3 = bf16[16,32,512]{2,1,0:T(8,128)(2,1)S(1)} async-done(((bf16[16,32,512]{2,1,0:T(8,128)(2,1)}), bf16[16,32,512]{2,1,0:T(8,128)(2,1)S(1)}, u32[]{:S(2)}, u32[]{:S(2)}) %all-to-all-start.3) | async-done | bytes 524320 | tf_op jit(solution)/shard_map/query_grad/all_to_all | solution.py:236
  168.0 4.3 %all-to-all-start.2 = ((bf16[8,32,512]{2,1,0:T(8,128)(2,1)}), bf16[8,32,512]{2,1,0:T(8,128)(2,1)S(1)}, u32[]{:S(2)}, u32[]{:S(2)}) async-start(bf16[8,32,512]{2,1,0:T(8,128)(2,1)} %reshape.27), calls=%async_computation.2 | async-start | bytes 524288 | tf_op jit(solution)/shard_map/normed_home/all_to_all | solution.py:208
  172.5 10.5 %all-to-all-done.2 = bf16[8,32,512]{2,1,0:T(8,128)(2,1)S(1)} async-done(((bf16[8,32,512]{2,1,0:T(8,128)(2,1)}), bf16[8,32,512]{2,1,0:T(8,128)(2,1)S(1)}, u32[]{:S(2)}, u32[]{:S(2)}) %all-to-all-start.2) | async-done | bytes 262176 | tf_op jit(solution)/shard_map/normed_home/all_to_all | solution.py:208
  183.0 12.9 %all_to_all.31 = bf16[8,32,512]{2,1,0:T(8,128)(2,1)S(1)} all-to-all(bf16[8,32,512]{2,1,0:T(8,128)(2,1)S(1)} %broadcast_in_dim.26), channel_id=1, replica_groups=mesh['section'=4,'dp'=8,'y'=4,'core'=2] {'dp'}, dimensions={0} | all-to-all | bytes 524288 | tf_op jit(solution)/shard_map/query_grad/all_to_all | solution.py:240
  195.9 3.7 %all-to-all-start.1 = ((bf16[8,16,4096]{2,1,0:T(8,128)(2,1)}), bf16[8,16,4096]{2,1,0:T(8,128)(2,1)S(1)}, u32[]{:S(2)}, u32[]{:S(2)}) async-start(bf16[8,16,4096]{2,1,0:T(8,128)(2,1)} %get-tuple-element.20), calls=%async_computation.1 | async-start | bytes 2097152 | tf_op jit(solution)/shard_map/passage_grads/all_to_all | solution.py:232
  200.7 24.1 %all-to-all-done.1 = bf16[8,16,4096]{2,1,0:T(8,128)(2,1)S(1)} async-done(((bf16[8,16,4096]{2,1,0:T(8,128)(2,1)}), bf16[8,16,4096]{2,1,0:T(8,128)(2,1)S(1)}, u32[]{:S(2)}, u32[]{:S(2)}) %all-to-all-start.1) | async-done | bytes 1048608 | tf_op jit(solution)/shard_map/passage_grads/all_to_all | solution.py:232
  224.9 3.5 %all-to-all-start.5 = ((bf16[4,128,512]{2,1,0:T(8,128)(2,1)}), bf16[4,128,512]{2,1,0:T(8,128)(2,1)S(1)}, u32[]{:S(2)}, u32[]{:S(2)}) async-start(bf16[4,128,512]{2,1,0:T(8,128)(2,1)} %bitcast.34), calls=%async_computation.5 | async-start | bytes 1048576 | tf_op jit(solution)/shard_map/weight_grad/all_to_all | solution.py:244
  229.2 7.2 %all-to-all-done.5 = bf16[4,128,512]{2,1,0:T(8,128)(2,1)S(1)} async-done(((bf16[4,128,512]{2,1,0:T(8,128)(2,1)}), bf16[4,128,512]{2,1,0:T(8,128)(2,1)S(1)}, u32[]{:S(2)}, u32[]{:S(2)}) %all-to-all-start.5) | async-done | bytes 524320 | tf_op jit(solution)/shard_map/weight_grad/all_to_all | solution.py:244
  (95 shorter events, 53.7 us)
Async XLA Ops:
  7.2 122.5 %all-gather.2.cloned.1.call-start = ((), (), s32[]{:S(2)}) async-start(), calls=%async_computation.6 | async-start | bytes 1216512 | tf_op jit(solution)/shard_map/passages/all_gather | solution.py:179
  7.2 5.5 %collective-permute-start = (bf16[128,512]{1,0:T(8,128)(2,1)}, bf16[128,512]{1,0:T(8,128)(2,1)S(1)}, u32[]{:S(2)}, u32[]{:S(2)}) collective-permute-start(bf16[128,512]{1,0:T(8,128)(2,1)} %param.10), channel_id=1, source_target_pairs={{0,2},{2,4},{4,6},{6,0},{1,3},{3,5},{5,7},{7,1},{8,10},{10,12},{12... | collective-permute-start | bytes 393224 | tf_op jit(solution)/shard_map/tower/ppermute | solution.py:23
  8.9 5.9 %collective-permute-start.2 = (bf16[128,512]{1,0:T(8,128)(2,1)}, bf16[128,512]{1,0:T(8,128)(2,1)S(1)}, u32[]{:S(2)}, u32[]{:S(2)}) collective-permute-start(bf16[128,512]{1,0:T(8,128)(2,1)} %param.10), channel_id=1, source_target_pairs={{0,6},{2,0},{4,2},{6,4},{1,7},{3,1},{5,3},{7,5},{8,14},{10,8},{12,... | collective-permute-start | bytes 393224 | tf_op jit(solution)/shard_map/tower/ppermute | solution.py:23
  9.6 8.0 %collective-permute-start.1 = (bf16[128,512]{1,0:T(8,128)(2,1)}, bf16[128,512]{1,0:T(8,128)(2,1)S(1)}, u32[]{:S(2)}, u32[]{:S(2)}) collective-permute-start(bf16[128,512]{1,0:T(8,128)(2,1)} %param.10), channel_id=1, source_target_pairs={{0,4},{2,6},{4,0},{6,2},{1,5},{3,7},{5,1},{7,3},{8,12},{10,14},{12... | collective-permute-start | bytes 393224 | tf_op jit(solution)/shard_map/tower/ppermute | solution.py:23
  24.3 6.8 %collective-permute-start.4 = (bf16[128,512]{1,0:T(8,128)(2,1)S(1)}, bf16[128,512]{1,0:T(8,128)(2,1)S(1)}, u32[]{:S(2)}, u32[]{:S(2)}) collective-permute-start(bf16[128,512]{1,0:T(8,128)(2,1)S(1)} %tower.4), channel_id=1, source_target_pairs={{0,64},{64,128},{128,192},{192,0},{1,65},{65,129},{129,193},{193,1... | collective-permute-start | bytes 393224 | tf_op jit(solution)/shard_map/tower/ppermute | solution.py:23
  31.1 5.5 %collective-permute-start.7 = (bf16[128,512]{1,0:T(8,128)(2,1)S(1)}, bf16[128,512]{1,0:T(8,128)(2,1)S(1)}, u32[]{:S(2)}, u32[]{:S(2)}) collective-permute-start(bf16[128,512]{1,0:T(8,128)(2,1)S(1)} %collective-permute-done.4), channel_id=1, source_target_pairs={{0,6},{2,0},{4,2},{6,4},{1,7},{3,1},{5,3},{7,5},{8,14},{10,8},{12,... | collective-permute-start | bytes 393224 | tf_op jit(solution)/shard_map/tower/ppermute | solution.py:23
  33.0 6.5 %collective-permute-start.6 = (bf16[128,512]{1,0:T(8,128)(2,1)S(1)}, bf16[128,512]{1,0:T(8,128)(2,1)S(1)}, u32[]{:S(2)}, u32[]{:S(2)}) collective-permute-start(bf16[128,512]{1,0:T(8,128)(2,1)S(1)} %collective-permute-done.4), channel_id=1, source_target_pairs={{0,4},{2,6},{4,0},{6,2},{1,5},{3,7},{5,1},{7,3},{8,12},{10,14},{12... | collective-permute-start | bytes 393224 | tf_op jit(solution)/shard_map/tower/ppermute | solution.py:23
  33.6 6.8 %collective-permute-start.5 = (bf16[128,512]{1,0:T(8,128)(2,1)S(1)}, bf16[128,512]{1,0:T(8,128)(2,1)S(1)}, u32[]{:S(2)}, u32[]{:S(2)}) collective-permute-start(bf16[128,512]{1,0:T(8,128)(2,1)S(1)} %collective-permute-done.4), channel_id=1, source_target_pairs={{0,2},{2,4},{4,6},{6,0},{1,3},{3,5},{5,7},{7,1},{8,10},{10,12},{12... | collective-permute-start | bytes 393224 | tf_op jit(solution)/shard_map/tower/ppermute | solution.py:23
  40.5 2.0 collective-permute-start.8
  44.1 6.8 %collective-permute-start.9 = (bf16[128,512]{1,0:T(8,128)(2,1)S(1)}, bf16[128,512]{1,0:T(8,128)(2,1)S(1)}, u32[]{:S(2)}, u32[]{:S(2)}) collective-permute-start(bf16[128,512]{1,0:T(8,128)(2,1)S(1)} %tower.5), channel_id=1, source_target_pairs={{0,64},{64,128},{128,192},{192,0},{1,65},{65,129},{129,193},{193,1... | collective-permute-start | bytes 393224 | tf_op jit(solution)/shard_map/tower/ppermute | solution.py:23
  50.9 6.6 %collective-permute-start.12 = (bf16[128,512]{1,0:T(8,128)(2,1)S(1)}, bf16[128,512]{1,0:T(8,128)(2,1)S(1)}, u32[]{:S(2)}, u32[]{:S(2)}) collective-permute-start(bf16[128,512]{1,0:T(8,128)(2,1)S(1)} %collective-permute-done.9), channel_id=1, source_target_pairs={{0,6},{2,0},{4,2},{6,4},{1,7},{3,1},{5,3},{7,5},{8,14},{10,8},{12,... | collective-permute-start | bytes 393224 | tf_op jit(solution)/shard_map/tower/ppermute | solution.py:23
  53.8 6.5 %collective-permute-start.11 = (bf16[128,512]{1,0:T(8,128)(2,1)S(1)}, bf16[128,512]{1,0:T(8,128)(2,1)S(1)}, u32[]{:S(2)}, u32[]{:S(2)}) collective-permute-start(bf16[128,512]{1,0:T(8,128)(2,1)S(1)} %collective-permute-done.9), channel_id=1, source_target_pairs={{0,4},{2,6},{4,0},{6,2},{1,5},{3,7},{5,1},{7,3},{8,12},{10,14},{12... | collective-permute-start | bytes 393224 | tf_op jit(solution)/shard_map/tower/ppermute | solution.py:23
  53.8 6.5 %collective-permute-start.10 = (bf16[128,512]{1,0:T(8,128)(2,1)S(1)}, bf16[128,512]{1,0:T(8,128)(2,1)S(1)}, u32[]{:S(2)}, u32[]{:S(2)}) collective-permute-start(bf16[128,512]{1,0:T(8,128)(2,1)S(1)} %collective-permute-done.9), channel_id=1, source_target_pairs={{0,2},{2,4},{4,6},{6,0},{1,3},{3,5},{5,7},{7,1},{8,10},{10,12},{12... | collective-permute-start | bytes 393224 | tf_op jit(solution)/shard_map/tower/ppermute | solution.py:23
  60.4 2.2 collective-permute-start.13
  64.1 6.8 %collective-permute-start.14 = (bf16[128,512]{1,0:T(8,128)(2,1)S(1)}, bf16[128,512]{1,0:T(8,128)(2,1)S(1)}, u32[]{:S(2)}, u32[]{:S(2)}) collective-permute-start(bf16[128,512]{1,0:T(8,128)(2,1)S(1)} %tower.6), channel_id=1, source_target_pairs={{0,64},{64,128},{128,192},{192,0},{1,65},{65,129},{129,193},{193,1... | collective-permute-start | bytes 393224 | tf_op jit(solution)/shard_map/tower/ppermute | solution.py:23
  71.0 6.7 %collective-permute-start.17 = (bf16[128,512]{1,0:T(8,128)(2,1)S(1)}, bf16[128,512]{1,0:T(8,128)(2,1)S(1)}, u32[]{:S(2)}, u32[]{:S(2)}) collective-permute-start(bf16[128,512]{1,0:T(8,128)(2,1)S(1)} %collective-permute-done.14), channel_id=1, source_target_pairs={{0,6},{2,0},{4,2},{6,4},{1,7},{3,1},{5,3},{7,5},{8,14},{10,8},{12,... | collective-permute-start | bytes 393224 | tf_op jit(solution)/shard_map/tower/ppermute | solution.py:23
  74.0 6.5 %collective-permute-start.16 = (bf16[128,512]{1,0:T(8,128)(2,1)S(1)}, bf16[128,512]{1,0:T(8,128)(2,1)S(1)}, u32[]{:S(2)}, u32[]{:S(2)}) collective-permute-start(bf16[128,512]{1,0:T(8,128)(2,1)S(1)} %collective-permute-done.14), channel_id=1, source_target_pairs={{0,4},{2,6},{4,0},{6,2},{1,5},{3,7},{5,1},{7,3},{8,12},{10,14},{12... | collective-permute-start | bytes 393224 | tf_op jit(solution)/shard_map/tower/ppermute | solution.py:23
  74.0 6.5 %collective-permute-start.15 = (bf16[128,512]{1,0:T(8,128)(2,1)S(1)}, bf16[128,512]{1,0:T(8,128)(2,1)S(1)}, u32[]{:S(2)}, u32[]{:S(2)}) collective-permute-start(bf16[128,512]{1,0:T(8,128)(2,1)S(1)} %collective-permute-done.14), channel_id=1, source_target_pairs={{0,2},{2,4},{4,6},{6,0},{1,3},{3,5},{5,7},{7,1},{8,10},{10,12},{12... | collective-permute-start | bytes 393224 | tf_op jit(solution)/shard_map/tower/ppermute | solution.py:23
  84.1 3.4 %collective-permute-start.21 = (bf16[128,512]{1,0:T(8,128)(2,1)S(1)}, bf16[128,512]{1,0:T(8,128)(2,1)S(1)}, u32[]{:S(2)}, u32[]{:S(2)}) collective-permute-start(bf16[128,512]{1,0:T(8,128)(2,1)S(1)} %tower.7), channel_id=1, source_target_pairs={{192,128},{193,129},{194,130},{195,131},{196,132},{197,133},{198,1... | collective-permute-start | bytes 393224 | tf_op jit(solution)/shard_map/to_sections/ppermute | solution.py:195
  84.8 2.8 %collective-permute-start.20 = (bf16[128,512]{1,0:T(8,128)(2,1)S(1)}, bf16[128,512]{1,0:T(8,128)(2,1)S(1)}, u32[]{:S(2)}, u32[]{:S(2)}) collective-permute-start(bf16[128,512]{1,0:T(8,128)(2,1)S(1)} %tower.7), channel_id=1, source_target_pairs={{192,64},{193,65},{194,66},{195,67},{196,68},{197,69},{198,70},{19... | collective-permute-start | bytes 393224 | tf_op jit(solution)/shard_map/to_sections/ppermute | solution.py:195
  85.5 8.6 %collective-permute-start.19 = (bf16[128,512]{1,0:T(8,128)(2,1)S(1)}, bf16[128,512]{1,0:T(8,128)(2,1)S(1)}, u32[]{:S(2)}, u32[]{:S(2)}) collective-permute-start(bf16[128,512]{1,0:T(8,128)(2,1)S(1)} %tower.7), channel_id=1, source_target_pairs={{192,0},{193,1},{194,2},{195,3},{196,4},{197,5},{198,6},{199,7},{2... | collective-permute-start | bytes 393224 | tf_op jit(solution)/shard_map/to_sections/ppermute | solution.py:195
  94.1 6.7 %collective-permute-start.24 = (bf16[128,512]{1,0:T(8,128)(2,1)S(1)}, bf16[128,512]{1,0:T(8,128)(2,1)S(1)}, u32[]{:S(2)}, u32[]{:S(2)}) collective-permute-start(bf16[128,512]{1,0:T(8,128)(2,1)S(1)} %add_add_fusion), channel_id=1, source_target_pairs={{0,6},{2,0},{4,2},{6,4},{1,7},{3,1},{5,3},{7,5},{8,14},{10,8},{12,... | collective-permute-start | bytes 393224 | tf_op jit(solution)/shard_map/head/ppermute | solution.py:23
  97.2 6.5 %collective-permute-start.23 = (bf16[128,512]{1,0:T(8,128)(2,1)S(1)}, bf16[128,512]{1,0:T(8,128)(2,1)S(1)}, u32[]{:S(2)}, u32[]{:S(2)}) collective-permute-start(bf16[128,512]{1,0:T(8,128)(2,1)S(1)} %add_add_fusion), channel_id=1, source_target_pairs={{0,4},{2,6},{4,0},{6,2},{1,5},{3,7},{5,1},{7,3},{8,12},{10,14},{12... | collective-permute-start | bytes 393224 | tf_op jit(solution)/shard_map/head/ppermute | solution.py:23
  97.2 6.5 %collective-permute-start.22 = (bf16[128,512]{1,0:T(8,128)(2,1)S(1)}, bf16[128,512]{1,0:T(8,128)(2,1)S(1)}, u32[]{:S(2)}, u32[]{:S(2)}) collective-permute-start(bf16[128,512]{1,0:T(8,128)(2,1)S(1)} %add_add_fusion), channel_id=1, source_target_pairs={{0,2},{2,4},{4,6},{6,0},{1,3},{3,5},{5,7},{7,1},{8,10},{10,12},{12... | collective-permute-start | bytes 393224 | tf_op jit(solution)/shard_map/head/ppermute | solution.py:23
  109.1 7.0 %collective-permute-start.28 = (bf16[128,512]{1,0:T(8,128)(2,1)S(1)}, bf16[128,512]{1,0:T(8,128)(2,1)S(1)}, u32[]{:S(2)}, u32[]{:S(2)}) collective-permute-start(bf16[128,512]{1,0:T(8,128)(2,1)S(1)} %get-tuple-element.15), channel_id=1, source_target_pairs={{0,6},{2,0},{4,2},{6,4},{1,7},{3,1},{5,3},{7,5},{8,14},{10,8},{12,... | collective-permute-start | bytes 393224 | tf_op jit(solution)/shard_map/score/ppermute | solution.py:23
  112.2 6.8 %collective-permute-start.27 = (bf16[128,512]{1,0:T(8,128)(2,1)S(1)}, bf16[128,512]{1,0:T(8,128)(2,1)S(1)}, u32[]{:S(2)}, u32[]{:S(2)}) collective-permute-start(bf16[128,512]{1,0:T(8,128)(2,1)S(1)} %get-tuple-element.15), channel_id=1, source_target_pairs={{0,4},{2,6},{4,0},{6,2},{1,5},{3,7},{5,1},{7,3},{8,12},{10,14},{12... | collective-permute-start | bytes 393224 | tf_op jit(solution)/shard_map/score/ppermute | solution.py:23
  112.2 7.1 %collective-permute-start.26 = (bf16[128,512]{1,0:T(8,128)(2,1)S(1)}, bf16[128,512]{1,0:T(8,128)(2,1)S(1)}, u32[]{:S(2)}, u32[]{:S(2)}) collective-permute-start(bf16[128,512]{1,0:T(8,128)(2,1)S(1)} %get-tuple-element.15), channel_id=1, source_target_pairs={{0,2},{2,4},{4,6},{6,0},{1,3},{3,5},{5,7},{7,1},{8,10},{10,12},{12... | collective-permute-start | bytes 393224 | tf_op jit(solution)/shard_map/score/ppermute | solution.py:23
  119.4 10.2 %collective-permute-start.29 = (bf16[4,128,512]{2,1,0:T(8,128)(2,1)S(1)}, bf16[4,128,512]{2,1,0:T(8,128)(2,1)S(1)}, u32[]{:S(2)}, u32[]{:S(2)}) collective-permute-start(bf16[4,128,512]{2,1,0:T(8,128)(2,1)S(1)} %pad_maximum_fusion.5.near), channel_id=1, source_target_pairs={{0,1},{1,0},{2,3},{3,2},{4,5},{5,4},{6,7},{7,6},{8,9},{9,8},{10,11... | collective-permute-start | bytes 1572872 | tf_op jit(solution)/shard_map/score/ppermute | solution.py:23
  152.4 15.6 %all-to-all-start.3 = ((bf16[16,32,512]{2,1,0:T(8,128)(2,1)}), bf16[16,32,512]{2,1,0:T(8,128)(2,1)S(1)}, u32[]{:S(2)}, u32[]{:S(2)}) async-start(bf16[16,32,512]{2,1,0:T(8,128)(2,1)} %bitcast.32), calls=%async_computation.3 | async-start | bytes 1048576 | tf_op jit(solution)/shard_map/query_grad/all_to_all | solution.py:236
  168.0 14.9 %all-to-all-start.2 = ((bf16[8,32,512]{2,1,0:T(8,128)(2,1)}), bf16[8,32,512]{2,1,0:T(8,128)(2,1)S(1)}, u32[]{:S(2)}, u32[]{:S(2)}) async-start(bf16[8,32,512]{2,1,0:T(8,128)(2,1)} %reshape.27), calls=%async_computation.2 | async-start | bytes 524288 | tf_op jit(solution)/shard_map/normed_home/all_to_all | solution.py:208
  195.9 29.0 %all-to-all-start.1 = ((bf16[8,16,4096]{2,1,0:T(8,128)(2,1)}), bf16[8,16,4096]{2,1,0:T(8,128)(2,1)S(1)}, u32[]{:S(2)}, u32[]{:S(2)}) async-start(bf16[8,16,4096]{2,1,0:T(8,128)(2,1)} %get-tuple-element.20), calls=%async_computation.1 | async-start | bytes 2097152 | tf_op jit(solution)/shard_map/passage_grads/all_to_all | solution.py:232
  224.9 11.5 %all-to-all-start.5 = ((bf16[4,128,512]{2,1,0:T(8,128)(2,1)}), bf16[4,128,512]{2,1,0:T(8,128)(2,1)S(1)}, u32[]{:S(2)}, u32[]{:S(2)}) async-start(bf16[4,128,512]{2,1,0:T(8,128)(2,1)} %bitcast.34), calls=%async_computation.5 | async-start | bytes 1048576 | tf_op jit(solution)/shard_map/weight_grad/all_to_all | solution.py:244
  (15 other events, 299.0 us)
Sparse Core Ops, SparseCore 0:
  87.6 41.9 all-gather.1

commit v2 on v1

--- a/solution.py
+++ b/solution.py
@@ -1,5 +1,4 @@
 import functools
-import math
 
 import jax
 import jax.numpy as jnp
@@ -15,7 +14,9 @@
 BF16 = jnp.bfloat16
 VMEM = pl.BlockSpec(memory_space=pltpu.VMEM)
 SMEM = pl.BlockSpec(memory_space=pltpu.SMEM)
-PARAMS = pltpu.CompilerParams(vmem_limit_bytes=48 * 1024 * 1024)
+LOOSE = pl.BlockSpec(memory_space=pltpu.HBM)
+COST = pl.CostEstimate(flops=1024, bytes_accessed=1024, transcendentals=0)
+PARAMS = pltpu.CompilerParams(vmem_limit_bytes=16 * 1024 * 1024)
 
 
 def turned(block, axis, steps):
@@ -26,6 +27,21 @@
 def spread(block):
     count = lax.axis_size("y")
     near = jnp.stack([block] + [turned(block, "y", k) for k in range(1, count)])
+    return near, turned(near, "core", 1)
+
+
+def stack_kernel(place, *rest):
+    out = rest[-1]
+    for k in range(out.shape[0]):
+        out[k] = rest[k][...]
+
+
+def spread_after(block, place, loose):
+    if not loose:
+        return spread(block)
+    count = lax.axis_size("y")
+    blocks = [block] + [turned(block, "y", k) for k in range(1, count)]
+    (near,) = call(stack_kernel, [((count,) + block.shape, block.dtype)], [place] + blocks, loose)
     return near, turned(near, "core", 1)
 
 
@@ -51,29 +67,101 @@
             yield ref, k, lax.rem(y - k + count, count) * 2 + c
 
 
+def at_block(owner, wide):
+    return pl.ds(pl.multiple_of(owner * wide, wide), wide)
+
+
 def mixed_rows(place, near, far, weight, normed=None):
     scale = row_scale(near, far)
     wide = near.shape[2]
     total = 0.0
     for ref, k, owner in owners(place, near, far):
         rows = (ref[k].astype(F32) * scale).astype(BF16)
-        at = pl.ds(pl.multiple_of(owner * wide, wide), wide)
+        at = at_block(owner, wide)
         if normed is not None:
             normed[:, at] = rows
         total = total + jnp.dot(rows, weight[at, :], preferred_element_type=F32)
     return total
 
 
-def layer_kernel(place, near, far, weight, out):
+def load_kernel(place, source, *rest):
+    out, sem = rest[-2:]
+    copy = pltpu.make_async_copy(source, out, sem)
+    copy.start()
+    copy.wait()
+
+
+def loaded(place, weight, after):
+    (out,) = call(
+        load_kernel,
+        [(weight.shape, weight.dtype)],
+        [place, weight],
+        after,
+        scratch=[pltpu.SemaphoreType.DMA],
+        far_off=(1,),
+    )
+    return out
+
+
+def layer_kernel(place, near, far, weight, *rest):
+    out = rest[-1]
     mixed = mixed_rows(place, near, far, weight)
     out[...] = (near[0].astype(F32) + silu(mixed)).astype(BF16)
 
 
-def head_kernel(place, near, far, weight, emb, slope, normed):
+def head_kernel(place, near, far, weight, emb, slope, pieces, normed):
     head = mixed_rows(place, near, far, weight, normed)
     sig = jax.nn.sigmoid(head)
     emb[...] = (near[0].astype(F32) + head * sig).astype(BF16)
     slope[...] = sig * (1.0 + head * (1.0 - sig))
+    cycle, rows, taken = pieces.shape
+    sections = normed.shape[0] // rows
+    piece = taken // sections
+    own = pl.ds(pl.multiple_of(place[0] * rows, rows), rows)
+    for k in range(cycle):
+        for s in range(sections):
+            at = (s * cycle + k) * piece
+            pieces[k, :, s * piece : (s + 1) * piece] = normed[own, at : at + piece]
+
+
+def head_grad_kernel(place, parts, slope, *rest):
+    out = rest[-1]
+    cycle, rows, wide = out.shape
+    total = 0.0
+    for k in range(parts.shape[0]):
+        total = total + parts[k].astype(F32)
+    own = pl.ds(pl.multiple_of(place[0] * rows, rows), rows)
+    grad = (total * slope[own, :]).astype(BF16)
+    for k in range(cycle):
+        out[k] = grad
+
+
+def weight_grad_kernel(place, grads, pieces, out):
+    cycle, rows, wide = grads.shape
+    taken = out.shape[1]
+    part = lax.dot_general(
+        pieces[...].reshape(cycle * rows, pieces.shape[2]),
+        grads[...].reshape(cycle * rows, wide),
+        (((0,), (0,)), ((), ())),
+        preferred_element_type=F32,
+    ).astype(BF16)
+    for s in range(out.shape[0]):
+        out[s] = part[s * taken : (s + 1) * taken]
+
+
+def update_kernel(
+    place, parts, master, moment_one, moment_two, grads, new_master, new_one, new_two, new_grads
+):
+    grad = 0.0
+    for k in range(parts.shape[0]):
+        grad = grad + parts[k].astype(F32)
+    one = 0.9 * moment_one[...] + 0.1 * grad
+    two = 0.95 * moment_two[...] + 0.05 * grad * grad
+    update = one / correct_one / (jnp.sqrt(two / correct_two) + 1e-08)
+    new_master[...] = master[...] - 0.001 * (update + 0.1 * master[...])
+    new_one[...] = one
+    new_two[...] = two
+    new_grads[...] = grads[...].astype(F32)
 
 
 def masks(place, passages, query_cells, positives, sizes):
@@ -142,14 +230,19 @@
             grads[d, :, j : j + wide] = part[d * block : (d + 1) * block]
 
 
-def call(kernel, outs, *args):
+def call(kernel, outs, args, loose=(), scratch=(), far_off=()):
+    specs = [SMEM] + [VMEM] * (len(args) - 1) + [LOOSE] * len(loose)
+    for k in far_off:
+        specs[k] = LOOSE
     return pl.pallas_call(
         kernel,
         out_shape=[jax.ShapeDtypeStruct(shape, dtype) for shape, dtype in outs],
-        in_specs=[SMEM] + [VMEM] * (len(args) - 1),
+        in_specs=specs,
         out_specs=[VMEM] * len(outs),
+        scratch_shapes=scratch,
         compiler_params=PARAMS,
-    )(*args)
+        cost_estimate=COST,
+    )(*args, *loose)
 
 
 def shards(
@@ -174,17 +267,24 @@
     queries, wide = query_inputs.shape
     block, width = passages.shape
     sizes = (width, cycle, 2 * count, block)
+    rows = queries // sections
+    taken = width // cycle
     with jax.named_scope("passages"):
         cells = jnp.broadcast_to(passage_cells.astype(BF16)[:, None], (block, queries))
-        held = lax.all_gather(
-            jnp.concatenate([passages, cells], axis=1), "dp", axis=0, tiled=True
-        )
+        own = jnp.concatenate([passages, cells], axis=1)
+        held = lax.all_gather(own, "dp", axis=0, tiled=True)
+    section_weights = pltpu.with_memory_space_constraint(section_weights, pltpu.HBM)
+    head_weight = pltpu.with_memory_space_constraint(head_weight, pltpu.HBM)
     local = query_inputs
     for layer in range(sections):
         with jax.named_scope("tower"):
-            near, far = spread(local)
+            after = [local, held] if layer + 2 == sections else [local]
+            layer_weight = loaded(place, section_weights, after)
+            near, far = spread_after(local, place, [layer_weight])
             (local,) = call(
-                layer_kernel, [((queries, wide), BF16)], place, near, far, section_weights
+                layer_kernel,
+                [((queries, wide), BF16)],
+                [place, near, far, layer_weight],
             )
             if layer + 1 < sections:
                 local = turned(local, "section", 1)
@@ -194,20 +294,22 @@
         for other in range(last):
             final = final + lax.ppermute(local, "section", [(last, other)])
     with jax.named_scope("head"):
-        near, far = spread(final)
-        query_cols, slope, normed = call(
+        head_weight = loaded(place, head_weight, [final])
+        near, far = spread_after(final, place, [head_weight])
+        query_cols, slope, pieces = call(
             head_kernel,
-            [((queries, wide), BF16), ((queries, wide), F32), ((queries, width), BF16)],
-            place, near, far, head_weight,
-        )
-    rows = queries // sections
+            [
+                ((queries, wide), BF16),
+                ((queries, wide), F32),
+                ((cycle, rows, taken), BF16),
+            ],
+            [place, near, far, head_weight],
+            scratch=[pltpu.VMEM((queries, width), BF16)],
+        )
     with jax.named_scope("normed_home"):
-        mine = lax.dynamic_slice_in_dim(normed, section_at * rows, rows, 0)
-        mine = mine.reshape(rows, sections, cycle, width // (sections * cycle))
-        mine = mine.transpose(2, 0, 1, 3).reshape(cycle, rows, width // cycle)
-        normed_all = lax.all_to_all(mine, "dp", 0, 0).reshape(cycle * rows, width // cycle)
+        pieces = lax.all_to_all(pieces, "dp", 0, 0)
     with jax.named_scope("score"):
-        near, far = spread(query_cols)
+        near, far = spread_after(query_cols, place, [pieces])
         row_cells, row_positives = query_cells[None, :], positives[None, :]
         group = sections * count * 2
         score, stats, full = call(
@@ -217,36 +319,41 @@
                 ((group, 8, queries), F32),
                 ((queries, width), BF16),
             ],
-            place, near, far, held, row_cells, row_positives,
+            [place, near, far, held, row_cells, row_positives],
         )
     with jax.named_scope("stats"):
         stats = lax.all_to_all(stats, ("section", "y", "core"), 0, 0)
     with jax.named_scope("grad"):
-        half = (sections, count, rows, wide)
+        part = (sections, count, rows, wide)
         loss, send, keep, grads = call(
             functools.partial(grad_kernel, sizes),
-            [((1, queries), F32), (half, BF16), (half, BF16), ((cycle, block, width), BF16)],
-            place, stats, score, full, held, row_cells, row_positives,
+            [((1, queries), F32), (part, BF16), (part, BF16), ((cycle, block, width), BF16)],
+            [place, stats, score, full, held, row_cells, row_positives],
         )
     with jax.named_scope("passage_grads"):
-        grads = lax.all_to_all(grads, "dp", 0, 0)
-        passage_grads = jnp.sum(grads.astype(F32), axis=0)
+        passage_grads = lax.psum_scatter(
+            grads.reshape(cycle * block, width), "dp", scatter_dimension=0, tiled=True
+        )
     with jax.named_scope("query_grad"):
         keep = (keep.astype(F32) + turned(send, "core", 1).astype(F32)).astype(BF16)
         parts = lax.all_to_all(keep.reshape(sections * count, rows, wide), ("section", "y"), 0, 0)
-        query_grad = jnp.sum(parts.astype(F32), axis=0)
-        head_grad = query_grad * lax.dynamic_slice_in_dim(slope, section_at * rows, rows, 0)
-        head_grad = jnp.broadcast_to(head_grad.astype(BF16)[None], (cycle, rows, wide))
-        head_grad = lax.all_to_all(head_grad, "dp", 0, 0).reshape(cycle * rows, wide)
+        (head_grad,) = call(
+            head_grad_kernel, [((cycle, rows, wide), BF16)], [place, parts, slope]
+        )
+        head_grad = lax.all_to_all(head_grad, "dp", 0, 0)
     with jax.named_scope("weight_grad"):
-        part = jnp.einsum("qd,qc->dc", normed_all, head_grad, preferred_element_type=F32)
-        part = part.astype(BF16).reshape(sections, width // (sections * cycle), wide)
+        (part,) = call(
+            weight_grad_kernel,
+            [((sections, taken // sections, wide), BF16)],
+            [place, head_grad, pieces],
+        )
         part = lax.all_to_all(part, "section", 0, 0)
-        weight_grad = jnp.sum(part.astype(F32), axis=0)
-    new_moment_one = 0.9 * moment_one + 0.1 * weight_grad
-    new_moment_two = 0.95 * moment_two + 0.05 * weight_grad * weight_grad
-    update = new_moment_one / correct_one / (jnp.sqrt(new_moment_two / correct_two) + 1e-08)
-    new_master = master - 0.001 * (update + 0.1 * master)
+        tile = (master.shape, F32)
+        new_master, new_moment_one, new_moment_two, passage_grads = call(
+            update_kernel,
+            [tile, tile, tile, ((block, width), F32)],
+            [place, part, master, moment_one, moment_two, passage_grads],
+        )
     return (loss[0], passage_grads, new_master, new_moment_one, new_moment_two)
 
 

time: 245 us -> 205 us (0.84)
  waiting for transfers between devices: 126 us -> 51.8 us
  blocking collectives: 26.8 us -> 55.4 us
  Pallas kernels: 12.9 us -> 32 us
  starting transfers between devices: 52.5 us -> 45.5 us
  local copies, waits for them, and re-layouts: 5.75 us -> 3.14 us
  other arithmetic: 5.09 us -> 2.49 us
    all_to_all x4 -> x1, waiting for transfers between devices: 51.6 us -> 2.2 us  [shards(): pieces = lax.all_to_all(pieces, 'dp', 0, 0)]
    all_to_all x1 -> x3, blocking collectives: 12.9 us -> 42.9 us  [the longest x1 17.4 us: shards(): head_grad = lax.all_to_all(head_grad, 'dp', 0, 0)]
    pallas_call x7 -> x21, Pallas kernels: 12.9 us -> 32 us  [call(): pl.pallas_call(kernel, out_shape=[jax.ShapeDtypeStruct(shape, dtype) for...]
    ppermute x28, waiting for transfers between devices: 57.4 us -> 42.2 us  [turned(): lax.ppermute(block, axis, [(i, (i + steps) % count) for i in range(count)])]
    all_gather x1, waiting for transfers between devices: 10.1 us -> 0.01 us  [shards(): held = lax.all_gather(own, 'dp', axis=0, tiled=True)]
    all_to_all x4 -> x1, starting transfers between devices: 16.3 us -> 8.45 us  [shards(): pieces = lax.all_to_all(pieces, 'dp', 0, 0)]
  transfers between devices with their start and end apart: 36 -> 34, of which waited for: 30 -> 20; matrix products, arithmetic and copies ran while one was open for 2% -> 0% of each run, Pallas kernels for 1% -> 10%
where the time goes in v2:
time: 205 us
  blocking collectives  55.4 us (27%)
  waiting for transfers between devices  51.8 us (25%)
  starting transfers between devices  45.5 us (22%)
  Pallas kernels  32 us (16%)
  between operations  14.4 us (7%)
  local copies, waits for them, and re-layouts  3.14 us (2%)
  other arithmetic  2.49 us (1%)
    ppermute x28, waiting for transfers between devices, turned(): lax.ppermute(block, axis, [(i, (i + steps) % count) for i in range(count)])  42.2 us
    ppermute x28, starting transfers between devices, turned(): lax.ppermute(block, axis, [(i, (i + steps) % count) for i in range(count)])  34.3 us
    pallas_call x21, Pallas kernels, call(): pl.pallas_call(kernel, out_shape=[jax.ShapeDtypeStruct(shape, dtype) for...  32 us
    all_to_all x1, blocking collectives, shards(): head_grad = lax.all_to_all(head_grad, 'dp', 0, 0)  17.4 us
    all_to_all x1, blocking collectives, shards(): lax.all_to_all(keep.reshape(sections * count, rows, wide), ('section', 'y...  15 us
    all_to_all x1, blocking collectives, shards(): stats = lax.all_to_all(stats, ('section', 'y', 'core'), 0, 0)  12.6 us
    all_to_all x1, blocking collectives, shards(): part = lax.all_to_all(part, 'section', 0, 0)  10.5 us
    all_to_all x1, starting transfers between devices, shards(): pieces = lax.all_to_all(pieces, 'dp', 0, 0)  8.45 us
  transfers between devices with their start and end apart: 34, of which 20 were waited for; matrix products, arithmetic and copies ran while one was open for 0% of the time, Pallas kernels for 10%

profile of v2, /device:TPU:8, one launch (start us, length us, event | category | flops | bytes accessed | tf_op | source)
XLA Modules:
  0.0 204.7 jit_solution(5469174952840664444)
XLA Ops:
  9.5 2.3 %collective-permute-start.2 = (bf16[128,512]{1,0:T(8,128)(2,1)}, bf16[128,512]{1,0:T(8,128)(2,1)S(1)}, u32[]{:S(2)}, u32[]{:S(2)}) collective-permute-start(bf16[128,512]{1,0:T(8,128)(2,1)} %rest_0_.3), channel_id=1, source_target_pairs={{0,6},{2,0},{4,2},{6,4},{1,7},{3,1},{5,3},{7,5},{8,14},{10,8},{12,... | collective-permute-start | bytes 393224 | tf_op jit(solution)/shard_map/tower/ppermute | solution.py:24
  15.5 2.7 %tower.12.rest_4_.weight = bf16[4096,512]{1,0:T(8,128)(2,1)S(1)} custom-call(s32[4]{0:T(128)S(1)} %pad_add_fusion.place, bf16[4096,512]{1,0:T(8,128)(2,1)} %source.8, bf16[128,512]{1,0:T(8,128)(2,1)S(1)} %copy-done.2), custom_call_target="tpu_custom_call" | custom-call | flops 1024 | bytes 1024 | tf_op jit(solution)/shard_map/tower/pallas_call | solution.py:237
  20.3 1.9 collective-permute-done.3.far
  25.4 5.3 %collective-permute-done.4.rest_0_ = bf16[128,512]{1,0:T(8,128)(2,1)S(1)} collective-permute-done((bf16[128,512]{1,0:T(8,128)(2,1)S(1)}, bf16[128,512]{1,0:T(8,128)(2,1)S(1)}, u32[]{:S(2)}, u32[]{:S(2)}) %collective-permute-start.4) | collective-permute-done | bytes 131104 | tf_op jit(solution)/shard_map/tower/ppermute | solution.py:24
  30.6 2.9 %collective-permute-start.7 = (bf16[128,512]{1,0:T(8,128)(2,1)S(1)}, bf16[128,512]{1,0:T(8,128)(2,1)S(1)}, u32[]{:S(2)}, u32[]{:S(2)}) collective-permute-start(bf16[128,512]{1,0:T(8,128)(2,1)S(1)} %collective-permute-done.4.rest_0_), channel_id=1, source_target_pairs={{0,6},{2,0},{4,2},{6,4},{1,7},{3,1},{5,3},{7,5},{8,14},{10,8},{12,... | collective-permute-start | bytes 393224 | tf_op jit(solution)/shard_map/tower/ppermute | solution.py:24
  33.6 2.0 collective-permute-start.5
  35.6 2.8 %tower.15.rest_4_.weight = bf16[4096,512]{1,0:T(8,128)(2,1)S(1)} custom-call(s32[4]{0:T(128)S(1)} %pad_add_fusion.place, bf16[4096,512]{1,0:T(8,128)(2,1)} %source.8, bf16[128,512]{1,0:T(8,128)(2,1)S(1)} %collective-permute-done.4.rest_0_), custom_call_target="tpu_custom_call" | custom-call | flops 1024 | bytes 1024 | tf_op jit(solution)/shard_map/tower/pallas_call | solution.py:237
  40.7 1.9 collective-permute-done.8.far
  44.5 6.4 %collective-permute-done.9.rest_0_ = bf16[128,512]{1,0:T(8,128)(2,1)S(1)} collective-permute-done((bf16[128,512]{1,0:T(8,128)(2,1)S(1)}, bf16[128,512]{1,0:T(8,128)(2,1)S(1)}, u32[]{:S(2)}, u32[]{:S(2)}) %collective-permute-start.9) | collective-permute-done | bytes 131104 | tf_op jit(solution)/shard_map/tower/ppermute | solution.py:24
  51.0 2.8 %collective-permute-start.12 = (bf16[128,512]{1,0:T(8,128)(2,1)S(1)}, bf16[128,512]{1,0:T(8,128)(2,1)S(1)}, u32[]{:S(2)}, u32[]{:S(2)}) collective-permute-start(bf16[128,512]{1,0:T(8,128)(2,1)S(1)} %collective-permute-done.9.rest_0_), channel_id=1, source_target_pairs={{0,6},{2,0},{4,2},{6,4},{1,7},{3,1},{5,3},{7,5},{8,14},{10,8},{12,... | collective-permute-start | bytes 393224 | tf_op jit(solution)/shard_map/tower/ppermute | solution.py:24
  53.8 2.5 %collective-permute-start.10 = (bf16[128,512]{1,0:T(8,128)(2,1)S(1)}, bf16[128,512]{1,0:T(8,128)(2,1)S(1)}, u32[]{:S(2)}, u32[]{:S(2)}) collective-permute-start(bf16[128,512]{1,0:T(8,128)(2,1)S(1)} %collective-permute-done.9.rest_0_), channel_id=1, source_target_pairs={{0,2},{2,4},{4,6},{6,0},{1,3},{3,5},{5,7},{7,1},{8,10},{10,12},{12... | collective-permute-start | bytes 393224 | tf_op jit(solution)/shard_map/tower/ppermute | solution.py:24
  57.6 2.7 %tower.18.rest_4_.weight = bf16[4096,512]{1,0:T(8,128)(2,1)S(1)} custom-call(s32[4]{0:T(128)S(1)} %pad_add_fusion.place, bf16[4096,512]{1,0:T(8,128)(2,1)} %source.8, bf16[128,512]{1,0:T(8,128)(2,1)S(1)} %collective-permute-done.9.rest_0_, bf16[128,4224]{1,0:T(8,128)(2,1)S(1)} %copy-done), custom_call_target="tpu_custom_call" | custom-call | flops 1024 | bytes 1024 | tf_op jit(solution)/shard_map/tower/pallas_call | solution.py:237
  64.8 6.7 %collective-permute-done.14.rest_0_ = bf16[128,512]{1,0:T(8,128)(2,1)S(1)} collective-permute-done((bf16[128,512]{1,0:T(8,128)(2,1)S(1)}, bf16[128,512]{1,0:T(8,128)(2,1)S(1)}, u32[]{:S(2)}, u32[]{:S(2)}) %collective-permute-start.14) | collective-permute-done | bytes 131104 | tf_op jit(solution)/shard_map/tower/ppermute | solution.py:24
  71.5 3.2 %collective-permute-start.17 = (bf16[128,512]{1,0:T(8,128)(2,1)S(1)}, bf16[128,512]{1,0:T(8,128)(2,1)S(1)}, u32[]{:S(2)}, u32[]{:S(2)}) collective-permute-start(bf16[128,512]{1,0:T(8,128)(2,1)S(1)} %collective-permute-done.14.rest_0_), channel_id=1, source_target_pairs={{0,6},{2,0},{4,2},{6,4},{1,7},{3,1},{5,3},{7,5},{8,14},{10,8},{12,... | collective-permute-start | bytes 393224 | tf_op jit(solution)/shard_map/tower/ppermute | solution.py:24
  74.8 2.0 collective-permute-start.15
  76.8 2.7 %tower.21.rest_4_.weight = bf16[4096,512]{1,0:T(8,128)(2,1)S(1)} custom-call(s32[4]{0:T(128)S(1)} %pad_add_fusion.place, bf16[4096,512]{1,0:T(8,128)(2,1)} %source.8, bf16[128,512]{1,0:T(8,128)(2,1)S(1)} %collective-permute-done.14.rest_0_), custom_call_target="tpu_custom_call" | custom-call | flops 1024 | bytes 1024 | tf_op jit(solution)/shard_map/tower/pallas_call | solution.py:237
  81.9 1.9 collective-permute-done.18.far
  88.0 7.3 %collective-permute-done.19 = bf16[128,512]{1,0:T(8,128)(2,1)S(1)} collective-permute-done((bf16[128,512]{1,0:T(8,128)(2,1)S(1)}, bf16[128,512]{1,0:T(8,128)(2,1)S(1)}, u32[]{:S(2)}, u32[]{:S(2)}) %collective-permute-start.19) | collective-permute-done | bytes 131104 | tf_op jit(solution)/shard_map/to_sections/ppermute | solution.py:295
  95.4 2.9 %collective-permute-start.24 = (bf16[128,512]{1,0:T(8,128)(2,1)S(1)}, bf16[128,512]{1,0:T(8,128)(2,1)S(1)}, u32[]{:S(2)}, u32[]{:S(2)}) collective-permute-start(bf16[128,512]{1,0:T(8,128)(2,1)S(1)} %add_add_fusion.rest_0_), channel_id=1, source_target_pairs={{0,6},{2,0},{4,2},{6,4},{1,7},{3,1},{5,3},{7,5},{8,14},{10,8},{12,... | collective-permute-start | bytes 393224 | tf_op jit(solution)/shard_map/head/ppermute | solution.py:24
  98.3 2.4 %collective-permute-start.22 = (bf16[128,512]{1,0:T(8,128)(2,1)S(1)}, bf16[128,512]{1,0:T(8,128)(2,1)S(1)}, u32[]{:S(2)}, u32[]{:S(2)}) collective-permute-start(bf16[128,512]{1,0:T(8,128)(2,1)S(1)} %add_add_fusion.rest_0_), channel_id=1, source_target_pairs={{0,2},{2,4},{4,6},{6,0},{1,3},{3,5},{5,7},{7,1},{8,10},{10,12},{12... | collective-permute-start | bytes 393224 | tf_op jit(solution)/shard_map/head/ppermute | solution.py:24
  100.7 2.7 %head.3.rest_4_.weight = bf16[4096,512]{1,0:T(8,128)(2,1)S(1)} custom-call(s32[4]{0:T(128)S(1)} %pad_add_fusion.place, bf16[4096,512]{1,0:T(8,128)(2,1)} %source.9, bf16[128,512]{1,0:T(8,128)(2,1)S(1)} %add_add_fusion.rest_0_), custom_call_target="tpu_custom_call" | custom-call | flops 1024 | bytes 1024 | tf_op jit(solution)/shard_map/head/pallas_call | solution.py:237
  107.4 2.1 %head.5 = (bf16[128,512]{1,0:T(8,128)(2,1)S(1)}, f32[128,512]{1,0:T(8,128)S(1)}, bf16[8,32,512]{2,1,0:T(8,128)(2,1)}) custom-call(s32[4]{0:T(128)S(1)} %pad_add_fusion.place, bf16[4,128,512]{2,1,0:T(8,128)(2,1)S(1)} %head.4.near, bf16[4,128,512]{2,1,0:T(8,128)(2,1)S(1)} %collective-permute-done.25.far, bf16[4096,512]{1,0:T(8,128)(2,1)S(1)} %head.3.rest_4_.weight), custom_call_target="tpu_custom_call" | custom-call | flops 1024 | bytes 1024 | tf_op jit(solution)/shard_map/head/pallas_call | solution.py:237
  109.5 8.4 %all-to-all-start = ((bf16[8,32,512]{2,1,0:T(8,128)(2,1)}), bf16[8,32,512]{2,1,0:T(8,128)(2,1)S(1)}, u32[]{:S(2)}, u32[]{:S(2)}) async-start(bf16[8,32,512]{2,1,0:T(8,128)(2,1)} %get-tuple-element.20), calls=%async_computation | async-start | bytes 524288 | tf_op jit(solution)/shard_map/normed_home/all_to_all | solution.py:310
  118.0 3.3 %collective-permute-start.28 = (bf16[128,512]{1,0:T(8,128)(2,1)S(1)}, bf16[128,512]{1,0:T(8,128)(2,1)S(1)}, u32[]{:S(2)}, u32[]{:S(2)}) collective-permute-start(bf16[128,512]{1,0:T(8,128)(2,1)S(1)} %get-tuple-element.19.rest_0_), channel_id=1, source_target_pairs={{0,6},{2,0},{4,2},{6,4},{1,7},{3,1},{5,3},{7,5},{8,14},{10,8},{12,... | collective-permute-start | bytes 393224 | tf_op jit(solution)/shard_map/score/ppermute | solution.py:24
  121.3 2.0 collective-permute-start.26
  125.2 2.6 %collective-permute-done.27.rest_2_ = bf16[128,512]{1,0:T(8,128)(2,1)S(1)} collective-permute-done((bf16[128,512]{1,0:T(8,128)(2,1)S(1)}, bf16[128,512]{1,0:T(8,128)(2,1)S(1)}, u32[]{:S(2)}, u32[]{:S(2)}) %collective-permute-start.27) | collective-permute-done | bytes 131104 | tf_op jit(solution)/shard_map/score/ppermute | solution.py:24
  127.9 2.2 %all-to-all-done.rest_4_.pieces = bf16[8,32,512]{2,1,0:T(8,128)(2,1)S(1)} async-done(((bf16[8,32,512]{2,1,0:T(8,128)(2,1)}), bf16[8,32,512]{2,1,0:T(8,128)(2,1)S(1)}, u32[]{:S(2)}, u32[]{:S(2)}) %all-to-all-start) | async-done | bytes 262176 | tf_op jit(solution)/shard_map/normed_home/all_to_all | solution.py:310
  134.0 12.6 %all_to_all.25.stats = f32[32,8,128]{2,1,0:T(8,128)S(1)} all-to-all(f32[32,8,128]{2,1,0:T(8,128)S(1)} %get-tuple-element.21), channel_id=1, replica_groups=mesh['section'=4,'dp'=8,'y'=4,'core'=2] {'section','y','core'}, dimensions={0} | all-to-all | bytes 262144 | tf_op jit(solution)/shard_map/stats/all_to_all | solution.py:325
  146.6 2.3 %grad.1 = (f32[1,128]{1,0:T(1,128)}, bf16[4,4,32,512]{3,2,1,0:T(8,128)(2,1)S(1)}, bf16[4,4,32,512]{3,2,1,0:T(8,128)(2,1)S(1)}, bf16[8,16,4096]{2,1,0:T(8,128)(2,1)}) custom-call(s32[4]{0:T(128)S(1)} %pad_add_fusion.place, f32[32,8,128]{2,1,0:T(8,128)S(1)} %all_to_all.25.stats, f32[128,128]{1,0:T(8,128)S(1)} %get-tuple-element.22.score, ...), custom_call_target="tpu_custom_call" | custom-call | flops 1024 | bytes 1024 | tf_op jit(solution)/shard_map/grad/pallas_call | solution.py:237
  151.0 15.0 %all_to_all.26.parts = bf16[16,32,512]{2,1,0:T(8,128)(2,1)S(1)} all-to-all(bf16[16,32,512]{2,1,0:T(8,128)(2,1)S(1)} %bitcast.13), channel_id=1, replica_groups=mesh['section'=4,'dp'=8,'y'=4,'core'=2] {'section','y'}, dimensions={0} | all-to-all | bytes 1048576 | tf_op jit(solution)/shard_map/query_grad/all_to_all | solution.py:339
  166.6 17.4 %all_to_all.27.grads = bf16[8,32,512]{2,1,0:T(8,128)(2,1)S(1)} all-to-all(bf16[8,32,512]{2,1,0:T(8,128)(2,1)S(1)} %query_grad.1), channel_id=1, replica_groups=mesh['section'=4,'dp'=8,'y'=4,'core'=2] {'dp'}, dimensions={0} | all-to-all | bytes 524288 | tf_op jit(solution)/shard_map/query_grad/all_to_all | solution.py:343
  184.9 10.5 %all_to_all.28.parts = bf16[4,128,512]{2,1,0:T(8,128)(2,1)S(1)} all-to-all(bf16[4,128,512]{2,1,0:T(8,128)(2,1)S(1)} %weight_grad.2), channel_id=1, replica_groups=mesh['section'=4,'dp'=8,'y'=4,'core'=2] {'section'}, dimensions={0} | all-to-all | bytes 1048576 | tf_op jit(solution)/shard_map/weight_grad/all_to_all | solution.py:350
  (87 shorter events, 43.7 us)
Async XLA Ops:
  7.2 49.2 %all-gather.2.cloned.1.call-start = ((), (), s32[]{:S(2)}) async-start(), calls=%async_computation.6 | async-start | bytes 1216512 | tf_op jit(solution)/shard_map/passages/all_gather | solution.py:275
  9.5 8.7 %collective-permute-start.2 = (bf16[128,512]{1,0:T(8,128)(2,1)}, bf16[128,512]{1,0:T(8,128)(2,1)S(1)}, u32[]{:S(2)}, u32[]{:S(2)}) collective-permute-start(bf16[128,512]{1,0:T(8,128)(2,1)} %rest_0_.3), channel_id=1, source_target_pairs={{0,6},{2,0},{4,2},{6,4},{1,7},{3,1},{5,3},{7,5},{8,14},{10,8},{12,... | collective-permute-start | bytes 393224 | tf_op jit(solution)/shard_map/tower/ppermute | solution.py:24
  11.8 7.1 %collective-permute-start.1 = (bf16[128,512]{1,0:T(8,128)(2,1)}, bf16[128,512]{1,0:T(8,128)(2,1)S(1)}, u32[]{:S(2)}, u32[]{:S(2)}) collective-permute-start(bf16[128,512]{1,0:T(8,128)(2,1)} %rest_0_.3), channel_id=1, source_target_pairs={{0,4},{2,6},{4,0},{6,2},{1,5},{3,7},{5,1},{7,3},{8,12},{10,14},{12... | collective-permute-start | bytes 393224 | tf_op jit(solution)/shard_map/tower/ppermute | solution.py:24
  12.7 7.0 %collective-permute-start = (bf16[128,512]{1,0:T(8,128)(2,1)}, bf16[128,512]{1,0:T(8,128)(2,1)S(1)}, u32[]{:S(2)}, u32[]{:S(2)}) collective-permute-start(bf16[128,512]{1,0:T(8,128)(2,1)} %rest_0_.3), channel_id=1, source_target_pairs={{0,2},{2,4},{4,6},{6,0},{1,3},{3,5},{5,7},{7,1},{8,10},{10,12},{12... | collective-permute-start | bytes 393224 | tf_op jit(solution)/shard_map/tower/ppermute | solution.py:24
  20.2 2.0 collective-permute-start.3
  23.8 6.8 %collective-permute-start.4 = (bf16[128,512]{1,0:T(8,128)(2,1)S(1)}, bf16[128,512]{1,0:T(8,128)(2,1)S(1)}, u32[]{:S(2)}, u32[]{:S(2)}) collective-permute-start(bf16[128,512]{1,0:T(8,128)(2,1)S(1)} %tower.14), channel_id=1, source_target_pairs={{0,64},{64,128},{128,192},{192,0},{1,65},{65,129},{129,193},{193,1... | collective-permute-start | bytes 393224 | tf_op jit(solution)/shard_map/tower/ppermute | solution.py:24
  30.6 7.7 %collective-permute-start.7 = (bf16[128,512]{1,0:T(8,128)(2,1)S(1)}, bf16[128,512]{1,0:T(8,128)(2,1)S(1)}, u32[]{:S(2)}, u32[]{:S(2)}) collective-permute-start(bf16[128,512]{1,0:T(8,128)(2,1)S(1)} %collective-permute-done.4.rest_0_), channel_id=1, source_target_pairs={{0,6},{2,0},{4,2},{6,4},{1,7},{3,1},{5,3},{7,5},{8,14},{10,8},{12,... | collective-permute-start | bytes 393224 | tf_op jit(solution)/shard_map/tower/ppermute | solution.py:24
  33.5 6.5 %collective-permute-start.6 = (bf16[128,512]{1,0:T(8,128)(2,1)S(1)}, bf16[128,512]{1,0:T(8,128)(2,1)S(1)}, u32[]{:S(2)}, u32[]{:S(2)}) collective-permute-start(bf16[128,512]{1,0:T(8,128)(2,1)S(1)} %collective-permute-done.4.rest_0_), channel_id=1, source_target_pairs={{0,4},{2,6},{4,0},{6,2},{1,5},{3,7},{5,1},{7,3},{8,12},{10,14},{12... | collective-permute-start | bytes 393224 | tf_op jit(solution)/shard_map/tower/ppermute | solution.py:24
  33.6 6.5 %collective-permute-start.5 = (bf16[128,512]{1,0:T(8,128)(2,1)S(1)}, bf16[128,512]{1,0:T(8,128)(2,1)S(1)}, u32[]{:S(2)}, u32[]{:S(2)}) collective-permute-start(bf16[128,512]{1,0:T(8,128)(2,1)S(1)} %collective-permute-done.4.rest_0_), channel_id=1, source_target_pairs={{0,2},{2,4},{4,6},{6,0},{1,3},{3,5},{5,7},{7,1},{8,10},{10,12},{12... | collective-permute-start | bytes 393224 | tf_op jit(solution)/shard_map/tower/ppermute | solution.py:24
  40.6 2.0 collective-permute-start.8
  44.2 6.8 %collective-permute-start.9 = (bf16[128,512]{1,0:T(8,128)(2,1)S(1)}, bf16[128,512]{1,0:T(8,128)(2,1)S(1)}, u32[]{:S(2)}, u32[]{:S(2)}) collective-permute-start(bf16[128,512]{1,0:T(8,128)(2,1)S(1)} %tower.17), channel_id=1, source_target_pairs={{0,64},{64,128},{128,192},{192,0},{1,65},{65,129},{129,193},{193,1... | collective-permute-start | bytes 393224 | tf_op jit(solution)/shard_map/tower/ppermute | solution.py:24
  51.0 9.3 %collective-permute-start.12 = (bf16[128,512]{1,0:T(8,128)(2,1)S(1)}, bf16[128,512]{1,0:T(8,128)(2,1)S(1)}, u32[]{:S(2)}, u32[]{:S(2)}) collective-permute-start(bf16[128,512]{1,0:T(8,128)(2,1)S(1)} %collective-permute-done.9.rest_0_), channel_id=1, source_target_pairs={{0,6},{2,0},{4,2},{6,4},{1,7},{3,1},{5,3},{7,5},{8,14},{10,8},{12,... | collective-permute-start | bytes 393224 | tf_op jit(solution)/shard_map/tower/ppermute | solution.py:24
  53.8 6.5 %collective-permute-start.11 = (bf16[128,512]{1,0:T(8,128)(2,1)S(1)}, bf16[128,512]{1,0:T(8,128)(2,1)S(1)}, u32[]{:S(2)}, u32[]{:S(2)}) collective-permute-start(bf16[128,512]{1,0:T(8,128)(2,1)S(1)} %collective-permute-done.9.rest_0_), channel_id=1, source_target_pairs={{0,4},{2,6},{4,0},{6,2},{1,5},{3,7},{5,1},{7,3},{8,12},{10,14},{12... | collective-permute-start | bytes 393224 | tf_op jit(solution)/shard_map/tower/ppermute | solution.py:24
  53.8 6.5 %collective-permute-start.10 = (bf16[128,512]{1,0:T(8,128)(2,1)S(1)}, bf16[128,512]{1,0:T(8,128)(2,1)S(1)}, u32[]{:S(2)}, u32[]{:S(2)}) collective-permute-start(bf16[128,512]{1,0:T(8,128)(2,1)S(1)} %collective-permute-done.9.rest_0_), channel_id=1, source_target_pairs={{0,2},{2,4},{4,6},{6,0},{1,3},{3,5},{5,7},{7,1},{8,10},{10,12},{12... | collective-permute-start | bytes 393224 | tf_op jit(solution)/shard_map/tower/ppermute | solution.py:24
  60.9 2.2 %collective-permute-start.13 = (bf16[4,128,512]{2,1,0:T(8,128)(2,1)S(1)}, bf16[4,128,512]{2,1,0:T(8,128)(2,1)S(1)}, u32[]{:S(2)}, u32[]{:S(2)}) collective-permute-start(bf16[4,128,512]{2,1,0:T(8,128)(2,1)S(1)} %tower.19.near), channel_id=1, source_target_pairs={{0,1},{1,0},{2,3},{3,2},{4,5},{5,4},{6,7},{7,6},{8,9},{9,8},{10,11... | collective-permute-start | bytes 1572872 | tf_op jit(solution)/shard_map/tower/ppermute | solution.py:24
  64.7 6.8 %collective-permute-start.14 = (bf16[128,512]{1,0:T(8,128)(2,1)S(1)}, bf16[128,512]{1,0:T(8,128)(2,1)S(1)}, u32[]{:S(2)}, u32[]{:S(2)}) collective-permute-start(bf16[128,512]{1,0:T(8,128)(2,1)S(1)} %tower.20), channel_id=1, source_target_pairs={{0,64},{64,128},{128,192},{192,0},{1,65},{65,129},{129,193},{193,1... | collective-permute-start | bytes 393224 | tf_op jit(solution)/shard_map/tower/ppermute | solution.py:24
  71.5 8.0 %collective-permute-start.17 = (bf16[128,512]{1,0:T(8,128)(2,1)S(1)}, bf16[128,512]{1,0:T(8,128)(2,1)S(1)}, u32[]{:S(2)}, u32[]{:S(2)}) collective-permute-start(bf16[128,512]{1,0:T(8,128)(2,1)S(1)} %collective-permute-done.14.rest_0_), channel_id=1, source_target_pairs={{0,6},{2,0},{4,2},{6,4},{1,7},{3,1},{5,3},{7,5},{8,14},{10,8},{12,... | collective-permute-start | bytes 393224 | tf_op jit(solution)/shard_map/tower/ppermute | solution.py:24
  74.7 6.5 %collective-permute-start.16 = (bf16[128,512]{1,0:T(8,128)(2,1)S(1)}, bf16[128,512]{1,0:T(8,128)(2,1)S(1)}, u32[]{:S(2)}, u32[]{:S(2)}) collective-permute-start(bf16[128,512]{1,0:T(8,128)(2,1)S(1)} %collective-permute-done.14.rest_0_), channel_id=1, source_target_pairs={{0,4},{2,6},{4,0},{6,2},{1,5},{3,7},{5,1},{7,3},{8,12},{10,14},{12... | collective-permute-start | bytes 393224 | tf_op jit(solution)/shard_map/tower/ppermute | solution.py:24
  74.8 6.5 %collective-permute-start.15 = (bf16[128,512]{1,0:T(8,128)(2,1)S(1)}, bf16[128,512]{1,0:T(8,128)(2,1)S(1)}, u32[]{:S(2)}, u32[]{:S(2)}) collective-permute-start(bf16[128,512]{1,0:T(8,128)(2,1)S(1)} %collective-permute-done.14.rest_0_), channel_id=1, source_target_pairs={{0,2},{2,4},{4,6},{6,0},{1,3},{3,5},{5,7},{7,1},{8,10},{10,12},{12... | collective-permute-start | bytes 393224 | tf_op jit(solution)/shard_map/tower/ppermute | solution.py:24
  81.8 2.0 collective-permute-start.18
  85.4 2.7 %collective-permute-start.21 = (bf16[128,512]{1,0:T(8,128)(2,1)S(1)}, bf16[128,512]{1,0:T(8,128)(2,1)S(1)}, u32[]{:S(2)}, u32[]{:S(2)}) collective-permute-start(bf16[128,512]{1,0:T(8,128)(2,1)S(1)} %tower.23), channel_id=1, source_target_pairs={{192,128},{193,129},{194,130},{195,131},{196,132},{197,133},{198,1... | collective-permute-start | bytes 393224 | tf_op jit(solution)/shard_map/to_sections/ppermute | solution.py:295
  86.7 8.6 %collective-permute-start.19 = (bf16[128,512]{1,0:T(8,128)(2,1)S(1)}, bf16[128,512]{1,0:T(8,128)(2,1)S(1)}, u32[]{:S(2)}, u32[]{:S(2)}) collective-permute-start(bf16[128,512]{1,0:T(8,128)(2,1)S(1)} %tower.23), channel_id=1, source_target_pairs={{192,0},{193,1},{194,2},{195,3},{196,4},{197,5},{198,6},{199,7},{2... | collective-permute-start | bytes 393224 | tf_op jit(solution)/shard_map/to_sections/ppermute | solution.py:295
  95.4 8.1 %collective-permute-start.24 = (bf16[128,512]{1,0:T(8,128)(2,1)S(1)}, bf16[128,512]{1,0:T(8,128)(2,1)S(1)}, u32[]{:S(2)}, u32[]{:S(2)}) collective-permute-start(bf16[128,512]{1,0:T(8,128)(2,1)S(1)} %add_add_fusion.rest_0_), channel_id=1, source_target_pairs={{0,6},{2,0},{4,2},{6,4},{1,7},{3,1},{5,3},{7,5},{8,14},{10,8},{12,... | collective-permute-start | bytes 393224 | tf_op jit(solution)/shard_map/head/ppermute | solution.py:24
  98.3 6.5 %collective-permute-start.23 = (bf16[128,512]{1,0:T(8,128)(2,1)S(1)}, bf16[128,512]{1,0:T(8,128)(2,1)S(1)}, u32[]{:S(2)}, u32[]{:S(2)}) collective-permute-start(bf16[128,512]{1,0:T(8,128)(2,1)S(1)} %add_add_fusion.rest_0_), channel_id=1, source_target_pairs={{0,4},{2,6},{4,0},{6,2},{1,5},{3,7},{5,1},{7,3},{8,12},{10,14},{12... | collective-permute-start | bytes 393224 | tf_op jit(solution)/shard_map/head/ppermute | solution.py:24
  98.3 6.5 %collective-permute-start.22 = (bf16[128,512]{1,0:T(8,128)(2,1)S(1)}, bf16[128,512]{1,0:T(8,128)(2,1)S(1)}, u32[]{:S(2)}, u32[]{:S(2)}) collective-permute-start(bf16[128,512]{1,0:T(8,128)(2,1)S(1)} %add_add_fusion.rest_0_), channel_id=1, source_target_pairs={{0,2},{2,4},{4,6},{6,0},{1,3},{3,5},{5,7},{7,1},{8,10},{10,12},{12... | collective-permute-start | bytes 393224 | tf_op jit(solution)/shard_map/head/ppermute | solution.py:24
  105.4 2.0 collective-permute-start.25
  109.5 20.6 %all-to-all-start = ((bf16[8,32,512]{2,1,0:T(8,128)(2,1)}), bf16[8,32,512]{2,1,0:T(8,128)(2,1)S(1)}, u32[]{:S(2)}, u32[]{:S(2)}) async-start(bf16[8,32,512]{2,1,0:T(8,128)(2,1)} %get-tuple-element.20), calls=%async_computation | async-start | bytes 524288 | tf_op jit(solution)/shard_map/normed_home/all_to_all | solution.py:310
  117.9 77.4 %reduce-scatter.2.cloned.1.call-start = ((), (), s32[]{:S(2)}) async-start(), calls=%async_computation.7 | async-start | bytes 1179648 | tf_op jit(solution)/shard_map/passage_grads/reduce_scatter | solution.py:334
  118.0 7.2 %collective-permute-start.28 = (bf16[128,512]{1,0:T(8,128)(2,1)S(1)}, bf16[128,512]{1,0:T(8,128)(2,1)S(1)}, u32[]{:S(2)}, u32[]{:S(2)}) collective-permute-start(bf16[128,512]{1,0:T(8,128)(2,1)S(1)} %get-tuple-element.19.rest_0_), channel_id=1, source_target_pairs={{0,6},{2,0},{4,2},{6,4},{1,7},{3,1},{5,3},{7,5},{8,14},{10,8},{12,... | collective-permute-start | bytes 393224 | tf_op jit(solution)/shard_map/score/ppermute | solution.py:24
  121.3 6.5 %collective-permute-start.27 = (bf16[128,512]{1,0:T(8,128)(2,1)S(1)}, bf16[128,512]{1,0:T(8,128)(2,1)S(1)}, u32[]{:S(2)}, u32[]{:S(2)}) collective-permute-start(bf16[128,512]{1,0:T(8,128)(2,1)S(1)} %get-tuple-element.19.rest_0_), channel_id=1, source_target_pairs={{0,4},{2,6},{4,0},{6,2},{1,5},{3,7},{5,1},{7,3},{8,12},{10,14},{12... | collective-permute-start | bytes 393224 | tf_op jit(solution)/shard_map/score/ppermute | solution.py:24
  121.3 6.6 %collective-permute-start.26 = (bf16[128,512]{1,0:T(8,128)(2,1)S(1)}, bf16[128,512]{1,0:T(8,128)(2,1)S(1)}, u32[]{:S(2)}, u32[]{:S(2)}) collective-permute-start(bf16[128,512]{1,0:T(8,128)(2,1)S(1)} %get-tuple-element.19.rest_0_), channel_id=1, source_target_pairs={{0,2},{2,4},{4,6},{6,0},{1,3},{3,5},{5,7},{7,1},{8,10},{10,12},{12... | collective-permute-start | bytes 393224 | tf_op jit(solution)/shard_map/score/ppermute | solution.py:24
  130.7 2.2 %collective-permute-start.29 = (bf16[4,128,512]{2,1,0:T(8,128)(2,1)S(1)}, bf16[4,128,512]{2,1,0:T(8,128)(2,1)S(1)}, u32[]{:S(2)}, u32[]{:S(2)}) collective-permute-start(bf16[4,128,512]{2,1,0:T(8,128)(2,1)S(1)} %score.2.near), channel_id=1, source_target_pairs={{0,1},{1,0},{2,3},{3,2},{4,5},{5,4},{6,7},{7,6},{8,9},{9,8},{10,11... | collective-permute-start | bytes 1572872 | tf_op jit(solution)/shard_map/score/ppermute | solution.py:24
  (11 other events, 228.9 us)
Sparse Core Ops, SparseCore 0:
  10.4 41.4 all-gather.1
  149.2 36.4 reduce-scatter.1

commit v3 on v2

--- a/solution.py
+++ b/solution.py
@@ -49,39 +49,37 @@
     return u * jax.nn.sigmoid(u)
 
 
-def row_scale(near, far):
-    square = 0.0
-    for ref in (near, far):
-        for k in range(ref.shape[0]):
-            wide = ref[k].astype(F32)
-            square = square + jnp.sum(wide * wide, axis=1, keepdims=True)
-    width = 2 * near.shape[0] * near.shape[2]
-    return lax.rsqrt(square / width + 1e-06)
-
-
-def owners(place, near, far):
-    count = near.shape[0]
-    y, core = place[2], place[3]
-    for k in range(count):
-        for ref, c in ((near, core), (far, 1 - core)):
-            yield ref, k, lax.rem(y - k + count, count) * 2 + c
+def owners(place, ref, same):
+    count = ref.shape[0]
+    core = place[3] if same else 1 - place[3]
+    return [lax.rem(place[2] - k + count, count) * 2 + core for k in range(count)]
 
 
 def at_block(owner, wide):
     return pl.ds(pl.multiple_of(owner * wide, wide), wide)
 
 
-def mixed_rows(place, near, far, weight, normed=None):
-    scale = row_scale(near, far)
-    wide = near.shape[2]
-    total = 0.0
-    for ref, k, owner in owners(place, near, far):
-        rows = (ref[k].astype(F32) * scale).astype(BF16)
-        at = at_block(owner, wide)
-        if normed is not None:
-            normed[:, at] = rows
-        total = total + jnp.dot(rows, weight[at, :], preferred_element_type=F32)
-    return total
+def mixed_part(place, ref, same, weight):
+    total = square = 0.0
+    for k, owner in enumerate(owners(place, ref, same)):
+        wide = ref[k].astype(F32)
+        square = square + jnp.sum(wide * wide, axis=1, keepdims=True)
+        rows = weight[at_block(owner, ref.shape[2]), :]
+        total = total + jnp.dot(ref[k], rows, preferred_element_type=F32)
+    return total, square
+
+
+def near_kernel(place, near, weight, part, squares):
+    total, square = mixed_part(place, near, True, weight)
+    part[...] = total
+    squares[...] = jnp.broadcast_to(square, squares.shape)
+
+
+def mixed_rows(place, near, far, weight, part, squares):
+    total, square = mixed_part(place, far, False, weight)
+    width = 2 * near.shape[0] * near.shape[2]
+    scale = lax.rsqrt((square + squares[:, :1]) / width + 1e-06)
+    return (part[...] + total) * scale, scale
 
 
 def load_kernel(place, source, *rest):
@@ -103,29 +101,44 @@
     return out
 
 
-def layer_kernel(place, near, far, weight, *rest):
-    out = rest[-1]
-    mixed = mixed_rows(place, near, far, weight)
+def started(place, near, weight):
+    rows, wide = near.shape[1:]
+    return call(near_kernel, [((rows, wide), F32), ((rows, 128), F32)], [place, near, weight])
+
+
+def layer_kernel(place, near, far, weight, part, squares, out):
+    mixed, _ = mixed_rows(place, near, far, weight, part, squares)
     out[...] = (near[0].astype(F32) + silu(mixed)).astype(BF16)
 
 
-def head_kernel(place, near, far, weight, emb, slope, pieces, normed):
-    head = mixed_rows(place, near, far, weight, normed)
+def head_kernel(place, near, far, weight, part, squares, emb, slope, pieces, normed):
+    head, scale = mixed_rows(place, near, far, weight, part, squares)
+    for ref, same in ((near, True), (far, False)):
+        for k, owner in enumerate(owners(place, ref, same)):
+            rows = (ref[k].astype(F32) * scale).astype(BF16)
+            normed[:, at_block(owner, ref.shape[2])] = rows
     sig = jax.nn.sigmoid(head)
     emb[...] = (near[0].astype(F32) + head * sig).astype(BF16)
     slope[...] = sig * (1.0 + head * (1.0 - sig))
     cycle, rows, taken = pieces.shape
+    taken -= 128
+    shape = (rows, 128)
+    row = lax.broadcasted_iota(jnp.int32, shape, 0)
+    cells = jnp.zeros(shape, jnp.int32)
+    for i in range(place.shape[0] - 4):
+        cells = jnp.where(row == i, place[4 + i], cells)
+    cells = cells.astype(F32).astype(BF16)
     sections = normed.shape[0] // rows
     piece = taken // sections
     own = pl.ds(pl.multiple_of(place[0] * rows, rows), rows)
     for k in range(cycle):
+        pieces[k, :, taken:] = cells
         for s in range(sections):
             at = (s * cycle + k) * piece
             pieces[k, :, s * piece : (s + 1) * piece] = normed[own, at : at + piece]
 
 
-def head_grad_kernel(place, parts, slope, *rest):
-    out = rest[-1]
+def head_grad_kernel(place, parts, slope, out):
     cycle, rows, wide = out.shape
     total = 0.0
     for k in range(parts.shape[0]):
@@ -140,7 +153,7 @@
     cycle, rows, wide = grads.shape
     taken = out.shape[1]
     part = lax.dot_general(
-        pieces[...].reshape(cycle * rows, pieces.shape[2]),
+        pieces[:, :, : pieces.shape[2] - 128].reshape(cycle * rows, pieces.shape[2] - 128),
         grads[...].reshape(cycle * rows, wide),
         (((0,), (0,)), ((), ())),
         preferred_element_type=F32,
@@ -164,31 +177,35 @@
     new_grads[...] = grads[...].astype(F32)
 
 
-def masks(place, passages, query_cells, positives, sizes):
+def masks(place, pieces, query_cells, positives, sizes):
     width, cycle, parts, block = sizes
-    rows, queries = passages.shape[0], positives.shape[1]
+    rows, queries = cycle * block, positives.shape[1]
     at = lax.broadcasted_iota(jnp.int32, (rows, queries), 0)
     owner, inner = at // block, at % block
     part = place[2] * 2 + place[3]
     index = ((place[0] * cycle + owner) * parts + part) * block + inner
     hit = index == positives[...]
-    cells = passages[:, width : width + queries].astype(F32)
+    first = pieces.shape[2] - 128
+    cells = pieces[:, :block, first : first + queries].astype(F32).reshape(rows, queries)
     allowed = jnp.logical_or(hit, cells == query_cells[...].astype(F32))
     return hit, allowed
 
 
-def score_kernel(sizes, place, near, far, passages, query_cells, positives, score, stats, full):
+def score_kernel(
+    sizes, place, near, far, passages, pieces, query_cells, positives, score, stats, full
+):
     wide = near.shape[2]
     total = 0.0
-    for ref, k, owner in owners(place, near, far):
-        at = pl.ds(pl.multiple_of(owner * wide, wide), wide)
-        full[:, at] = ref[k]
-        total = total + lax.dot_general(
-            passages[:, at], ref[k], (((1,), (1,)), ((), ())), preferred_element_type=F32
-        )
+    for ref, same in ((near, True), (far, False)):
+        for k, owner in enumerate(owners(place, ref, same)):
+            at = at_block(owner, wide)
+            full[:, at] = ref[k]
+            total = total + lax.dot_general(
+                passages[:, at], ref[k], (((1,), (1,)), ((), ())), preferred_element_type=F32
+            )
     total = total * sizes[0] ** -0.5
     score[...] = total
-    hit, allowed = masks(place, passages, query_cells, positives, sizes)
+    hit, allowed = masks(place, pieces, query_cells, positives, sizes)
     masked = jnp.where(allowed, total, FAR)
     top = jnp.max(masked, axis=0, keepdims=True)
     summed = jnp.sum(jnp.exp(masked - top), axis=0, keepdims=True)
@@ -199,7 +216,8 @@
 
 
 def grad_kernel(
-    sizes, place, stats, score, full, passages, query_cells, positives, loss, send, keep, grads
+    sizes, place, stats, score, full, passages, pieces, query_cells, positives,
+    loss, send, keep, grads,
 ):
     width = sizes[0]
     top, summed, positive = stats[:, 0, :], stats[:, 1, :], stats[:, 2, :]
@@ -207,7 +225,7 @@
     total = jnp.sum(summed * jnp.exp(top - upper), axis=0, keepdims=True)
     lse = upper + jnp.log(total)
     loss[...] = lse - jnp.sum(positive, axis=0, keepdims=True)
-    hit, allowed = masks(place, passages, query_cells, positives, sizes)
+    hit, allowed = masks(place, pieces, query_cells, positives, sizes)
     masked = jnp.where(allowed, score[...], FAR)
     prob = jnp.exp(masked - lse) - jnp.where(hit, 1.0, 0.0)
     turned_prob = prob.T.astype(BF16)
@@ -261,30 +279,28 @@
     cycle = lax.axis_size("dp")
     count = lax.axis_size("y")
     section_at = lax.axis_index("section")
-    place = jnp.stack(
-        [section_at, lax.axis_index("dp"), lax.axis_index("y"), lax.axis_index("core")]
-    ).astype(jnp.int32)
+    place = [section_at, lax.axis_index("dp"), lax.axis_index("y"), lax.axis_index("core")]
+    place = jnp.concatenate([jnp.stack(place).astype(jnp.int32), passage_cells])
     queries, wide = query_inputs.shape
     block, width = passages.shape
     sizes = (width, cycle, 2 * count, block)
     rows = queries // sections
     taken = width // cycle
     with jax.named_scope("passages"):
-        cells = jnp.broadcast_to(passage_cells.astype(BF16)[:, None], (block, queries))
-        own = jnp.concatenate([passages, cells], axis=1)
-        held = lax.all_gather(own, "dp", axis=0, tiled=True)
+        held = lax.all_gather(passages, "dp", axis=0, tiled=True)
     section_weights = pltpu.with_memory_space_constraint(section_weights, pltpu.HBM)
     head_weight = pltpu.with_memory_space_constraint(head_weight, pltpu.HBM)
+    arrived = pltpu.with_memory_space_constraint(held, pltpu.HBM)
     local = query_inputs
     for layer in range(sections):
         with jax.named_scope("tower"):
-            after = [local, held] if layer + 2 == sections else [local]
+            after = [local, arrived] if layer + 2 == sections else [local]
             layer_weight = loaded(place, section_weights, after)
             near, far = spread_after(local, place, [layer_weight])
             (local,) = call(
                 layer_kernel,
                 [((queries, wide), BF16)],
-                [place, near, far, layer_weight],
+                [place, near, far, layer_weight, *started(place, near, layer_weight)],
             )
             if layer + 1 < sections:
                 local = turned(local, "section", 1)
@@ -301,9 +317,9 @@
             [
                 ((queries, wide), BF16),
                 ((queries, wide), F32),
-                ((cycle, rows, taken), BF16),
+                ((cycle, rows, taken + 128), BF16),
             ],
-            [place, near, far, head_weight],
+            [place, near, far, head_weight, *started(place, near, head_weight)],
             scratch=[pltpu.VMEM((queries, width), BF16)],
         )
     with jax.named_scope("normed_home"):
@@ -319,7 +335,7 @@
                 ((group, 8, queries), F32),
                 ((queries, width), BF16),
             ],
-            [place, near, far, held, row_cells, row_positives],
+            [place, near, far, held, pieces, row_cells, row_positives],
         )
     with jax.named_scope("stats"):
         stats = lax.all_to_all(stats, ("section", "y", "core"), 0, 0)
@@ -328,7 +344,7 @@
         loss, send, keep, grads = call(
             functools.partial(grad_kernel, sizes),
             [((1, queries), F32), (part, BF16), (part, BF16), ((cycle, block, width), BF16)],
-            [place, stats, score, full, held, row_cells, row_positives],
+            [place, stats, score, full, held, pieces, row_cells, row_positives],
         )
     with jax.named_scope("passage_grads"):
         passage_grads = lax.psum_scatter(

time: 205 us -> 202 us (0.985)
  Pallas kernels: 32 us -> 35 us
  other arithmetic: 2.49 us -> 0.19 us
  waiting for transfers between devices: 51.8 us -> 49.6 us
    ppermute x28, waiting for transfers between devices: 42.2 us -> 38 us  [turned(): lax.ppermute(block, axis, [(i, (i + steps) % count) for i in range(count)])]
    pallas_call x21 -> x26, Pallas kernels: 32 us -> 35 us  [call(): pl.pallas_call(kernel, out_shape=[jax.ShapeDtypeStruct(shape, dtype) for...]
  transfers between devices with their start and end apart: 34 -> 34, of which waited for: 20 -> 20; matrix products, arithmetic and copies ran while one was open for 0% -> 0% of each run, Pallas kernels for 10% -> 12%
where the time goes in v3:
time: 202 us; the launch traced here: 201 us
  blocking collectives  54 us (27%)
  waiting for transfers between devices  49.6 us (25%)
  starting transfers between devices  45.1 us (22%)
  Pallas kernels  35 us (17%)
  between operations  14.4 us (7%)
  local copies, waits for them, and re-layouts  2.56 us (1%)
    ppermute x28, waiting for transfers between devices, turned(): lax.ppermute(block, axis, [(i, (i + steps) % count) for i in range(count)])  38 us
    pallas_call x26, Pallas kernels, call(): pl.pallas_call(kernel, out_shape=[jax.ShapeDtypeStruct(shape, dtype) for...  35 us
    ppermute x28, starting transfers between devices, turned(): lax.ppermute(block, axis, [(i, (i + steps) % count) for i in range(count)])  33.9 us
    all_to_all x1, blocking collectives, shards(): head_grad = lax.all_to_all(head_grad, 'dp', 0, 0)  16.1 us
    all_to_all x1, blocking collectives, shards(): lax.all_to_all(keep.reshape(sections * count, rows, wide), ('section', 'y...  15 us
    all_to_all x1, blocking collectives, shards(): stats = lax.all_to_all(stats, ('section', 'y', 'core'), 0, 0)  12.5 us
    all_to_all x1, blocking collectives, shards(): part = lax.all_to_all(part, 'section', 0, 0)  10.5 us
    all_to_all x1, starting transfers between devices, shards(): pieces = lax.all_to_all(pieces, 'dp', 0, 0)  8.47 us
  transfers between devices with their start and end apart: 34, of which 20 were waited for; matrix products, arithmetic and copies ran while one was open for 0% of the time, Pallas kernels for 12%

profile of v3, /device:TPU:8, one launch (start us, length us, event | category | flops | bytes accessed | tf_op | source)
XLA Modules:
  0.0 200.9 jit_solution(12954424788390503220)
XLA Ops:
  7.9 2.3 %collective-permute-start.2 = (bf16[128,512]{1,0:T(8,128)(2,1)}, bf16[128,512]{1,0:T(8,128)(2,1)S(1)}, u32[]{:S(2)}, u32[]{:S(2)}) collective-permute-start(bf16[128,512]{1,0:T(8,128)(2,1)} %rest_0_.3), channel_id=1, source_target_pairs={{0,6},{2,0},{4,2},{6,4},{1,7},{3,1},{5,3},{7,5},{8,14},{10,8},{12,... | collective-permute-start | bytes 393224 | tf_op jit(solution)/shard_map/tower/ppermute | solution.py:24
  11.0 1.9 collective-permute-start
  14.5 2.7 %tower.16.rest_4_.weight = bf16[4096,512]{1,0:T(8,128)(2,1)S(1)} custom-call(s32[20]{0:T(128)S(1)} %concatenate.3.place, bf16[4096,512]{1,0:T(8,128)(2,1)} %source.8, bf16[128,512]{1,0:T(8,128)(2,1)S(1)} %copy-done.1), custom_call_target="tpu_custom_call" | custom-call | flops 1024 | bytes 1024 | tf_op jit(solution)/shard_map/tower/pallas_call | solution.py:255
  23.2 5.3 %collective-permute-done.4.rest_0_ = bf16[128,512]{1,0:T(8,128)(2,1)S(1)} collective-permute-done((bf16[128,512]{1,0:T(8,128)(2,1)S(1)}, bf16[128,512]{1,0:T(8,128)(2,1)S(1)}, u32[]{:S(2)}, u32[]{:S(2)}) %collective-permute-start.4) | collective-permute-done | bytes 131104 | tf_op jit(solution)/shard_map/tower/ppermute | solution.py:24
  28.5 2.9 %collective-permute-start.7 = (bf16[128,512]{1,0:T(8,128)(2,1)S(1)}, bf16[128,512]{1,0:T(8,128)(2,1)S(1)}, u32[]{:S(2)}, u32[]{:S(2)}) collective-permute-start(bf16[128,512]{1,0:T(8,128)(2,1)S(1)} %collective-permute-done.4.rest_0_), channel_id=1, source_target_pairs={{0,6},{2,0},{4,2},{6,4},{1,7},{3,1},{5,3},{7,5},{8,14},{10,8},{12,... | collective-permute-start | bytes 393224 | tf_op jit(solution)/shard_map/tower/ppermute | solution.py:24
  31.4 2.0 %collective-permute-start.5 = (bf16[128,512]{1,0:T(8,128)(2,1)S(1)}, bf16[128,512]{1,0:T(8,128)(2,1)S(1)}, u32[]{:S(2)}, u32[]{:S(2)}) collective-permute-start(bf16[128,512]{1,0:T(8,128)(2,1)S(1)} %collective-permute-done.4.rest_0_), channel_id=1, source_target_pairs={{0,2},{2,4},{4,6},{6,0},{1,3},{3,5},{5,7},{7,1},{8,10},{10,12},{12... | collective-permute-start | bytes 393224 | tf_op jit(solution)/shard_map/tower/ppermute | solution.py:24
  33.4 2.7 %tower.20.rest_4_.weight = bf16[4096,512]{1,0:T(8,128)(2,1)S(1)} custom-call(s32[20]{0:T(128)S(1)} %concatenate.3.place, bf16[4096,512]{1,0:T(8,128)(2,1)} %source.8, bf16[128,512]{1,0:T(8,128)(2,1)S(1)} %collective-permute-done.4.rest_0_), custom_call_target="tpu_custom_call" | custom-call | flops 1024 | bytes 1024 | tf_op jit(solution)/shard_map/tower/pallas_call | solution.py:255
  41.9 6.4 %collective-permute-done.9.rest_0_ = bf16[128,512]{1,0:T(8,128)(2,1)S(1)} collective-permute-done((bf16[128,512]{1,0:T(8,128)(2,1)S(1)}, bf16[128,512]{1,0:T(8,128)(2,1)S(1)}, u32[]{:S(2)}, u32[]{:S(2)}) %collective-permute-start.9) | collective-permute-done | bytes 131104 | tf_op jit(solution)/shard_map/tower/ppermute | solution.py:24
  48.4 2.9 %collective-permute-start.12 = (bf16[128,512]{1,0:T(8,128)(2,1)S(1)}, bf16[128,512]{1,0:T(8,128)(2,1)S(1)}, u32[]{:S(2)}, u32[]{:S(2)}) collective-permute-start(bf16[128,512]{1,0:T(8,128)(2,1)S(1)} %collective-permute-done.9.rest_0_), channel_id=1, source_target_pairs={{0,6},{2,0},{4,2},{6,4},{1,7},{3,1},{5,3},{7,5},{8,14},{10,8},{12,... | collective-permute-start | bytes 393224 | tf_op jit(solution)/shard_map/tower/ppermute | solution.py:24
  51.2 2.4 %collective-permute-start.10 = (bf16[128,512]{1,0:T(8,128)(2,1)S(1)}, bf16[128,512]{1,0:T(8,128)(2,1)S(1)}, u32[]{:S(2)}, u32[]{:S(2)}) collective-permute-start(bf16[128,512]{1,0:T(8,128)(2,1)S(1)} %collective-permute-done.9.rest_0_), channel_id=1, source_target_pairs={{0,2},{2,4},{4,6},{6,0},{1,3},{3,5},{5,7},{7,1},{8,10},{10,12},{12... | collective-permute-start | bytes 393224 | tf_op jit(solution)/shard_map/tower/ppermute | solution.py:24
  53.6 2.7 %tower.24.rest_4_.weight = bf16[4096,512]{1,0:T(8,128)(2,1)S(1)} custom-call(s32[20]{0:T(128)S(1)} %concatenate.3.place, bf16[4096,512]{1,0:T(8,128)(2,1)} %source.8, bf16[128,512]{1,0:T(8,128)(2,1)S(1)} %collective-permute-done.9.rest_0_, bf16[128,4096]{1,0:T(8,128)(2,1)} %all-gather.2.cloned.1.call-done.rest_1_.passages), custom_call_target="tpu_custom_call" | custom-call | flops 1024 | bytes 1024 | tf_op jit(solution)/shard_map/tower/pallas_call | solution.py:255
  61.6 6.7 %collective-permute-done.14.rest_0_ = bf16[128,512]{1,0:T(8,128)(2,1)S(1)} collective-permute-done((bf16[128,512]{1,0:T(8,128)(2,1)S(1)}, bf16[128,512]{1,0:T(8,128)(2,1)S(1)}, u32[]{:S(2)}, u32[]{:S(2)}) %collective-permute-start.14) | collective-permute-done | bytes 131104 | tf_op jit(solution)/shard_map/tower/ppermute | solution.py:24
  68.4 3.2 %collective-permute-start.17 = (bf16[128,512]{1,0:T(8,128)(2,1)S(1)}, bf16[128,512]{1,0:T(8,128)(2,1)S(1)}, u32[]{:S(2)}, u32[]{:S(2)}) collective-permute-start(bf16[128,512]{1,0:T(8,128)(2,1)S(1)} %collective-permute-done.14.rest_0_), channel_id=1, source_target_pairs={{0,6},{2,0},{4,2},{6,4},{1,7},{3,1},{5,3},{7,5},{8,14},{10,8},{12,... | collective-permute-start | bytes 393224 | tf_op jit(solution)/shard_map/tower/ppermute | solution.py:24
  71.6 2.1 %collective-permute-start.15 = (bf16[128,512]{1,0:T(8,128)(2,1)S(1)}, bf16[128,512]{1,0:T(8,128)(2,1)S(1)}, u32[]{:S(2)}, u32[]{:S(2)}) collective-permute-start(bf16[128,512]{1,0:T(8,128)(2,1)S(1)} %collective-permute-done.14.rest_0_), channel_id=1, source_target_pairs={{0,2},{2,4},{4,6},{6,0},{1,3},{3,5},{5,7},{7,1},{8,10},{10,12},{12... | collective-permute-start | bytes 393224 | tf_op jit(solution)/shard_map/tower/ppermute | solution.py:24
  73.6 2.7 %tower.28.rest_4_.weight = bf16[4096,512]{1,0:T(8,128)(2,1)S(1)} custom-call(s32[20]{0:T(128)S(1)} %concatenate.3.place, bf16[4096,512]{1,0:T(8,128)(2,1)} %source.8, bf16[128,512]{1,0:T(8,128)(2,1)S(1)} %collective-permute-done.14.rest_0_), custom_call_target="tpu_custom_call" | custom-call | flops 1024 | bytes 1024 | tf_op jit(solution)/shard_map/tower/pallas_call | solution.py:255
  84.4 7.3 %collective-permute-done.19 = bf16[128,512]{1,0:T(8,128)(2,1)S(1)} collective-permute-done((bf16[128,512]{1,0:T(8,128)(2,1)S(1)}, bf16[128,512]{1,0:T(8,128)(2,1)S(1)}, u32[]{:S(2)}, u32[]{:S(2)}) %collective-permute-start.19) | collective-permute-done | bytes 131104 | tf_op jit(solution)/shard_map/to_sections/ppermute | solution.py:311
  91.7 2.9 %collective-permute-start.24 = (bf16[128,512]{1,0:T(8,128)(2,1)S(1)}, bf16[128,512]{1,0:T(8,128)(2,1)S(1)}, u32[]{:S(2)}, u32[]{:S(2)}) collective-permute-start(bf16[128,512]{1,0:T(8,128)(2,1)S(1)} %add_add_fusion.rest_0_), channel_id=1, source_target_pairs={{0,6},{2,0},{4,2},{6,4},{1,7},{3,1},{5,3},{7,5},{8,14},{10,8},{12,... | collective-permute-start | bytes 393224 | tf_op jit(solution)/shard_map/head/ppermute | solution.py:24
  94.7 2.4 %collective-permute-start.22 = (bf16[128,512]{1,0:T(8,128)(2,1)S(1)}, bf16[128,512]{1,0:T(8,128)(2,1)S(1)}, u32[]{:S(2)}, u32[]{:S(2)}) collective-permute-start(bf16[128,512]{1,0:T(8,128)(2,1)S(1)} %add_add_fusion.rest_0_), channel_id=1, source_target_pairs={{0,2},{2,4},{4,6},{6,0},{1,3},{3,5},{5,7},{7,1},{8,10},{10,12},{12... | collective-permute-start | bytes 393224 | tf_op jit(solution)/shard_map/head/ppermute | solution.py:24
  97.0 2.7 %head.4.rest_4_.weight = bf16[4096,512]{1,0:T(8,128)(2,1)S(1)} custom-call(s32[20]{0:T(128)S(1)} %concatenate.3.place, bf16[4096,512]{1,0:T(8,128)(2,1)} %source.9, bf16[128,512]{1,0:T(8,128)(2,1)S(1)} %add_add_fusion.rest_0_), custom_call_target="tpu_custom_call" | custom-call | flops 1024 | bytes 1024 | tf_op jit(solution)/shard_map/head/pallas_call | solution.py:255
  103.7 2.1 %head.7 = (bf16[128,512]{1,0:T(8,128)(2,1)S(1)}, f32[128,512]{1,0:T(8,128)S(1)}, bf16[8,32,640]{2,1,0:T(8,128)(2,1)}) custom-call(s32[20]{0:T(128)S(1)} %concatenate.3.place, bf16[4,128,512]{2,1,0:T(8,128)(2,1)S(1)} %head.5.near, bf16[4,128,512]{2,1,0:T(8,128)(2,1)S(1)} %collective-permute-done.25.far, bf16[4096,512]{1,0:T(8,128)(2,1)S(1)} %head.4.rest_4_.weight, ...), custom_call_target="tpu_custom_call" | custom-call | flops 1024 | bytes 1024 | tf_op jit(solution)/shard_map/head/pallas_call | solution.py:255
  105.8 8.5 %all-to-all-start = ((bf16[8,32,640]{2,1,0:T(8,128)(2,1)}), bf16[8,32,640]{2,1,0:T(8,128)(2,1)S(1)}, u32[]{:S(2)}, u32[]{:S(2)}) async-start(bf16[8,32,640]{2,1,0:T(8,128)(2,1)} %get-tuple-element.40), calls=%async_computation | async-start | bytes 655360 | tf_op jit(solution)/shard_map/normed_home/all_to_all | solution.py:326
  114.3 3.2 %collective-permute-start.28 = (bf16[128,512]{1,0:T(8,128)(2,1)S(1)}, bf16[128,512]{1,0:T(8,128)(2,1)S(1)}, u32[]{:S(2)}, u32[]{:S(2)}) collective-permute-start(bf16[128,512]{1,0:T(8,128)(2,1)S(1)} %get-tuple-element.39.rest_0_), channel_id=1, source_target_pairs={{0,6},{2,0},{4,2},{6,4},{1,7},{3,1},{5,3},{7,5},{8,14},{10,8},{12,... | collective-permute-start | bytes 393224 | tf_op jit(solution)/shard_map/score/ppermute | solution.py:24
  117.6 2.0 %collective-permute-start.26 = (bf16[128,512]{1,0:T(8,128)(2,1)S(1)}, bf16[128,512]{1,0:T(8,128)(2,1)S(1)}, u32[]{:S(2)}, u32[]{:S(2)}) collective-permute-start(bf16[128,512]{1,0:T(8,128)(2,1)S(1)} %get-tuple-element.39.rest_0_), channel_id=1, source_target_pairs={{0,2},{2,4},{4,6},{6,0},{1,3},{3,5},{5,7},{7,1},{8,10},{10,12},{12... | collective-permute-start | bytes 393224 | tf_op jit(solution)/shard_map/score/ppermute | solution.py:24
  119.6 1.9 collective-permute-done.28.rest_3_
  121.5 2.6 %collective-permute-done.27.rest_2_ = bf16[128,512]{1,0:T(8,128)(2,1)S(1)} collective-permute-done((bf16[128,512]{1,0:T(8,128)(2,1)S(1)}, bf16[128,512]{1,0:T(8,128)(2,1)S(1)}, u32[]{:S(2)}, u32[]{:S(2)}) %collective-permute-start.27) | collective-permute-done | bytes 131104 | tf_op jit(solution)/shard_map/score/ppermute | solution.py:24
  124.2 3.6 %all-to-all-done.rest_4_.pieces = bf16[8,32,640]{2,1,0:T(8,128)(2,1)S(1)} async-done(((bf16[8,32,640]{2,1,0:T(8,128)(2,1)}), bf16[8,32,640]{2,1,0:T(8,128)(2,1)S(1)}, u32[]{:S(2)}, u32[]{:S(2)}) %all-to-all-start) | async-done | bytes 327712 | tf_op jit(solution)/shard_map/normed_home/all_to_all | solution.py:326
  128.5 1.9 collective-permute-done.29.far
  131.5 12.5 %all_to_all.25.stats = f32[32,8,128]{2,1,0:T(8,128)S(1)} all-to-all(f32[32,8,128]{2,1,0:T(8,128)S(1)} %get-tuple-element.41), channel_id=1, replica_groups=mesh['section'=4,'dp'=8,'y'=4,'core'=2] {'section','y','core'}, dimensions={0} | all-to-all | bytes 262144 | tf_op jit(solution)/shard_map/stats/all_to_all | solution.py:341
  144.0 2.3 %grad.1 = (f32[1,128]{1,0:T(1,128)}, bf16[4,4,32,512]{3,2,1,0:T(8,128)(2,1)S(1)}, bf16[4,4,32,512]{3,2,1,0:T(8,128)(2,1)S(1)}, bf16[8,16,4096]{2,1,0:T(8,128)(2,1)}) custom-call(s32[20]{0:T(128)S(1)} %concatenate.3.place, f32[32,8,128]{2,1,0:T(8,128)S(1)} %all_to_all.25.stats, f32[128,128]{1,0:T(8,128)S(1)} %get-tuple-element.42.score, ...), custom_call_target="tpu_custom_call" | custom-call | flops 1024 | bytes 1024 | tf_op jit(solution)/shard_map/grad/pallas_call | solution.py:255
  148.5 15.0 %all_to_all.26.parts = bf16[16,32,512]{2,1,0:T(8,128)(2,1)S(1)} all-to-all(bf16[16,32,512]{2,1,0:T(8,128)(2,1)S(1)} %bitcast.13), channel_id=1, replica_groups=mesh['section'=4,'dp'=8,'y'=4,'core'=2] {'section','y'}, dimensions={0} | all-to-all | bytes 1048576 | tf_op jit(solution)/shard_map/query_grad/all_to_all | solution.py:355
  164.1 16.1 %all_to_all.27.grads = bf16[8,32,512]{2,1,0:T(8,128)(2,1)S(1)} all-to-all(bf16[8,32,512]{2,1,0:T(8,128)(2,1)S(1)} %query_grad.1), channel_id=1, replica_groups=mesh['section'=4,'dp'=8,'y'=4,'core'=2] {'dp'}, dimensions={0} | all-to-all | bytes 524288 | tf_op jit(solution)/shard_map/query_grad/all_to_all | solution.py:359
  181.0 10.5 %all_to_all.28.parts = bf16[4,128,512]{2,1,0:T(8,128)(2,1)S(1)} all-to-all(bf16[4,128,512]{2,1,0:T(8,128)(2,1)S(1)} %weight_grad.2), channel_id=1, replica_groups=mesh['section'=4,'dp'=8,'y'=4,'core'=2] {'section'}, dimensions={0} | all-to-all | bytes 1048576 | tf_op jit(solution)/shard_map/weight_grad/all_to_all | solution.py:366
  (87 shorter events, 40.1 us)
Async XLA Ops:
  7.2 46.4 %all-gather.2.cloned.1.call-start = ((), (), s32[]{:S(2)}) async-start(), calls=%async_computation.6 | async-start | bytes 1179648 | tf_op jit(solution)/shard_map/passages/all_gather | solution.py:290
  7.9 9.4 %collective-permute-start.2 = (bf16[128,512]{1,0:T(8,128)(2,1)}, bf16[128,512]{1,0:T(8,128)(2,1)S(1)}, u32[]{:S(2)}, u32[]{:S(2)}) collective-permute-start(bf16[128,512]{1,0:T(8,128)(2,1)} %rest_0_.3), channel_id=1, source_target_pairs={{0,6},{2,0},{4,2},{6,4},{1,7},{3,1},{5,3},{7,5},{8,14},{10,8},{12,... | collective-permute-start | bytes 393224 | tf_op jit(solution)/shard_map/tower/ppermute | solution.py:24
  10.2 7.1 %collective-permute-start.1 = (bf16[128,512]{1,0:T(8,128)(2,1)}, bf16[128,512]{1,0:T(8,128)(2,1)S(1)}, u32[]{:S(2)}, u32[]{:S(2)}) collective-permute-start(bf16[128,512]{1,0:T(8,128)(2,1)} %rest_0_.3), channel_id=1, source_target_pairs={{0,4},{2,6},{4,0},{6,2},{1,5},{3,7},{5,1},{7,3},{8,12},{10,14},{12... | collective-permute-start | bytes 393224 | tf_op jit(solution)/shard_map/tower/ppermute | solution.py:24
  11.0 7.0 %collective-permute-start = (bf16[128,512]{1,0:T(8,128)(2,1)}, bf16[128,512]{1,0:T(8,128)(2,1)S(1)}, u32[]{:S(2)}, u32[]{:S(2)}) collective-permute-start(bf16[128,512]{1,0:T(8,128)(2,1)} %rest_0_.3), channel_id=1, source_target_pairs={{0,2},{2,4},{4,6},{6,0},{1,3},{3,5},{5,7},{7,1},{8,10},{10,12},{12... | collective-permute-start | bytes 393224 | tf_op jit(solution)/shard_map/tower/ppermute | solution.py:24
  18.6 2.0 collective-permute-start.3
  21.7 6.8 %collective-permute-start.4 = (bf16[128,512]{1,0:T(8,128)(2,1)S(1)}, bf16[128,512]{1,0:T(8,128)(2,1)S(1)}, u32[]{:S(2)}, u32[]{:S(2)}) collective-permute-start(bf16[128,512]{1,0:T(8,128)(2,1)S(1)} %tower.19), channel_id=1, source_target_pairs={{0,64},{64,128},{128,192},{192,0},{1,65},{65,129},{129,193},{193,1... | collective-permute-start | bytes 393224 | tf_op jit(solution)/shard_map/tower/ppermute | solution.py:24
  28.5 7.7 %collective-permute-start.7 = (bf16[128,512]{1,0:T(8,128)(2,1)S(1)}, bf16[128,512]{1,0:T(8,128)(2,1)S(1)}, u32[]{:S(2)}, u32[]{:S(2)}) collective-permute-start(bf16[128,512]{1,0:T(8,128)(2,1)S(1)} %collective-permute-done.4.rest_0_), channel_id=1, source_target_pairs={{0,6},{2,0},{4,2},{6,4},{1,7},{3,1},{5,3},{7,5},{8,14},{10,8},{12,... | collective-permute-start | bytes 393224 | tf_op jit(solution)/shard_map/tower/ppermute | solution.py:24
  31.4 6.5 %collective-permute-start.6 = (bf16[128,512]{1,0:T(8,128)(2,1)S(1)}, bf16[128,512]{1,0:T(8,128)(2,1)S(1)}, u32[]{:S(2)}, u32[]{:S(2)}) collective-permute-start(bf16[128,512]{1,0:T(8,128)(2,1)S(1)} %collective-permute-done.4.rest_0_), channel_id=1, source_target_pairs={{0,4},{2,6},{4,0},{6,2},{1,5},{3,7},{5,1},{7,3},{8,12},{10,14},{12... | collective-permute-start | bytes 393224 | tf_op jit(solution)/shard_map/tower/ppermute | solution.py:24
  31.4 6.5 %collective-permute-start.5 = (bf16[128,512]{1,0:T(8,128)(2,1)S(1)}, bf16[128,512]{1,0:T(8,128)(2,1)S(1)}, u32[]{:S(2)}, u32[]{:S(2)}) collective-permute-start(bf16[128,512]{1,0:T(8,128)(2,1)S(1)} %collective-permute-done.4.rest_0_), channel_id=1, source_target_pairs={{0,2},{2,4},{4,6},{6,0},{1,3},{3,5},{5,7},{7,1},{8,10},{10,12},{12... | collective-permute-start | bytes 393224 | tf_op jit(solution)/shard_map/tower/ppermute | solution.py:24
  38.5 2.0 collective-permute-start.8
  41.5 6.8 %collective-permute-start.9 = (bf16[128,512]{1,0:T(8,128)(2,1)S(1)}, bf16[128,512]{1,0:T(8,128)(2,1)S(1)}, u32[]{:S(2)}, u32[]{:S(2)}) collective-permute-start(bf16[128,512]{1,0:T(8,128)(2,1)S(1)} %tower.23), channel_id=1, source_target_pairs={{0,64},{64,128},{128,192},{192,0},{1,65},{65,129},{129,193},{193,1... | collective-permute-start | bytes 393224 | tf_op jit(solution)/shard_map/tower/ppermute | solution.py:24
  48.4 8.0 %collective-permute-start.12 = (bf16[128,512]{1,0:T(8,128)(2,1)S(1)}, bf16[128,512]{1,0:T(8,128)(2,1)S(1)}, u32[]{:S(2)}, u32[]{:S(2)}) collective-permute-start(bf16[128,512]{1,0:T(8,128)(2,1)S(1)} %collective-permute-done.9.rest_0_), channel_id=1, source_target_pairs={{0,6},{2,0},{4,2},{6,4},{1,7},{3,1},{5,3},{7,5},{8,14},{10,8},{12,... | collective-permute-start | bytes 393224 | tf_op jit(solution)/shard_map/tower/ppermute | solution.py:24
  51.2 6.5 %collective-permute-start.11 = (bf16[128,512]{1,0:T(8,128)(2,1)S(1)}, bf16[128,512]{1,0:T(8,128)(2,1)S(1)}, u32[]{:S(2)}, u32[]{:S(2)}) collective-permute-start(bf16[128,512]{1,0:T(8,128)(2,1)S(1)} %collective-permute-done.9.rest_0_), channel_id=1, source_target_pairs={{0,4},{2,6},{4,0},{6,2},{1,5},{3,7},{5,1},{7,3},{8,12},{10,14},{12... | collective-permute-start | bytes 393224 | tf_op jit(solution)/shard_map/tower/ppermute | solution.py:24
  51.2 6.5 %collective-permute-start.10 = (bf16[128,512]{1,0:T(8,128)(2,1)S(1)}, bf16[128,512]{1,0:T(8,128)(2,1)S(1)}, u32[]{:S(2)}, u32[]{:S(2)}) collective-permute-start(bf16[128,512]{1,0:T(8,128)(2,1)S(1)} %collective-permute-done.9.rest_0_), channel_id=1, source_target_pairs={{0,2},{2,4},{4,6},{6,0},{1,3},{3,5},{5,7},{7,1},{8,10},{10,12},{12... | collective-permute-start | bytes 393224 | tf_op jit(solution)/shard_map/tower/ppermute | solution.py:24
  58.3 2.0 collective-permute-start.13
  61.3 7.0 %collective-permute-start.14 = (bf16[128,512]{1,0:T(8,128)(2,1)S(1)}, bf16[128,512]{1,0:T(8,128)(2,1)S(1)}, u32[]{:S(2)}, u32[]{:S(2)}) collective-permute-start(bf16[128,512]{1,0:T(8,128)(2,1)S(1)} %tower.27), channel_id=1, source_target_pairs={{0,64},{64,128},{128,192},{192,0},{1,65},{65,129},{129,193},{193,1... | collective-permute-start | bytes 393224 | tf_op jit(solution)/shard_map/tower/ppermute | solution.py:24
  68.4 8.0 %collective-permute-start.17 = (bf16[128,512]{1,0:T(8,128)(2,1)S(1)}, bf16[128,512]{1,0:T(8,128)(2,1)S(1)}, u32[]{:S(2)}, u32[]{:S(2)}) collective-permute-start(bf16[128,512]{1,0:T(8,128)(2,1)S(1)} %collective-permute-done.14.rest_0_), channel_id=1, source_target_pairs={{0,6},{2,0},{4,2},{6,4},{1,7},{3,1},{5,3},{7,5},{8,14},{10,8},{12,... | collective-permute-start | bytes 393224 | tf_op jit(solution)/shard_map/tower/ppermute | solution.py:24
  71.5 6.5 %collective-permute-start.16 = (bf16[128,512]{1,0:T(8,128)(2,1)S(1)}, bf16[128,512]{1,0:T(8,128)(2,1)S(1)}, u32[]{:S(2)}, u32[]{:S(2)}) collective-permute-start(bf16[128,512]{1,0:T(8,128)(2,1)S(1)} %collective-permute-done.14.rest_0_), channel_id=1, source_target_pairs={{0,4},{2,6},{4,0},{6,2},{1,5},{3,7},{5,1},{7,3},{8,12},{10,14},{12... | collective-permute-start | bytes 393224 | tf_op jit(solution)/shard_map/tower/ppermute | solution.py:24
  71.6 6.5 %collective-permute-start.15 = (bf16[128,512]{1,0:T(8,128)(2,1)S(1)}, bf16[128,512]{1,0:T(8,128)(2,1)S(1)}, u32[]{:S(2)}, u32[]{:S(2)}) collective-permute-start(bf16[128,512]{1,0:T(8,128)(2,1)S(1)} %collective-permute-done.14.rest_0_), channel_id=1, source_target_pairs={{0,2},{2,4},{4,6},{6,0},{1,3},{3,5},{5,7},{7,1},{8,10},{10,12},{12... | collective-permute-start | bytes 393224 | tf_op jit(solution)/shard_map/tower/ppermute | solution.py:24
  78.6 2.0 collective-permute-start.18
  81.7 2.7 %collective-permute-start.21 = (bf16[128,512]{1,0:T(8,128)(2,1)S(1)}, bf16[128,512]{1,0:T(8,128)(2,1)S(1)}, u32[]{:S(2)}, u32[]{:S(2)}) collective-permute-start(bf16[128,512]{1,0:T(8,128)(2,1)S(1)} %tower.31), channel_id=1, source_target_pairs={{192,128},{193,129},{194,130},{195,131},{196,132},{197,133},{198,1... | collective-permute-start | bytes 393224 | tf_op jit(solution)/shard_map/to_sections/ppermute | solution.py:311
  83.0 8.6 %collective-permute-start.19 = (bf16[128,512]{1,0:T(8,128)(2,1)S(1)}, bf16[128,512]{1,0:T(8,128)(2,1)S(1)}, u32[]{:S(2)}, u32[]{:S(2)}) collective-permute-start(bf16[128,512]{1,0:T(8,128)(2,1)S(1)} %tower.31), channel_id=1, source_target_pairs={{192,0},{193,1},{194,2},{195,3},{196,4},{197,5},{198,6},{199,7},{2... | collective-permute-start | bytes 393224 | tf_op jit(solution)/shard_map/to_sections/ppermute | solution.py:311
  91.7 8.1 %collective-permute-start.24 = (bf16[128,512]{1,0:T(8,128)(2,1)S(1)}, bf16[128,512]{1,0:T(8,128)(2,1)S(1)}, u32[]{:S(2)}, u32[]{:S(2)}) collective-permute-start(bf16[128,512]{1,0:T(8,128)(2,1)S(1)} %add_add_fusion.rest_0_), channel_id=1, source_target_pairs={{0,6},{2,0},{4,2},{6,4},{1,7},{3,1},{5,3},{7,5},{8,14},{10,8},{12,... | collective-permute-start | bytes 393224 | tf_op jit(solution)/shard_map/head/ppermute | solution.py:24
  94.7 6.5 %collective-permute-start.23 = (bf16[128,512]{1,0:T(8,128)(2,1)S(1)}, bf16[128,512]{1,0:T(8,128)(2,1)S(1)}, u32[]{:S(2)}, u32[]{:S(2)}) collective-permute-start(bf16[128,512]{1,0:T(8,128)(2,1)S(1)} %add_add_fusion.rest_0_), channel_id=1, source_target_pairs={{0,4},{2,6},{4,0},{6,2},{1,5},{3,7},{5,1},{7,3},{8,12},{10,14},{12... | collective-permute-start | bytes 393224 | tf_op jit(solution)/shard_map/head/ppermute | solution.py:24
  94.7 6.5 %collective-permute-start.22 = (bf16[128,512]{1,0:T(8,128)(2,1)S(1)}, bf16[128,512]{1,0:T(8,128)(2,1)S(1)}, u32[]{:S(2)}, u32[]{:S(2)}) collective-permute-start(bf16[128,512]{1,0:T(8,128)(2,1)S(1)} %add_add_fusion.rest_0_), channel_id=1, source_target_pairs={{0,2},{2,4},{4,6},{6,0},{1,3},{3,5},{5,7},{7,1},{8,10},{10,12},{12... | collective-permute-start | bytes 393224 | tf_op jit(solution)/shard_map/head/ppermute | solution.py:24
  101.7 2.0 collective-permute-start.25
  105.8 22.0 %all-to-all-start = ((bf16[8,32,640]{2,1,0:T(8,128)(2,1)}), bf16[8,32,640]{2,1,0:T(8,128)(2,1)S(1)}, u32[]{:S(2)}, u32[]{:S(2)}) async-start(bf16[8,32,640]{2,1,0:T(8,128)(2,1)} %get-tuple-element.40), calls=%async_computation | async-start | bytes 655360 | tf_op jit(solution)/shard_map/normed_home/all_to_all | solution.py:326
  114.3 77.2 %reduce-scatter.2.cloned.1.call-start = ((), (), s32[]{:S(2)}) async-start(), calls=%async_computation.7 | async-start | bytes 1179648 | tf_op jit(solution)/shard_map/passage_grads/reduce_scatter | solution.py:350
  114.3 7.1 %collective-permute-start.28 = (bf16[128,512]{1,0:T(8,128)(2,1)S(1)}, bf16[128,512]{1,0:T(8,128)(2,1)S(1)}, u32[]{:S(2)}, u32[]{:S(2)}) collective-permute-start(bf16[128,512]{1,0:T(8,128)(2,1)S(1)} %get-tuple-element.39.rest_0_), channel_id=1, source_target_pairs={{0,6},{2,0},{4,2},{6,4},{1,7},{3,1},{5,3},{7,5},{8,14},{10,8},{12,... | collective-permute-start | bytes 393224 | tf_op jit(solution)/shard_map/score/ppermute | solution.py:24
  117.6 6.5 %collective-permute-start.27 = (bf16[128,512]{1,0:T(8,128)(2,1)S(1)}, bf16[128,512]{1,0:T(8,128)(2,1)S(1)}, u32[]{:S(2)}, u32[]{:S(2)}) collective-permute-start(bf16[128,512]{1,0:T(8,128)(2,1)S(1)} %get-tuple-element.39.rest_0_), channel_id=1, source_target_pairs={{0,4},{2,6},{4,0},{6,2},{1,5},{3,7},{5,1},{7,3},{8,12},{10,14},{12... | collective-permute-start | bytes 393224 | tf_op jit(solution)/shard_map/score/ppermute | solution.py:24
  117.6 6.7 %collective-permute-start.26 = (bf16[128,512]{1,0:T(8,128)(2,1)S(1)}, bf16[128,512]{1,0:T(8,128)(2,1)S(1)}, u32[]{:S(2)}, u32[]{:S(2)}) collective-permute-start(bf16[128,512]{1,0:T(8,128)(2,1)S(1)} %get-tuple-element.39.rest_0_), channel_id=1, source_target_pairs={{0,2},{2,4},{4,6},{6,0},{1,3},{3,5},{5,7},{7,1},{8,10},{10,12},{12... | collective-permute-start | bytes 393224 | tf_op jit(solution)/shard_map/score/ppermute | solution.py:24
  128.4 2.0 collective-permute-start.29
  (10 other events, 223.9 us)
Sparse Core Ops, SparseCore 0:
  9.8 41.5 all-gather.1
  146.7 35.0 reduce-scatter.1

commit v4 on v3

--- a/solution.py
+++ b/solution.py
@@ -30,18 +30,13 @@
     return near, turned(near, "core", 1)
 
 
-def stack_kernel(place, *rest):
-    out = rest[-1]
-    for k in range(out.shape[0]):
-        out[k] = rest[k][...]
-
-
-def spread_after(block, place, loose):
+def spread_after(block, loose):
     if not loose:
         return spread(block)
     count = lax.axis_size("y")
     blocks = [block] + [turned(block, "y", k) for k in range(1, count)]
-    (near,) = call(stack_kernel, [((count,) + block.shape, block.dtype)], [place] + blocks, loose)
+    blocks, _ = lax.optimization_barrier((blocks, loose))
+    near = jnp.stack(blocks)
     return near, turned(near, "core", 1)
 
 
@@ -163,8 +158,11 @@
 
 
 def update_kernel(
-    place, parts, master, moment_one, moment_two, grads, new_master, new_one, new_two, new_grads
+    place, parts, master, moment_one, moment_two, grads,
+    new_master, new_one, new_two, new_grads, held, sem,
 ):
+    copy = pltpu.make_async_copy(grads, held, sem)
+    copy.start()
     grad = 0.0
     for k in range(parts.shape[0]):
         grad = grad + parts[k].astype(F32)
@@ -174,7 +172,8 @@
     new_master[...] = master[...] - 0.001 * (update + 0.1 * master[...])
     new_one[...] = one
     new_two[...] = two
-    new_grads[...] = grads[...].astype(F32)
+    copy.wait()
+    new_grads[...] = held[...].astype(F32)
 
 
 def masks(place, pieces, query_cells, positives, sizes):
@@ -296,7 +295,7 @@
         with jax.named_scope("tower"):
             after = [local, arrived] if layer + 2 == sections else [local]
             layer_weight = loaded(place, section_weights, after)
-            near, far = spread_after(local, place, [layer_weight])
+            near, far = spread_after(local, [layer_weight])
             (local,) = call(
                 layer_kernel,
                 [((queries, wide), BF16)],
@@ -311,7 +310,7 @@
             final = final + lax.ppermute(local, "section", [(last, other)])
     with jax.named_scope("head"):
         head_weight = loaded(place, head_weight, [final])
-        near, far = spread_after(final, place, [head_weight])
+        near, far = spread_after(final, [head_weight])
         query_cols, slope, pieces = call(
             head_kernel,
             [
@@ -325,7 +324,7 @@
     with jax.named_scope("normed_home"):
         pieces = lax.all_to_all(pieces, "dp", 0, 0)
     with jax.named_scope("score"):
-        near, far = spread_after(query_cols, place, [pieces])
+        near, far = spread_after(query_cols, [pieces])
         row_cells, row_positives = query_cells[None, :], positives[None, :]
         group = sections * count * 2
         score, stats, full = call(
@@ -368,7 +367,12 @@
         new_master, new_moment_one, new_moment_two, passage_grads = call(
             update_kernel,
             [tile, tile, tile, ((block, width), F32)],
-            [place, part, master, moment_one, moment_two, passage_grads],
+            [
+                place, part, master, moment_one, moment_two,
+                pltpu.with_memory_space_constraint(passage_grads, pltpu.HBM),
+            ],
+            scratch=[pltpu.VMEM((block, width), BF16), pltpu.SemaphoreType.DMA],
+            far_off=(5,),
         )
     return (loss[0], passage_grads, new_master, new_moment_one, new_moment_two)
 

time: 202 us -> 198 us (0.980)
  Pallas kernels: 35 us -> 32.4 us
    pallas_call x26 -> x20, Pallas kernels: 35 us -> 32.4 us  [call(): pl.pallas_call(kernel, out_shape=[jax.ShapeDtypeStruct(shape, dtype) for...]
  transfers between devices with their start and end apart: 34 -> 34, of which waited for: 20 -> 21; matrix products, arithmetic and copies ran while one was open for 0% -> 1% of each run, Pallas kernels for 12% -> 11%
where the time goes in v4:
time: 198 us; the launch traced here: 197 us
  blocking collectives  54 us (27%)
  waiting for transfers between devices  48 us (24%)
  starting transfers between devices  46 us (23%)
  Pallas kernels  32.4 us (16%)
  between operations  14.4 us (7%)
    ppermute x28, waiting for transfers between devices, turned(): lax.ppermute(block, axis, [(i, (i + steps) % count) for i in range(count)])  36.3 us
    ppermute x28, starting transfers between devices, turned(): lax.ppermute(block, axis, [(i, (i + steps) % count) for i in range(count)])  34.8 us
    pallas_call x20, Pallas kernels, call(): pl.pallas_call(kernel, out_shape=[jax.ShapeDtypeStruct(shape, dtype) for...  32.4 us
    all_to_all x1, blocking collectives, shards(): head_grad = lax.all_to_all(head_grad, 'dp', 0, 0)  16 us
    all_to_all x1, blocking collectives, shards(): lax.all_to_all(keep.reshape(sections * count, rows, wide), ('section', 'y...  14.9 us
    all_to_all x1, blocking collectives, shards(): stats = lax.all_to_all(stats, ('section', 'y', 'core'), 0, 0)  12.5 us
    all_to_all x1, blocking collectives, shards(): part = lax.all_to_all(part, 'section', 0, 0)  10.5 us
    all_to_all x1, starting transfers between devices, shards(): pieces = lax.all_to_all(pieces, 'dp', 0, 0)  8.45 us
  transfers between devices with their start and end apart: 34, of which 21 were waited for; matrix products, arithmetic and copies ran while one was open for 1% of the time, Pallas kernels for 11%

profile of v4, /device:TPU:8, one launch (start us, length us, event | category | flops | bytes accessed | tf_op | source)
XLA Modules:
  0.0 197.1 jit_solution(7327233974183893537)
XLA Ops:
  7.2 2.3 %collective-permute-start.2 = (bf16[128,512]{1,0:T(8,128)(2,1)}, bf16[128,512]{1,0:T(8,128)(2,1)S(1)}, u32[]{:S(2)}, u32[]{:S(2)}) collective-permute-start(bf16[128,512]{1,0:T(8,128)(2,1)} %rest_0_.1), channel_id=1, source_target_pairs={{0,6},{2,0},{4,2},{6,4},{1,7},{3,1},{5,3},{7,5},{8,14},{10,8},{12,... | collective-permute-start | bytes 393224 | tf_op jit(solution)/shard_map/tower/ppermute | solution.py:24
  10.3 1.9 collective-permute-start
  13.9 2.7 %tower.12.weight = bf16[4096,512]{1,0:T(8,128)(2,1)S(1)} custom-call(s32[20]{0:T(128)S(1)} %concatenate.3.place, bf16[4096,512]{1,0:T(8,128)(2,1)} %source.8, bf16[128,512]{1,0:T(8,128)(2,1)S(1)} %copy-done.1), custom_call_target="tpu_custom_call" | custom-call | flops 1024 | bytes 1024 | tf_op jit(solution)/shard_map/tower/pallas_call | solution.py:254
  22.1 5.3 %collective-permute-done.4.rest_0_ = bf16[128,512]{1,0:T(8,128)(2,1)S(1)} collective-permute-done((bf16[128,512]{1,0:T(8,128)(2,1)S(1)}, bf16[128,512]{1,0:T(8,128)(2,1)S(1)}, u32[]{:S(2)}, u32[]{:S(2)}) %collective-permute-start.4) | collective-permute-done | bytes 131104 | tf_op jit(solution)/shard_map/tower/ppermute | solution.py:24
  27.3 2.9 %collective-permute-start.7 = (bf16[128,512]{1,0:T(8,128)(2,1)S(1)}, bf16[128,512]{1,0:T(8,128)(2,1)S(1)}, u32[]{:S(2)}, u32[]{:S(2)}) collective-permute-start(bf16[128,512]{1,0:T(8,128)(2,1)S(1)} %collective-permute-done.4.rest_0_), channel_id=1, source_target_pairs={{0,6},{2,0},{4,2},{6,4},{1,7},{3,1},{5,3},{7,5},{8,14},{10,8},{12,... | collective-permute-start | bytes 393224 | tf_op jit(solution)/shard_map/tower/ppermute | solution.py:24
  30.2 2.0 %collective-permute-start.5 = (bf16[128,512]{1,0:T(8,128)(2,1)S(1)}, bf16[128,512]{1,0:T(8,128)(2,1)S(1)}, u32[]{:S(2)}, u32[]{:S(2)}) collective-permute-start(bf16[128,512]{1,0:T(8,128)(2,1)S(1)} %collective-permute-done.4.rest_0_), channel_id=1, source_target_pairs={{0,2},{2,4},{4,6},{6,0},{1,3},{3,5},{5,7},{7,1},{8,10},{10,12},{12... | collective-permute-start | bytes 393224 | tf_op jit(solution)/shard_map/tower/ppermute | solution.py:24
  32.2 2.8 %tower.15.weight = bf16[4096,512]{1,0:T(8,128)(2,1)S(1)} custom-call(s32[20]{0:T(128)S(1)} %concatenate.3.place, bf16[4096,512]{1,0:T(8,128)(2,1)} %source.8, bf16[128,512]{1,0:T(8,128)(2,1)S(1)} %collective-permute-done.4.rest_0_), custom_call_target="tpu_custom_call" | custom-call | flops 1024 | bytes 1024 | tf_op jit(solution)/shard_map/tower/pallas_call | solution.py:254
  40.2 6.5 %collective-permute-done.9.rest_0_ = bf16[128,512]{1,0:T(8,128)(2,1)S(1)} collective-permute-done((bf16[128,512]{1,0:T(8,128)(2,1)S(1)}, bf16[128,512]{1,0:T(8,128)(2,1)S(1)}, u32[]{:S(2)}, u32[]{:S(2)}) %collective-permute-start.9) | collective-permute-done | bytes 131104 | tf_op jit(solution)/shard_map/tower/ppermute | solution.py:24
  46.7 2.8 %collective-permute-start.12 = (bf16[128,512]{1,0:T(8,128)(2,1)S(1)}, bf16[128,512]{1,0:T(8,128)(2,1)S(1)}, u32[]{:S(2)}, u32[]{:S(2)}) collective-permute-start(bf16[128,512]{1,0:T(8,128)(2,1)S(1)} %collective-permute-done.9.rest_0_), channel_id=1, source_target_pairs={{0,6},{2,0},{4,2},{6,4},{1,7},{3,1},{5,3},{7,5},{8,14},{10,8},{12,... | collective-permute-start | bytes 393224 | tf_op jit(solution)/shard_map/tower/ppermute | solution.py:24
  49.5 2.4 %collective-permute-start.10 = (bf16[128,512]{1,0:T(8,128)(2,1)S(1)}, bf16[128,512]{1,0:T(8,128)(2,1)S(1)}, u32[]{:S(2)}, u32[]{:S(2)}) collective-permute-start(bf16[128,512]{1,0:T(8,128)(2,1)S(1)} %collective-permute-done.9.rest_0_), channel_id=1, source_target_pairs={{0,2},{2,4},{4,6},{6,0},{1,3},{3,5},{5,7},{7,1},{8,10},{10,12},{12... | collective-permute-start | bytes 393224 | tf_op jit(solution)/shard_map/tower/ppermute | solution.py:24
  52.6 2.7 %tower.18.weight = bf16[4096,512]{1,0:T(8,128)(2,1)S(1)} custom-call(s32[20]{0:T(128)S(1)} %concatenate.3.place, bf16[4096,512]{1,0:T(8,128)(2,1)} %source.8, bf16[128,512]{1,0:T(8,128)(2,1)S(1)} %collective-permute-done.9.rest_0_, bf16[128,4096]{1,0:T(8,128)(2,1)} %all-gather.2.cloned.1.call-done.rest_1_.passages), custom_call_target="tpu_custom_call" | custom-call | flops 1024 | bytes 1024 | tf_op jit(solution)/shard_map/tower/pallas_call | solution.py:254
  60.2 5.9 %collective-permute-done.14.rest_0_ = bf16[128,512]{1,0:T(8,128)(2,1)S(1)} collective-permute-done((bf16[128,512]{1,0:T(8,128)(2,1)S(1)}, bf16[128,512]{1,0:T(8,128)(2,1)S(1)}, u32[]{:S(2)}, u32[]{:S(2)}) %collective-permute-start.14) | collective-permute-done | bytes 131104 | tf_op jit(solution)/shard_map/tower/ppermute | solution.py:24
  66.1 3.2 %collective-permute-start.17 = (bf16[128,512]{1,0:T(8,128)(2,1)S(1)}, bf16[128,512]{1,0:T(8,128)(2,1)S(1)}, u32[]{:S(2)}, u32[]{:S(2)}) collective-permute-start(bf16[128,512]{1,0:T(8,128)(2,1)S(1)} %collective-permute-done.14.rest_0_), channel_id=1, source_target_pairs={{0,6},{2,0},{4,2},{6,4},{1,7},{3,1},{5,3},{7,5},{8,14},{10,8},{12,... | collective-permute-start | bytes 393224 | tf_op jit(solution)/shard_map/tower/ppermute | solution.py:24
  69.4 2.1 %collective-permute-start.15 = (bf16[128,512]{1,0:T(8,128)(2,1)S(1)}, bf16[128,512]{1,0:T(8,128)(2,1)S(1)}, u32[]{:S(2)}, u32[]{:S(2)}) collective-permute-start(bf16[128,512]{1,0:T(8,128)(2,1)S(1)} %collective-permute-done.14.rest_0_), channel_id=1, source_target_pairs={{0,2},{2,4},{4,6},{6,0},{1,3},{3,5},{5,7},{7,1},{8,10},{10,12},{12... | collective-permute-start | bytes 393224 | tf_op jit(solution)/shard_map/tower/ppermute | solution.py:24
  71.5 2.7 %tower.21.weight = bf16[4096,512]{1,0:T(8,128)(2,1)S(1)} custom-call(s32[20]{0:T(128)S(1)} %concatenate.3.place, bf16[4096,512]{1,0:T(8,128)(2,1)} %source.8, bf16[128,512]{1,0:T(8,128)(2,1)S(1)} %collective-permute-done.14.rest_0_), custom_call_target="tpu_custom_call" | custom-call | flops 1024 | bytes 1024 | tf_op jit(solution)/shard_map/tower/pallas_call | solution.py:254
  81.7 7.3 %collective-permute-done.19 = bf16[128,512]{1,0:T(8,128)(2,1)S(1)} collective-permute-done((bf16[128,512]{1,0:T(8,128)(2,1)S(1)}, bf16[128,512]{1,0:T(8,128)(2,1)S(1)}, u32[]{:S(2)}, u32[]{:S(2)}) %collective-permute-start.19) | collective-permute-done | bytes 131104 | tf_op jit(solution)/shard_map/to_sections/ppermute | solution.py:310
  89.0 3.0 %collective-permute-start.24 = (bf16[128,512]{1,0:T(8,128)(2,1)S(1)}, bf16[128,512]{1,0:T(8,128)(2,1)S(1)}, u32[]{:S(2)}, u32[]{:S(2)}) collective-permute-start(bf16[128,512]{1,0:T(8,128)(2,1)S(1)} %add_add_fusion.rest_0_), channel_id=1, source_target_pairs={{0,6},{2,0},{4,2},{6,4},{1,7},{3,1},{5,3},{7,5},{8,14},{10,8},{12,... | collective-permute-start | bytes 393224 | tf_op jit(solution)/shard_map/head/ppermute | solution.py:24
  92.0 2.3 %collective-permute-start.22 = (bf16[128,512]{1,0:T(8,128)(2,1)S(1)}, bf16[128,512]{1,0:T(8,128)(2,1)S(1)}, u32[]{:S(2)}, u32[]{:S(2)}) collective-permute-start(bf16[128,512]{1,0:T(8,128)(2,1)S(1)} %add_add_fusion.rest_0_), channel_id=1, source_target_pairs={{0,2},{2,4},{4,6},{6,0},{1,3},{3,5},{5,7},{7,1},{8,10},{10,12},{12... | collective-permute-start | bytes 393224 | tf_op jit(solution)/shard_map/head/ppermute | solution.py:24
  94.3 2.7 %head.3.weight = bf16[4096,512]{1,0:T(8,128)(2,1)S(1)} custom-call(s32[20]{0:T(128)S(1)} %concatenate.3.place, bf16[4096,512]{1,0:T(8,128)(2,1)} %source.9, bf16[128,512]{1,0:T(8,128)(2,1)S(1)} %add_add_fusion.rest_0_), custom_call_target="tpu_custom_call" | custom-call | flops 1024 | bytes 1024 | tf_op jit(solution)/shard_map/head/pallas_call | solution.py:254
  100.5 2.1 %head.5 = (bf16[128,512]{1,0:T(8,128)(2,1)S(1)}, f32[128,512]{1,0:T(8,128)S(1)}, bf16[8,32,640]{2,1,0:T(8,128)(2,1)}) custom-call(s32[20]{0:T(128)S(1)} %concatenate.3.place, bf16[4,128,512]{2,1,0:T(8,128)(2,1)S(1)} %pad_maximum_fusion.4.near, bf16[4,128,512]{2,1,0:T(8,128)(2,1)S(1)} %collective-permute-done.25.far, bf16[4096,512]{1,0:T(8,128)(2,1)S(1)} %head.3.weight, ...), custom_call_target="tpu_custom_call" | custom-call | flops 1024 | bytes 1024 | tf_op jit(solution)/shard_map/head/pallas_call | solution.py:254
  102.6 8.5 %all-to-all-start = ((bf16[8,32,640]{2,1,0:T(8,128)(2,1)}), bf16[8,32,640]{2,1,0:T(8,128)(2,1)S(1)}, u32[]{:S(2)}, u32[]{:S(2)}) async-start(bf16[8,32,640]{2,1,0:T(8,128)(2,1)} %get-tuple-element.84), calls=%async_computation | async-start | bytes 655360 | tf_op jit(solution)/shard_map/normed_home/all_to_all | solution.py:325
  111.1 3.3 %collective-permute-start.28 = (bf16[128,512]{1,0:T(8,128)(2,1)S(1)}, bf16[128,512]{1,0:T(8,128)(2,1)S(1)}, u32[]{:S(2)}, u32[]{:S(2)}) collective-permute-start(bf16[128,512]{1,0:T(8,128)(2,1)S(1)} %get-tuple-element.85), channel_id=1, source_target_pairs={{0,6},{2,0},{4,2},{6,4},{1,7},{3,1},{5,3},{7,5},{8,14},{10,8},{12,... | collective-permute-start | bytes 393224 | tf_op jit(solution)/shard_map/score/ppermute | solution.py:24
  114.4 2.0 %collective-permute-start.26 = (bf16[128,512]{1,0:T(8,128)(2,1)S(1)}, bf16[128,512]{1,0:T(8,128)(2,1)S(1)}, u32[]{:S(2)}, u32[]{:S(2)}) collective-permute-start(bf16[128,512]{1,0:T(8,128)(2,1)S(1)} %get-tuple-element.85), channel_id=1, source_target_pairs={{0,2},{2,4},{4,6},{6,0},{1,3},{3,5},{5,7},{7,1},{8,10},{10,12},{12... | collective-permute-start | bytes 393224 | tf_op jit(solution)/shard_map/score/ppermute | solution.py:24
  118.3 2.6 %collective-permute-done.27 = bf16[128,512]{1,0:T(8,128)(2,1)S(1)} collective-permute-done((bf16[128,512]{1,0:T(8,128)(2,1)S(1)}, bf16[128,512]{1,0:T(8,128)(2,1)S(1)}, u32[]{:S(2)}, u32[]{:S(2)}) %collective-permute-start.27) | collective-permute-done | bytes 131104 | tf_op jit(solution)/shard_map/score/ppermute | solution.py:24
  121.1 3.6 %all-to-all-done.pieces = bf16[8,32,640]{2,1,0:T(8,128)(2,1)S(1)} async-done(((bf16[8,32,640]{2,1,0:T(8,128)(2,1)}), bf16[8,32,640]{2,1,0:T(8,128)(2,1)S(1)}, u32[]{:S(2)}, u32[]{:S(2)}) %all-to-all-start) | async-done | bytes 327712 | tf_op jit(solution)/shard_map/normed_home/all_to_all | solution.py:325
  124.8 1.9 collective-permute-done.29.far
  127.9 12.5 %all_to_all.25.stats = f32[32,8,128]{2,1,0:T(8,128)S(1)} all-to-all(f32[32,8,128]{2,1,0:T(8,128)S(1)} %get-tuple-element.89), channel_id=1, replica_groups=mesh['section'=4,'dp'=8,'y'=4,'core'=2] {'section','y','core'}, dimensions={0} | all-to-all | bytes 262144 | tf_op jit(solution)/shard_map/stats/all_to_all | solution.py:340
  140.4 2.3 %grad.1 = (f32[1,128]{1,0:T(1,128)}, bf16[4,4,32,512]{3,2,1,0:T(8,128)(2,1)S(1)}, bf16[4,4,32,512]{3,2,1,0:T(8,128)(2,1)S(1)}, bf16[8,16,4096]{2,1,0:T(8,128)(2,1)}) custom-call(s32[20]{0:T(128)S(1)} %concatenate.3.place, f32[32,8,128]{2,1,0:T(8,128)S(1)} %all_to_all.25.stats, f32[128,128]{1,0:T(8,128)S(1)} %get-tuple-element.90.score, ...), custom_call_target="tpu_custom_call" | custom-call | flops 1024 | bytes 1024 | tf_op jit(solution)/shard_map/grad/pallas_call | solution.py:254
  144.8 14.9 %all_to_all.26.parts = bf16[16,32,512]{2,1,0:T(8,128)(2,1)S(1)} all-to-all(bf16[16,32,512]{2,1,0:T(8,128)(2,1)S(1)} %bitcast.43), channel_id=1, replica_groups=mesh['section'=4,'dp'=8,'y'=4,'core'=2] {'section','y'}, dimensions={0} | all-to-all | bytes 1048576 | tf_op jit(solution)/shard_map/query_grad/all_to_all | solution.py:354
  160.4 16.0 %all_to_all.27.grads = bf16[8,32,512]{2,1,0:T(8,128)(2,1)S(1)} all-to-all(bf16[8,32,512]{2,1,0:T(8,128)(2,1)S(1)} %query_grad.1), channel_id=1, replica_groups=mesh['section'=4,'dp'=8,'y'=4,'core'=2] {'dp'}, dimensions={0} | all-to-all | bytes 524288 | tf_op jit(solution)/shard_map/query_grad/all_to_all | solution.py:358
  177.3 10.5 %all_to_all.28.parts = bf16[4,128,512]{2,1,0:T(8,128)(2,1)S(1)} all-to-all(bf16[4,128,512]{2,1,0:T(8,128)(2,1)S(1)} %weight_grad.2), channel_id=1, replica_groups=mesh['section'=4,'dp'=8,'y'=4,'core'=2] {'section'}, dimensions={0} | all-to-all | bytes 1048576 | tf_op jit(solution)/shard_map/weight_grad/all_to_all | solution.py:365
  187.8 2.4 %weight_grad.3 = (f32[128,512]{1,0:T(8,128)}, f32[128,512]{1,0:T(8,128)}, f32[128,512]{1,0:T(8,128)}, f32[16,4096]{1,0:T(8,128)}) custom-call(s32[20]{0:T(128)S(1)} %concatenate.3.place, bf16[4,128,512]{2,1,0:T(8,128)(2,1)S(1)} %all_to_all.28.parts, f32[128,512]{1,0:T(8,128)S(1)} %copy-done.3, f32[128,512]{1,0:T(8,128)S(1)} %copy-done.4, ...), custom_call_target="tpu_custom_call" | custom-call | flops 1024 | bytes 1024 | tf_op jit(solution)/shard_map/weight_grad/pallas_call | solution.py:254
  (87 shorter events, 36.4 us)
Async XLA Ops:
  7.2 45.4 %all-gather.2.cloned.1.call-start = ((), (), s32[]{:S(2)}) async-start(), calls=%async_computation.6 | async-start | bytes 1179648 | tf_op jit(solution)/shard_map/passages/all_gather | solution.py:289
  7.2 9.4 %collective-permute-start.2 = (bf16[128,512]{1,0:T(8,128)(2,1)}, bf16[128,512]{1,0:T(8,128)(2,1)S(1)}, u32[]{:S(2)}, u32[]{:S(2)}) collective-permute-start(bf16[128,512]{1,0:T(8,128)(2,1)} %rest_0_.1), channel_id=1, source_target_pairs={{0,6},{2,0},{4,2},{6,4},{1,7},{3,1},{5,3},{7,5},{8,14},{10,8},{12,... | collective-permute-start | bytes 393224 | tf_op jit(solution)/shard_map/tower/ppermute | solution.py:24
  9.5 7.2 %collective-permute-start.1 = (bf16[128,512]{1,0:T(8,128)(2,1)}, bf16[128,512]{1,0:T(8,128)(2,1)S(1)}, u32[]{:S(2)}, u32[]{:S(2)}) collective-permute-start(bf16[128,512]{1,0:T(8,128)(2,1)} %rest_0_.1), channel_id=1, source_target_pairs={{0,4},{2,6},{4,0},{6,2},{1,5},{3,7},{5,1},{7,3},{8,12},{10,14},{12... | collective-permute-start | bytes 393224 | tf_op jit(solution)/shard_map/tower/ppermute | solution.py:24
  10.3 7.0 %collective-permute-start = (bf16[128,512]{1,0:T(8,128)(2,1)}, bf16[128,512]{1,0:T(8,128)(2,1)S(1)}, u32[]{:S(2)}, u32[]{:S(2)}) collective-permute-start(bf16[128,512]{1,0:T(8,128)(2,1)} %rest_0_.1), channel_id=1, source_target_pairs={{0,2},{2,4},{4,6},{6,0},{1,3},{3,5},{5,7},{7,1},{8,10},{10,12},{12... | collective-permute-start | bytes 393224 | tf_op jit(solution)/shard_map/tower/ppermute | solution.py:24
  17.4 2.0 %collective-permute-start.3 = (bf16[4,128,512]{2,1,0:T(8,128)(2,1)S(1)}, bf16[4,128,512]{2,1,0:T(8,128)(2,1)S(1)}, u32[]{:S(2)}, u32[]{:S(2)}) collective-permute-start(bf16[4,128,512]{2,1,0:T(8,128)(2,1)S(1)} %pad_maximum_fusion.near), channel_id=1, source_target_pairs={{0,1},{1,0},{2,3},{3,2},{4,5},{5,4},{6,7},{7,6},{8,9},{9,8},{10,11... | collective-permute-start | bytes 1572872 | tf_op jit(solution)/shard_map/tower/ppermute | solution.py:24
  20.5 6.8 %collective-permute-start.4 = (bf16[128,512]{1,0:T(8,128)(2,1)S(1)}, bf16[128,512]{1,0:T(8,128)(2,1)S(1)}, u32[]{:S(2)}, u32[]{:S(2)}) collective-permute-start(bf16[128,512]{1,0:T(8,128)(2,1)S(1)} %tower.14), channel_id=1, source_target_pairs={{0,64},{64,128},{128,192},{192,0},{1,65},{65,129},{129,193},{193,1... | collective-permute-start | bytes 393224 | tf_op jit(solution)/shard_map/tower/ppermute | solution.py:24
  27.3 7.7 %collective-permute-start.7 = (bf16[128,512]{1,0:T(8,128)(2,1)S(1)}, bf16[128,512]{1,0:T(8,128)(2,1)S(1)}, u32[]{:S(2)}, u32[]{:S(2)}) collective-permute-start(bf16[128,512]{1,0:T(8,128)(2,1)S(1)} %collective-permute-done.4.rest_0_), channel_id=1, source_target_pairs={{0,6},{2,0},{4,2},{6,4},{1,7},{3,1},{5,3},{7,5},{8,14},{10,8},{12,... | collective-permute-start | bytes 393224 | tf_op jit(solution)/shard_map/tower/ppermute | solution.py:24
  30.2 6.5 %collective-permute-start.6 = (bf16[128,512]{1,0:T(8,128)(2,1)S(1)}, bf16[128,512]{1,0:T(8,128)(2,1)S(1)}, u32[]{:S(2)}, u32[]{:S(2)}) collective-permute-start(bf16[128,512]{1,0:T(8,128)(2,1)S(1)} %collective-permute-done.4.rest_0_), channel_id=1, source_target_pairs={{0,4},{2,6},{4,0},{6,2},{1,5},{3,7},{5,1},{7,3},{8,12},{10,14},{12... | collective-permute-start | bytes 393224 | tf_op jit(solution)/shard_map/tower/ppermute | solution.py:24
  30.2 6.5 %collective-permute-start.5 = (bf16[128,512]{1,0:T(8,128)(2,1)S(1)}, bf16[128,512]{1,0:T(8,128)(2,1)S(1)}, u32[]{:S(2)}, u32[]{:S(2)}) collective-permute-start(bf16[128,512]{1,0:T(8,128)(2,1)S(1)} %collective-permute-done.4.rest_0_), channel_id=1, source_target_pairs={{0,2},{2,4},{4,6},{6,0},{1,3},{3,5},{5,7},{7,1},{8,10},{10,12},{12... | collective-permute-start | bytes 393224 | tf_op jit(solution)/shard_map/tower/ppermute | solution.py:24
  36.8 2.0 %collective-permute-start.8 = (bf16[4,128,512]{2,1,0:T(8,128)(2,1)S(1)}, bf16[4,128,512]{2,1,0:T(8,128)(2,1)S(1)}, u32[]{:S(2)}, u32[]{:S(2)}) collective-permute-start(bf16[4,128,512]{2,1,0:T(8,128)(2,1)S(1)} %pad_maximum_fusion.1.near), channel_id=1, source_target_pairs={{0,1},{1,0},{2,3},{3,2},{4,5},{5,4},{6,7},{7,6},{8,9},{9,8},{10,11... | collective-permute-start | bytes 1572872 | tf_op jit(solution)/shard_map/tower/ppermute | solution.py:24
  39.8 6.8 %collective-permute-start.9 = (bf16[128,512]{1,0:T(8,128)(2,1)S(1)}, bf16[128,512]{1,0:T(8,128)(2,1)S(1)}, u32[]{:S(2)}, u32[]{:S(2)}) collective-permute-start(bf16[128,512]{1,0:T(8,128)(2,1)S(1)} %tower.17), channel_id=1, source_target_pairs={{0,64},{64,128},{128,192},{192,0},{1,65},{65,129},{129,193},{193,1... | collective-permute-start | bytes 393224 | tf_op jit(solution)/shard_map/tower/ppermute | solution.py:24
  46.7 8.7 %collective-permute-start.12 = (bf16[128,512]{1,0:T(8,128)(2,1)S(1)}, bf16[128,512]{1,0:T(8,128)(2,1)S(1)}, u32[]{:S(2)}, u32[]{:S(2)}) collective-permute-start(bf16[128,512]{1,0:T(8,128)(2,1)S(1)} %collective-permute-done.9.rest_0_), channel_id=1, source_target_pairs={{0,6},{2,0},{4,2},{6,4},{1,7},{3,1},{5,3},{7,5},{8,14},{10,8},{12,... | collective-permute-start | bytes 393224 | tf_op jit(solution)/shard_map/tower/ppermute | solution.py:24
  49.5 6.5 %collective-permute-start.11 = (bf16[128,512]{1,0:T(8,128)(2,1)S(1)}, bf16[128,512]{1,0:T(8,128)(2,1)S(1)}, u32[]{:S(2)}, u32[]{:S(2)}) collective-permute-start(bf16[128,512]{1,0:T(8,128)(2,1)S(1)} %collective-permute-done.9.rest_0_), channel_id=1, source_target_pairs={{0,4},{2,6},{4,0},{6,2},{1,5},{3,7},{5,1},{7,3},{8,12},{10,14},{12... | collective-permute-start | bytes 393224 | tf_op jit(solution)/shard_map/tower/ppermute | solution.py:24
  49.5 6.4 %collective-permute-start.10 = (bf16[128,512]{1,0:T(8,128)(2,1)S(1)}, bf16[128,512]{1,0:T(8,128)(2,1)S(1)}, u32[]{:S(2)}, u32[]{:S(2)}) collective-permute-start(bf16[128,512]{1,0:T(8,128)(2,1)S(1)} %collective-permute-done.9.rest_0_), channel_id=1, source_target_pairs={{0,2},{2,4},{4,6},{6,0},{1,3},{3,5},{5,7},{7,1},{8,10},{10,12},{12... | collective-permute-start | bytes 393224 | tf_op jit(solution)/shard_map/tower/ppermute | solution.py:24
  56.1 2.0 %collective-permute-start.13 = (bf16[4,128,512]{2,1,0:T(8,128)(2,1)S(1)}, bf16[4,128,512]{2,1,0:T(8,128)(2,1)S(1)}, u32[]{:S(2)}, u32[]{:S(2)}) collective-permute-start(bf16[4,128,512]{2,1,0:T(8,128)(2,1)S(1)} %pad_maximum_fusion.2.near), channel_id=1, source_target_pairs={{0,1},{1,0},{2,3},{3,2},{4,5},{5,4},{6,7},{7,6},{8,9},{9,8},{10,11... | collective-permute-start | bytes 1572872 | tf_op jit(solution)/shard_map/tower/ppermute | solution.py:24
  59.1 7.0 %collective-permute-start.14 = (bf16[128,512]{1,0:T(8,128)(2,1)S(1)}, bf16[128,512]{1,0:T(8,128)(2,1)S(1)}, u32[]{:S(2)}, u32[]{:S(2)}) collective-permute-start(bf16[128,512]{1,0:T(8,128)(2,1)S(1)} %tower.20), channel_id=1, source_target_pairs={{0,64},{64,128},{128,192},{192,0},{1,65},{65,129},{129,193},{193,1... | collective-permute-start | bytes 393224 | tf_op jit(solution)/shard_map/tower/ppermute | solution.py:24
  66.1 8.1 %collective-permute-start.17 = (bf16[128,512]{1,0:T(8,128)(2,1)S(1)}, bf16[128,512]{1,0:T(8,128)(2,1)S(1)}, u32[]{:S(2)}, u32[]{:S(2)}) collective-permute-start(bf16[128,512]{1,0:T(8,128)(2,1)S(1)} %collective-permute-done.14.rest_0_), channel_id=1, source_target_pairs={{0,6},{2,0},{4,2},{6,4},{1,7},{3,1},{5,3},{7,5},{8,14},{10,8},{12,... | collective-permute-start | bytes 393224 | tf_op jit(solution)/shard_map/tower/ppermute | solution.py:24
  69.3 6.5 %collective-permute-start.16 = (bf16[128,512]{1,0:T(8,128)(2,1)S(1)}, bf16[128,512]{1,0:T(8,128)(2,1)S(1)}, u32[]{:S(2)}, u32[]{:S(2)}) collective-permute-start(bf16[128,512]{1,0:T(8,128)(2,1)S(1)} %collective-permute-done.14.rest_0_), channel_id=1, source_target_pairs={{0,4},{2,6},{4,0},{6,2},{1,5},{3,7},{5,1},{7,3},{8,12},{10,14},{12... | collective-permute-start | bytes 393224 | tf_op jit(solution)/shard_map/tower/ppermute | solution.py:24
  69.4 6.5 %collective-permute-start.15 = (bf16[128,512]{1,0:T(8,128)(2,1)S(1)}, bf16[128,512]{1,0:T(8,128)(2,1)S(1)}, u32[]{:S(2)}, u32[]{:S(2)}) collective-permute-start(bf16[128,512]{1,0:T(8,128)(2,1)S(1)} %collective-permute-done.14.rest_0_), channel_id=1, source_target_pairs={{0,2},{2,4},{4,6},{6,0},{1,3},{3,5},{5,7},{7,1},{8,10},{10,12},{12... | collective-permute-start | bytes 393224 | tf_op jit(solution)/shard_map/tower/ppermute | solution.py:24
  75.9 2.0 %collective-permute-start.18 = (bf16[4,128,512]{2,1,0:T(8,128)(2,1)S(1)}, bf16[4,128,512]{2,1,0:T(8,128)(2,1)S(1)}, u32[]{:S(2)}, u32[]{:S(2)}) collective-permute-start(bf16[4,128,512]{2,1,0:T(8,128)(2,1)S(1)} %pad_maximum_fusion.3.near), channel_id=1, source_target_pairs={{0,1},{1,0},{2,3},{3,2},{4,5},{5,4},{6,7},{7,6},{8,9},{9,8},{10,11... | collective-permute-start | bytes 1572872 | tf_op jit(solution)/shard_map/tower/ppermute | solution.py:24
  79.0 2.7 %collective-permute-start.21 = (bf16[128,512]{1,0:T(8,128)(2,1)S(1)}, bf16[128,512]{1,0:T(8,128)(2,1)S(1)}, u32[]{:S(2)}, u32[]{:S(2)}) collective-permute-start(bf16[128,512]{1,0:T(8,128)(2,1)S(1)} %tower.23), channel_id=1, source_target_pairs={{192,128},{193,129},{194,130},{195,131},{196,132},{197,133},{198,1... | collective-permute-start | bytes 393224 | tf_op jit(solution)/shard_map/to_sections/ppermute | solution.py:310
  80.3 8.6 %collective-permute-start.19 = (bf16[128,512]{1,0:T(8,128)(2,1)S(1)}, bf16[128,512]{1,0:T(8,128)(2,1)S(1)}, u32[]{:S(2)}, u32[]{:S(2)}) collective-permute-start(bf16[128,512]{1,0:T(8,128)(2,1)S(1)} %tower.23), channel_id=1, source_target_pairs={{192,0},{193,1},{194,2},{195,3},{196,4},{197,5},{198,6},{199,7},{2... | collective-permute-start | bytes 393224 | tf_op jit(solution)/shard_map/to_sections/ppermute | solution.py:310
  89.0 8.0 %collective-permute-start.24 = (bf16[128,512]{1,0:T(8,128)(2,1)S(1)}, bf16[128,512]{1,0:T(8,128)(2,1)S(1)}, u32[]{:S(2)}, u32[]{:S(2)}) collective-permute-start(bf16[128,512]{1,0:T(8,128)(2,1)S(1)} %add_add_fusion.rest_0_), channel_id=1, source_target_pairs={{0,6},{2,0},{4,2},{6,4},{1,7},{3,1},{5,3},{7,5},{8,14},{10,8},{12,... | collective-permute-start | bytes 393224 | tf_op jit(solution)/shard_map/head/ppermute | solution.py:24
  92.0 6.5 %collective-permute-start.23 = (bf16[128,512]{1,0:T(8,128)(2,1)S(1)}, bf16[128,512]{1,0:T(8,128)(2,1)S(1)}, u32[]{:S(2)}, u32[]{:S(2)}) collective-permute-start(bf16[128,512]{1,0:T(8,128)(2,1)S(1)} %add_add_fusion.rest_0_), channel_id=1, source_target_pairs={{0,4},{2,6},{4,0},{6,2},{1,5},{3,7},{5,1},{7,3},{8,12},{10,14},{12... | collective-permute-start | bytes 393224 | tf_op jit(solution)/shard_map/head/ppermute | solution.py:24
  92.0 6.5 %collective-permute-start.22 = (bf16[128,512]{1,0:T(8,128)(2,1)S(1)}, bf16[128,512]{1,0:T(8,128)(2,1)S(1)}, u32[]{:S(2)}, u32[]{:S(2)}) collective-permute-start(bf16[128,512]{1,0:T(8,128)(2,1)S(1)} %add_add_fusion.rest_0_), channel_id=1, source_target_pairs={{0,2},{2,4},{4,6},{6,0},{1,3},{3,5},{5,7},{7,1},{8,10},{10,12},{12... | collective-permute-start | bytes 393224 | tf_op jit(solution)/shard_map/head/ppermute | solution.py:24
  98.5 2.0 %collective-permute-start.25 = (bf16[4,128,512]{2,1,0:T(8,128)(2,1)S(1)}, bf16[4,128,512]{2,1,0:T(8,128)(2,1)S(1)}, u32[]{:S(2)}, u32[]{:S(2)}) collective-permute-start(bf16[4,128,512]{2,1,0:T(8,128)(2,1)S(1)} %pad_maximum_fusion.4.near), channel_id=1, source_target_pairs={{0,1},{1,0},{2,3},{3,2},{4,5},{5,4},{6,7},{7,6},{8,9},{9,8},{10,11... | collective-permute-start | bytes 1572872 | tf_op jit(solution)/shard_map/head/ppermute | solution.py:24
  102.6 22.0 %all-to-all-start = ((bf16[8,32,640]{2,1,0:T(8,128)(2,1)}), bf16[8,32,640]{2,1,0:T(8,128)(2,1)S(1)}, u32[]{:S(2)}, u32[]{:S(2)}) async-start(bf16[8,32,640]{2,1,0:T(8,128)(2,1)} %get-tuple-element.84), calls=%async_computation | async-start | bytes 655360 | tf_op jit(solution)/shard_map/normed_home/all_to_all | solution.py:325
  111.1 76.7 %reduce-scatter.2.cloned.1.call-start = ((), (), s32[]{:S(2)}) async-start(), calls=%async_computation.7 | async-start | bytes 1179648 | tf_op jit(solution)/shard_map/passage_grads/reduce_scatter | solution.py:349
  111.1 7.2 %collective-permute-start.28 = (bf16[128,512]{1,0:T(8,128)(2,1)S(1)}, bf16[128,512]{1,0:T(8,128)(2,1)S(1)}, u32[]{:S(2)}, u32[]{:S(2)}) collective-permute-start(bf16[128,512]{1,0:T(8,128)(2,1)S(1)} %get-tuple-element.85), channel_id=1, source_target_pairs={{0,6},{2,0},{4,2},{6,4},{1,7},{3,1},{5,3},{7,5},{8,14},{10,8},{12,... | collective-permute-start | bytes 393224 | tf_op jit(solution)/shard_map/score/ppermute | solution.py:24
  114.4 6.5 %collective-permute-start.27 = (bf16[128,512]{1,0:T(8,128)(2,1)S(1)}, bf16[128,512]{1,0:T(8,128)(2,1)S(1)}, u32[]{:S(2)}, u32[]{:S(2)}) collective-permute-start(bf16[128,512]{1,0:T(8,128)(2,1)S(1)} %get-tuple-element.85), channel_id=1, source_target_pairs={{0,4},{2,6},{4,0},{6,2},{1,5},{3,7},{5,1},{7,3},{8,12},{10,14},{12... | collective-permute-start | bytes 393224 | tf_op jit(solution)/shard_map/score/ppermute | solution.py:24
  114.4 6.7 %collective-permute-start.26 = (bf16[128,512]{1,0:T(8,128)(2,1)S(1)}, bf16[128,512]{1,0:T(8,128)(2,1)S(1)}, u32[]{:S(2)}, u32[]{:S(2)}) collective-permute-start(bf16[128,512]{1,0:T(8,128)(2,1)S(1)} %get-tuple-element.85), channel_id=1, source_target_pairs={{0,2},{2,4},{4,6},{6,0},{1,3},{3,5},{5,7},{7,1},{8,10},{10,12},{12... | collective-permute-start | bytes 393224 | tf_op jit(solution)/shard_map/score/ppermute | solution.py:24
  124.7 2.0 %collective-permute-start.29 = (bf16[4,128,512]{2,1,0:T(8,128)(2,1)S(1)}, bf16[4,128,512]{2,1,0:T(8,128)(2,1)S(1)}, u32[]{:S(2)}, u32[]{:S(2)}) collective-permute-start(bf16[4,128,512]{2,1,0:T(8,128)(2,1)S(1)} %pad_maximum_fusion.5.near), channel_id=1, source_target_pairs={{0,1},{1,0},{2,3},{3,2},{4,5},{5,4},{6,7},{7,6},{8,9},{9,8},{10,11... | collective-permute-start | bytes 1572872 | tf_op jit(solution)/shard_map/score/ppermute | solution.py:24
  (10 other events, 224.7 us)
Sparse Core Ops, SparseCore 0:
  12.4 40.1 all-gather.1
  143.0 35.1 reduce-scatter.1

commit v5 on v4

--- a/solution.py
+++ b/solution.py
@@ -215,8 +215,8 @@
 
 
 def grad_kernel(
-    sizes, place, stats, score, full, passages, pieces, query_cells, positives,
-    loss, send, keep, grads,
+    sizes, place, stats, score, passages, pieces, query_cells, positives,
+    loss, send, prob_out, turned_out,
 ):
     width = sizes[0]
     top, summed, positive = stats[:, 0, :], stats[:, 1, :], stats[:, 2, :]
@@ -228,21 +228,28 @@
     masked = jnp.where(allowed, score[...], FAR)
     prob = jnp.exp(masked - lse) - jnp.where(hit, 1.0, 0.0)
     turned_prob = prob.T.astype(BF16)
-    prob = prob.astype(BF16)
-    factor = width**-0.5
-    sections, count, rows, wide = keep.shape
-    core = place[3]
+    prob_out[...] = prob.astype(BF16)
+    turned_out[...] = turned_prob
+    query_parts(turned_prob, passages, send, 1 - place[3], width)
+
+
+def query_parts(turned_prob, passages, out, core, width):
+    sections, count, rows, wide = out.shape
     for j in range(count):
-        for ref, c in ((keep, core), (send, 1 - core)):
-            at = pl.ds(pl.multiple_of((2 * j + c) * wide, wide), wide)
-            part = jnp.dot(turned_prob, passages[:, at], preferred_element_type=F32) * factor
-            part = part.astype(BF16)
-            for s in range(sections):
-                ref[s, j] = part[s * rows : (s + 1) * rows]
+        at = at_block(2 * j + core, wide)
+        part = jnp.dot(turned_prob, passages[:, at], preferred_element_type=F32) * width**-0.5
+        part = part.astype(BF16)
+        for s in range(sections):
+            out[s, j] = part[s * rows : (s + 1) * rows]
+
+
+def rest_kernel(sizes, place, prob, turned_prob, full, passages, keep, grads):
+    width, wide = sizes[0], keep.shape[3]
+    query_parts(turned_prob[...], passages, keep, place[3], width)
+    cycle, block = grads.shape[:2]
     for j in range(0, width, wide):
-        part = jnp.dot(prob, full[:, j : j + wide], preferred_element_type=F32) * factor
-        part = part.astype(BF16)
-        cycle, block = grads.shape[:2]
+        part = jnp.dot(prob[...], full[:, j : j + wide], preferred_element_type=F32)
+        part = (part * width**-0.5).astype(BF16)
         for d in range(cycle):
             grads[d, :, j : j + wide] = part[d * block : (d + 1) * block]
 
@@ -340,10 +347,16 @@
         stats = lax.all_to_all(stats, ("section", "y", "core"), 0, 0)
     with jax.named_scope("grad"):
         part = (sections, count, rows, wide)
-        loss, send, keep, grads = call(
+        square = ((cycle * block, queries), BF16)
+        loss, send, prob, turned_prob = call(
             functools.partial(grad_kernel, sizes),
-            [((1, queries), F32), (part, BF16), (part, BF16), ((cycle, block, width), BF16)],
-            [place, stats, score, full, held, pieces, row_cells, row_positives],
+            [((1, queries), F32), (part, BF16), square, (square[0][::-1], BF16)],
+            [place, stats, score, held, pieces, row_cells, row_positives],
+        )
+        keep, grads = call(
+            functools.partial(rest_kernel, sizes),
+            [(part, BF16), ((cycle, block, width), BF16)],
+            [place, prob, turned_prob, full, held],
         )
     with jax.named_scope("passage_grads"):
         passage_grads = lax.psum_scatter(

time: 198 us -> 199 us (level)
    pallas_call x20 -> x21, Pallas kernels: 32.4 us -> 33.6 us  [call(): pl.pallas_call(kernel, out_shape=[jax.ShapeDtypeStruct(shape, dtype) for...]
  transfers between devices with their start and end apart: 34 -> 34, of which waited for: 21 -> 20; matrix products, arithmetic and copies ran while one was open for 1% -> 1% of each run, Pallas kernels for 11% -> 12%
where the time goes in v5:
time: 199 us; the launch traced here: 197 us
  blocking collectives  53.1 us (27%)
  waiting for transfers between devices  46.2 us (23%)
  starting transfers between devices  46 us (23%)
  Pallas kernels  33.6 us (17%)
  between operations  14.4 us (7%)
    ppermute x28, starting transfers between devices, turned(): lax.ppermute(block, axis, [(i, (i + steps) % count) for i in range(count)])  34.8 us
    ppermute x28, waiting for transfers between devices, turned(): lax.ppermute(block, axis, [(i, (i + steps) % count) for i in range(count)])  34.6 us
    pallas_call x21, Pallas kernels, call(): pl.pallas_call(kernel, out_shape=[jax.ShapeDtypeStruct(shape, dtype) for...  33.6 us
    all_to_all x1, blocking collectives, shards(): lax.all_to_all(keep.reshape(sections * count, rows, wide), ('section', 'y...  15.2 us
    all_to_all x1, blocking collectives, shards(): head_grad = lax.all_to_all(head_grad, 'dp', 0, 0)  14.8 us
    all_to_all x1, blocking collectives, shards(): stats = lax.all_to_all(stats, ('section', 'y', 'core'), 0, 0)  12.5 us
    all_to_all x1, blocking collectives, shards(): part = lax.all_to_all(part, 'section', 0, 0)  10.6 us
    all_to_all x1, starting transfers between devices, shards(): pieces = lax.all_to_all(pieces, 'dp', 0, 0)  8.45 us
  transfers between devices with their start and end apart: 34, of which 20 were waited for; matrix products, arithmetic and copies ran while one was open for 1% of the time, Pallas kernels for 12%

profile of v5, /device:TPU:8, one launch (start us, length us, event | category | flops | bytes accessed | tf_op | source)
XLA Modules:
  0.0 196.7 jit_solution(6771060398201130628)
XLA Ops:
  7.2 2.3 %collective-permute-start.2 = (bf16[128,512]{1,0:T(8,128)(2,1)}, bf16[128,512]{1,0:T(8,128)(2,1)S(1)}, u32[]{:S(2)}, u32[]{:S(2)}) collective-permute-start(bf16[128,512]{1,0:T(8,128)(2,1)} %rest_0_.1), channel_id=1, source_target_pairs={{0,6},{2,0},{4,2},{6,4},{1,7},{3,1},{5,3},{7,5},{8,14},{10,8},{12,... | collective-permute-start | bytes 393224 | tf_op jit(solution)/shard_map/tower/ppermute | solution.py:24
  10.3 1.9 collective-permute-start
  13.9 2.7 %tower.12.weight = bf16[4096,512]{1,0:T(8,128)(2,1)S(1)} custom-call(s32[20]{0:T(128)S(1)} %concatenate.3.place, bf16[4096,512]{1,0:T(8,128)(2,1)} %source.8, bf16[128,512]{1,0:T(8,128)(2,1)S(1)} %copy-done.1), custom_call_target="tpu_custom_call" | custom-call | flops 1024 | bytes 1024 | tf_op jit(solution)/shard_map/tower/pallas_call | solution.py:261
  22.1 5.3 %collective-permute-done.4.rest_0_ = bf16[128,512]{1,0:T(8,128)(2,1)S(1)} collective-permute-done((bf16[128,512]{1,0:T(8,128)(2,1)S(1)}, bf16[128,512]{1,0:T(8,128)(2,1)S(1)}, u32[]{:S(2)}, u32[]{:S(2)}) %collective-permute-start.4) | collective-permute-done | bytes 131104 | tf_op jit(solution)/shard_map/tower/ppermute | solution.py:24
  27.3 2.9 %collective-permute-start.7 = (bf16[128,512]{1,0:T(8,128)(2,1)S(1)}, bf16[128,512]{1,0:T(8,128)(2,1)S(1)}, u32[]{:S(2)}, u32[]{:S(2)}) collective-permute-start(bf16[128,512]{1,0:T(8,128)(2,1)S(1)} %collective-permute-done.4.rest_0_), channel_id=1, source_target_pairs={{0,6},{2,0},{4,2},{6,4},{1,7},{3,1},{5,3},{7,5},{8,14},{10,8},{12,... | collective-permute-start | bytes 393224 | tf_op jit(solution)/shard_map/tower/ppermute | solution.py:24
  30.2 2.0 %collective-permute-start.5 = (bf16[128,512]{1,0:T(8,128)(2,1)S(1)}, bf16[128,512]{1,0:T(8,128)(2,1)S(1)}, u32[]{:S(2)}, u32[]{:S(2)}) collective-permute-start(bf16[128,512]{1,0:T(8,128)(2,1)S(1)} %collective-permute-done.4.rest_0_), channel_id=1, source_target_pairs={{0,2},{2,4},{4,6},{6,0},{1,3},{3,5},{5,7},{7,1},{8,10},{10,12},{12... | collective-permute-start | bytes 393224 | tf_op jit(solution)/shard_map/tower/ppermute | solution.py:24
  32.2 2.8 %tower.15.weight = bf16[4096,512]{1,0:T(8,128)(2,1)S(1)} custom-call(s32[20]{0:T(128)S(1)} %concatenate.3.place, bf16[4096,512]{1,0:T(8,128)(2,1)} %source.8, bf16[128,512]{1,0:T(8,128)(2,1)S(1)} %collective-permute-done.4.rest_0_), custom_call_target="tpu_custom_call" | custom-call | flops 1024 | bytes 1024 | tf_op jit(solution)/shard_map/tower/pallas_call | solution.py:261
  40.2 6.5 %collective-permute-done.9.rest_0_ = bf16[128,512]{1,0:T(8,128)(2,1)S(1)} collective-permute-done((bf16[128,512]{1,0:T(8,128)(2,1)S(1)}, bf16[128,512]{1,0:T(8,128)(2,1)S(1)}, u32[]{:S(2)}, u32[]{:S(2)}) %collective-permute-start.9) | collective-permute-done | bytes 131104 | tf_op jit(solution)/shard_map/tower/ppermute | solution.py:24
  46.7 2.8 %collective-permute-start.12 = (bf16[128,512]{1,0:T(8,128)(2,1)S(1)}, bf16[128,512]{1,0:T(8,128)(2,1)S(1)}, u32[]{:S(2)}, u32[]{:S(2)}) collective-permute-start(bf16[128,512]{1,0:T(8,128)(2,1)S(1)} %collective-permute-done.9.rest_0_), channel_id=1, source_target_pairs={{0,6},{2,0},{4,2},{6,4},{1,7},{3,1},{5,3},{7,5},{8,14},{10,8},{12,... | collective-permute-start | bytes 393224 | tf_op jit(solution)/shard_map/tower/ppermute | solution.py:24
  49.5 2.4 %collective-permute-start.10 = (bf16[128,512]{1,0:T(8,128)(2,1)S(1)}, bf16[128,512]{1,0:T(8,128)(2,1)S(1)}, u32[]{:S(2)}, u32[]{:S(2)}) collective-permute-start(bf16[128,512]{1,0:T(8,128)(2,1)S(1)} %collective-permute-done.9.rest_0_), channel_id=1, source_target_pairs={{0,2},{2,4},{4,6},{6,0},{1,3},{3,5},{5,7},{7,1},{8,10},{10,12},{12... | collective-permute-start | bytes 393224 | tf_op jit(solution)/shard_map/tower/ppermute | solution.py:24
  52.6 2.7 %tower.18.weight = bf16[4096,512]{1,0:T(8,128)(2,1)S(1)} custom-call(s32[20]{0:T(128)S(1)} %concatenate.3.place, bf16[4096,512]{1,0:T(8,128)(2,1)} %source.8, bf16[128,512]{1,0:T(8,128)(2,1)S(1)} %collective-permute-done.9.rest_0_, bf16[128,4096]{1,0:T(8,128)(2,1)} %all-gather.2.cloned.1.call-done.rest_1_.passages), custom_call_target="tpu_custom_call" | custom-call | flops 1024 | bytes 1024 | tf_op jit(solution)/shard_map/tower/pallas_call | solution.py:261
  60.2 5.9 %collective-permute-done.14.rest_0_ = bf16[128,512]{1,0:T(8,128)(2,1)S(1)} collective-permute-done((bf16[128,512]{1,0:T(8,128)(2,1)S(1)}, bf16[128,512]{1,0:T(8,128)(2,1)S(1)}, u32[]{:S(2)}, u32[]{:S(2)}) %collective-permute-start.14) | collective-permute-done | bytes 131104 | tf_op jit(solution)/shard_map/tower/ppermute | solution.py:24
  66.1 3.2 %collective-permute-start.17 = (bf16[128,512]{1,0:T(8,128)(2,1)S(1)}, bf16[128,512]{1,0:T(8,128)(2,1)S(1)}, u32[]{:S(2)}, u32[]{:S(2)}) collective-permute-start(bf16[128,512]{1,0:T(8,128)(2,1)S(1)} %collective-permute-done.14.rest_0_), channel_id=1, source_target_pairs={{0,6},{2,0},{4,2},{6,4},{1,7},{3,1},{5,3},{7,5},{8,14},{10,8},{12,... | collective-permute-start | bytes 393224 | tf_op jit(solution)/shard_map/tower/ppermute | solution.py:24
  69.4 2.1 %collective-permute-start.15 = (bf16[128,512]{1,0:T(8,128)(2,1)S(1)}, bf16[128,512]{1,0:T(8,128)(2,1)S(1)}, u32[]{:S(2)}, u32[]{:S(2)}) collective-permute-start(bf16[128,512]{1,0:T(8,128)(2,1)S(1)} %collective-permute-done.14.rest_0_), channel_id=1, source_target_pairs={{0,2},{2,4},{4,6},{6,0},{1,3},{3,5},{5,7},{7,1},{8,10},{10,12},{12... | collective-permute-start | bytes 393224 | tf_op jit(solution)/shard_map/tower/ppermute | solution.py:24
  71.5 2.7 %tower.21.weight = bf16[4096,512]{1,0:T(8,128)(2,1)S(1)} custom-call(s32[20]{0:T(128)S(1)} %concatenate.3.place, bf16[4096,512]{1,0:T(8,128)(2,1)} %source.8, bf16[128,512]{1,0:T(8,128)(2,1)S(1)} %collective-permute-done.14.rest_0_), custom_call_target="tpu_custom_call" | custom-call | flops 1024 | bytes 1024 | tf_op jit(solution)/shard_map/tower/pallas_call | solution.py:261
  81.7 7.3 %collective-permute-done.19 = bf16[128,512]{1,0:T(8,128)(2,1)S(1)} collective-permute-done((bf16[128,512]{1,0:T(8,128)(2,1)S(1)}, bf16[128,512]{1,0:T(8,128)(2,1)S(1)}, u32[]{:S(2)}, u32[]{:S(2)}) %collective-permute-start.19) | collective-permute-done | bytes 131104 | tf_op jit(solution)/shard_map/to_sections/ppermute | solution.py:317
  89.0 3.0 %collective-permute-start.24 = (bf16[128,512]{1,0:T(8,128)(2,1)S(1)}, bf16[128,512]{1,0:T(8,128)(2,1)S(1)}, u32[]{:S(2)}, u32[]{:S(2)}) collective-permute-start(bf16[128,512]{1,0:T(8,128)(2,1)S(1)} %add_add_fusion.rest_0_), channel_id=1, source_target_pairs={{0,6},{2,0},{4,2},{6,4},{1,7},{3,1},{5,3},{7,5},{8,14},{10,8},{12,... | collective-permute-start | bytes 393224 | tf_op jit(solution)/shard_map/head/ppermute | solution.py:24
  92.0 2.3 %collective-permute-start.22 = (bf16[128,512]{1,0:T(8,128)(2,1)S(1)}, bf16[128,512]{1,0:T(8,128)(2,1)S(1)}, u32[]{:S(2)}, u32[]{:S(2)}) collective-permute-start(bf16[128,512]{1,0:T(8,128)(2,1)S(1)} %add_add_fusion.rest_0_), channel_id=1, source_target_pairs={{0,2},{2,4},{4,6},{6,0},{1,3},{3,5},{5,7},{7,1},{8,10},{10,12},{12... | collective-permute-start | bytes 393224 | tf_op jit(solution)/shard_map/head/ppermute | solution.py:24
  94.3 2.7 %head.3.weight = bf16[4096,512]{1,0:T(8,128)(2,1)S(1)} custom-call(s32[20]{0:T(128)S(1)} %concatenate.3.place, bf16[4096,512]{1,0:T(8,128)(2,1)} %source.9, bf16[128,512]{1,0:T(8,128)(2,1)S(1)} %add_add_fusion.rest_0_), custom_call_target="tpu_custom_call" | custom-call | flops 1024 | bytes 1024 | tf_op jit(solution)/shard_map/head/pallas_call | solution.py:261
  100.5 2.1 %head.5 = (bf16[128,512]{1,0:T(8,128)(2,1)S(1)}, f32[128,512]{1,0:T(8,128)S(1)}, bf16[8,32,640]{2,1,0:T(8,128)(2,1)}) custom-call(s32[20]{0:T(128)S(1)} %concatenate.3.place, bf16[4,128,512]{2,1,0:T(8,128)(2,1)S(1)} %pad_maximum_fusion.4.near, bf16[4,128,512]{2,1,0:T(8,128)(2,1)S(1)} %collective-permute-done.25.far, bf16[4096,512]{1,0:T(8,128)(2,1)S(1)} %head.3.weight, ...), custom_call_target="tpu_custom_call" | custom-call | flops 1024 | bytes 1024 | tf_op jit(solution)/shard_map/head/pallas_call | solution.py:261
  102.6 8.5 %all-to-all-start = ((bf16[8,32,640]{2,1,0:T(8,128)(2,1)}), bf16[8,32,640]{2,1,0:T(8,128)(2,1)S(1)}, u32[]{:S(2)}, u32[]{:S(2)}) async-start(bf16[8,32,640]{2,1,0:T(8,128)(2,1)} %get-tuple-element.86), calls=%async_computation | async-start | bytes 655360 | tf_op jit(solution)/shard_map/normed_home/all_to_all | solution.py:332
  111.1 3.3 %collective-permute-start.28 = (bf16[128,512]{1,0:T(8,128)(2,1)S(1)}, bf16[128,512]{1,0:T(8,128)(2,1)S(1)}, u32[]{:S(2)}, u32[]{:S(2)}) collective-permute-start(bf16[128,512]{1,0:T(8,128)(2,1)S(1)} %get-tuple-element.87), channel_id=1, source_target_pairs={{0,6},{2,0},{4,2},{6,4},{1,7},{3,1},{5,3},{7,5},{8,14},{10,8},{12,... | collective-permute-start | bytes 393224 | tf_op jit(solution)/shard_map/score/ppermute | solution.py:24
  114.4 2.0 %collective-permute-start.26 = (bf16[128,512]{1,0:T(8,128)(2,1)S(1)}, bf16[128,512]{1,0:T(8,128)(2,1)S(1)}, u32[]{:S(2)}, u32[]{:S(2)}) collective-permute-start(bf16[128,512]{1,0:T(8,128)(2,1)S(1)} %get-tuple-element.87), channel_id=1, source_target_pairs={{0,2},{2,4},{4,6},{6,0},{1,3},{3,5},{5,7},{7,1},{8,10},{10,12},{12... | collective-permute-start | bytes 393224 | tf_op jit(solution)/shard_map/score/ppermute | solution.py:24
  118.3 2.6 %collective-permute-done.27 = bf16[128,512]{1,0:T(8,128)(2,1)S(1)} collective-permute-done((bf16[128,512]{1,0:T(8,128)(2,1)S(1)}, bf16[128,512]{1,0:T(8,128)(2,1)S(1)}, u32[]{:S(2)}, u32[]{:S(2)}) %collective-permute-start.27) | collective-permute-done | bytes 131104 | tf_op jit(solution)/shard_map/score/ppermute | solution.py:24
  121.1 3.6 %all-to-all-done.pieces = bf16[8,32,640]{2,1,0:T(8,128)(2,1)S(1)} async-done(((bf16[8,32,640]{2,1,0:T(8,128)(2,1)}), bf16[8,32,640]{2,1,0:T(8,128)(2,1)S(1)}, u32[]{:S(2)}, u32[]{:S(2)}) %all-to-all-start) | async-done | bytes 327712 | tf_op jit(solution)/shard_map/normed_home/all_to_all | solution.py:332
  124.9 1.9 collective-permute-done.29.far
  127.9 12.5 %all_to_all.25.stats = f32[32,8,128]{2,1,0:T(8,128)S(1)} all-to-all(f32[32,8,128]{2,1,0:T(8,128)S(1)} %get-tuple-element.91), channel_id=1, replica_groups=mesh['section'=4,'dp'=8,'y'=4,'core'=2] {'section','y','core'}, dimensions={0} | all-to-all | bytes 262144 | tf_op jit(solution)/shard_map/stats/all_to_all | solution.py:347
  141.9 2.1 %grad.3 = (bf16[4,4,32,512]{3,2,1,0:T(8,128)(2,1)S(1)}, bf16[8,16,4096]{2,1,0:T(8,128)(2,1)}) custom-call(s32[20]{0:T(128)S(1)} %concatenate.3.place, bf16[128,128]{1,0:T(8,128)(2,1)S(1)} %get-tuple-element.94.prob, bf16[128,128]{1,0:T(8,128)(2,1)S(1)} %get-tuple-element.95.turned_prob, bf16[128,4096]{1,0:T(8,128)(2,1)S(1)} %get-tuple-element.96.full, ...), custom_call_target="tpu_custom_call" | custom-call | flops 1024 | bytes 1024 | tf_op jit(solution)/shard_map/grad/pallas_call | solution.py:261
  145.3 15.2 %all_to_all.26.parts = bf16[16,32,512]{2,1,0:T(8,128)(2,1)S(1)} all-to-all(bf16[16,32,512]{2,1,0:T(8,128)(2,1)S(1)} %bitcast.43), channel_id=1, replica_groups=mesh['section'=4,'dp'=8,'y'=4,'core'=2] {'section','y'}, dimensions={0} | all-to-all | bytes 1048576 | tf_op jit(solution)/shard_map/query_grad/all_to_all | solution.py:367
  161.1 14.8 %all_to_all.27.grads = bf16[8,32,512]{2,1,0:T(8,128)(2,1)S(1)} all-to-all(bf16[8,32,512]{2,1,0:T(8,128)(2,1)S(1)} %query_grad.1), channel_id=1, replica_groups=mesh['section'=4,'dp'=8,'y'=4,'core'=2] {'dp'}, dimensions={0} | all-to-all | bytes 524288 | tf_op jit(solution)/shard_map/query_grad/all_to_all | solution.py:371
  176.8 10.6 %all_to_all.28.parts = bf16[4,128,512]{2,1,0:T(8,128)(2,1)S(1)} all-to-all(bf16[4,128,512]{2,1,0:T(8,128)(2,1)S(1)} %weight_grad.2), channel_id=1, replica_groups=mesh['section'=4,'dp'=8,'y'=4,'core'=2] {'section'}, dimensions={0} | all-to-all | bytes 1048576 | tf_op jit(solution)/shard_map/weight_grad/all_to_all | solution.py:378
  187.4 2.4 %weight_grad.3 = (f32[128,512]{1,0:T(8,128)}, f32[128,512]{1,0:T(8,128)}, f32[128,512]{1,0:T(8,128)}, f32[16,4096]{1,0:T(8,128)}) custom-call(s32[20]{0:T(128)S(1)} %concatenate.3.place, bf16[4,128,512]{2,1,0:T(8,128)(2,1)S(1)} %all_to_all.28.parts, f32[128,512]{1,0:T(8,128)S(1)} %copy-done.3, f32[128,512]{1,0:T(8,128)S(1)} %copy-done.4, ...), custom_call_target="tpu_custom_call" | custom-call | flops 1024 | bytes 1024 | tf_op jit(solution)/shard_map/weight_grad/pallas_call | solution.py:261
  (88 shorter events, 37.1 us)
Async XLA Ops:
  7.2 45.4 %all-gather.2.cloned.1.call-start = ((), (), s32[]{:S(2)}) async-start(), calls=%async_computation.6 | async-start | bytes 1179648 | tf_op jit(solution)/shard_map/passages/all_gather | solution.py:296
  7.2 9.4 %collective-permute-start.2 = (bf16[128,512]{1,0:T(8,128)(2,1)}, bf16[128,512]{1,0:T(8,128)(2,1)S(1)}, u32[]{:S(2)}, u32[]{:S(2)}) collective-permute-start(bf16[128,512]{1,0:T(8,128)(2,1)} %rest_0_.1), channel_id=1, source_target_pairs={{0,6},{2,0},{4,2},{6,4},{1,7},{3,1},{5,3},{7,5},{8,14},{10,8},{12,... | collective-permute-start | bytes 393224 | tf_op jit(solution)/shard_map/tower/ppermute | solution.py:24
  9.5 7.2 %collective-permute-start.1 = (bf16[128,512]{1,0:T(8,128)(2,1)}, bf16[128,512]{1,0:T(8,128)(2,1)S(1)}, u32[]{:S(2)}, u32[]{:S(2)}) collective-permute-start(bf16[128,512]{1,0:T(8,128)(2,1)} %rest_0_.1), channel_id=1, source_target_pairs={{0,4},{2,6},{4,0},{6,2},{1,5},{3,7},{5,1},{7,3},{8,12},{10,14},{12... | collective-permute-start | bytes 393224 | tf_op jit(solution)/shard_map/tower/ppermute | solution.py:24
  10.3 7.0 %collective-permute-start = (bf16[128,512]{1,0:T(8,128)(2,1)}, bf16[128,512]{1,0:T(8,128)(2,1)S(1)}, u32[]{:S(2)}, u32[]{:S(2)}) collective-permute-start(bf16[128,512]{1,0:T(8,128)(2,1)} %rest_0_.1), channel_id=1, source_target_pairs={{0,2},{2,4},{4,6},{6,0},{1,3},{3,5},{5,7},{7,1},{8,10},{10,12},{12... | collective-permute-start | bytes 393224 | tf_op jit(solution)/shard_map/tower/ppermute | solution.py:24
  17.4 2.0 %collective-permute-start.3 = (bf16[4,128,512]{2,1,0:T(8,128)(2,1)S(1)}, bf16[4,128,512]{2,1,0:T(8,128)(2,1)S(1)}, u32[]{:S(2)}, u32[]{:S(2)}) collective-permute-start(bf16[4,128,512]{2,1,0:T(8,128)(2,1)S(1)} %pad_maximum_fusion.near), channel_id=1, source_target_pairs={{0,1},{1,0},{2,3},{3,2},{4,5},{5,4},{6,7},{7,6},{8,9},{9,8},{10,11... | collective-permute-start | bytes 1572872 | tf_op jit(solution)/shard_map/tower/ppermute | solution.py:24
  20.5 6.8 %collective-permute-start.4 = (bf16[128,512]{1,0:T(8,128)(2,1)S(1)}, bf16[128,512]{1,0:T(8,128)(2,1)S(1)}, u32[]{:S(2)}, u32[]{:S(2)}) collective-permute-start(bf16[128,512]{1,0:T(8,128)(2,1)S(1)} %tower.14), channel_id=1, source_target_pairs={{0,64},{64,128},{128,192},{192,0},{1,65},{65,129},{129,193},{193,1... | collective-permute-start | bytes 393224 | tf_op jit(solution)/shard_map/tower/ppermute | solution.py:24
  27.3 7.7 %collective-permute-start.7 = (bf16[128,512]{1,0:T(8,128)(2,1)S(1)}, bf16[128,512]{1,0:T(8,128)(2,1)S(1)}, u32[]{:S(2)}, u32[]{:S(2)}) collective-permute-start(bf16[128,512]{1,0:T(8,128)(2,1)S(1)} %collective-permute-done.4.rest_0_), channel_id=1, source_target_pairs={{0,6},{2,0},{4,2},{6,4},{1,7},{3,1},{5,3},{7,5},{8,14},{10,8},{12,... | collective-permute-start | bytes 393224 | tf_op jit(solution)/shard_map/tower/ppermute | solution.py:24
  30.2 6.5 %collective-permute-start.6 = (bf16[128,512]{1,0:T(8,128)(2,1)S(1)}, bf16[128,512]{1,0:T(8,128)(2,1)S(1)}, u32[]{:S(2)}, u32[]{:S(2)}) collective-permute-start(bf16[128,512]{1,0:T(8,128)(2,1)S(1)} %collective-permute-done.4.rest_0_), channel_id=1, source_target_pairs={{0,4},{2,6},{4,0},{6,2},{1,5},{3,7},{5,1},{7,3},{8,12},{10,14},{12... | collective-permute-start | bytes 393224 | tf_op jit(solution)/shard_map/tower/ppermute | solution.py:24
  30.2 6.5 %collective-permute-start.5 = (bf16[128,512]{1,0:T(8,128)(2,1)S(1)}, bf16[128,512]{1,0:T(8,128)(2,1)S(1)}, u32[]{:S(2)}, u32[]{:S(2)}) collective-permute-start(bf16[128,512]{1,0:T(8,128)(2,1)S(1)} %collective-permute-done.4.rest_0_), channel_id=1, source_target_pairs={{0,2},{2,4},{4,6},{6,0},{1,3},{3,5},{5,7},{7,1},{8,10},{10,12},{12... | collective-permute-start | bytes 393224 | tf_op jit(solution)/shard_map/tower/ppermute | solution.py:24
  36.8 2.0 %collective-permute-start.8 = (bf16[4,128,512]{2,1,0:T(8,128)(2,1)S(1)}, bf16[4,128,512]{2,1,0:T(8,128)(2,1)S(1)}, u32[]{:S(2)}, u32[]{:S(2)}) collective-permute-start(bf16[4,128,512]{2,1,0:T(8,128)(2,1)S(1)} %pad_maximum_fusion.1.near), channel_id=1, source_target_pairs={{0,1},{1,0},{2,3},{3,2},{4,5},{5,4},{6,7},{7,6},{8,9},{9,8},{10,11... | collective-permute-start | bytes 1572872 | tf_op jit(solution)/shard_map/tower/ppermute | solution.py:24
  39.8 6.8 %collective-permute-start.9 = (bf16[128,512]{1,0:T(8,128)(2,1)S(1)}, bf16[128,512]{1,0:T(8,128)(2,1)S(1)}, u32[]{:S(2)}, u32[]{:S(2)}) collective-permute-start(bf16[128,512]{1,0:T(8,128)(2,1)S(1)} %tower.17), channel_id=1, source_target_pairs={{0,64},{64,128},{128,192},{192,0},{1,65},{65,129},{129,193},{193,1... | collective-permute-start | bytes 393224 | tf_op jit(solution)/shard_map/tower/ppermute | solution.py:24
  46.7 8.7 %collective-permute-start.12 = (bf16[128,512]{1,0:T(8,128)(2,1)S(1)}, bf16[128,512]{1,0:T(8,128)(2,1)S(1)}, u32[]{:S(2)}, u32[]{:S(2)}) collective-permute-start(bf16[128,512]{1,0:T(8,128)(2,1)S(1)} %collective-permute-done.9.rest_0_), channel_id=1, source_target_pairs={{0,6},{2,0},{4,2},{6,4},{1,7},{3,1},{5,3},{7,5},{8,14},{10,8},{12,... | collective-permute-start | bytes 393224 | tf_op jit(solution)/shard_map/tower/ppermute | solution.py:24
  49.5 6.5 %collective-permute-start.11 = (bf16[128,512]{1,0:T(8,128)(2,1)S(1)}, bf16[128,512]{1,0:T(8,128)(2,1)S(1)}, u32[]{:S(2)}, u32[]{:S(2)}) collective-permute-start(bf16[128,512]{1,0:T(8,128)(2,1)S(1)} %collective-permute-done.9.rest_0_), channel_id=1, source_target_pairs={{0,4},{2,6},{4,0},{6,2},{1,5},{3,7},{5,1},{7,3},{8,12},{10,14},{12... | collective-permute-start | bytes 393224 | tf_op jit(solution)/shard_map/tower/ppermute | solution.py:24
  49.5 6.4 %collective-permute-start.10 = (bf16[128,512]{1,0:T(8,128)(2,1)S(1)}, bf16[128,512]{1,0:T(8,128)(2,1)S(1)}, u32[]{:S(2)}, u32[]{:S(2)}) collective-permute-start(bf16[128,512]{1,0:T(8,128)(2,1)S(1)} %collective-permute-done.9.rest_0_), channel_id=1, source_target_pairs={{0,2},{2,4},{4,6},{6,0},{1,3},{3,5},{5,7},{7,1},{8,10},{10,12},{12... | collective-permute-start | bytes 393224 | tf_op jit(solution)/shard_map/tower/ppermute | solution.py:24
  56.1 2.0 %collective-permute-start.13 = (bf16[4,128,512]{2,1,0:T(8,128)(2,1)S(1)}, bf16[4,128,512]{2,1,0:T(8,128)(2,1)S(1)}, u32[]{:S(2)}, u32[]{:S(2)}) collective-permute-start(bf16[4,128,512]{2,1,0:T(8,128)(2,1)S(1)} %pad_maximum_fusion.2.near), channel_id=1, source_target_pairs={{0,1},{1,0},{2,3},{3,2},{4,5},{5,4},{6,7},{7,6},{8,9},{9,8},{10,11... | collective-permute-start | bytes 1572872 | tf_op jit(solution)/shard_map/tower/ppermute | solution.py:24
  59.1 7.0 %collective-permute-start.14 = (bf16[128,512]{1,0:T(8,128)(2,1)S(1)}, bf16[128,512]{1,0:T(8,128)(2,1)S(1)}, u32[]{:S(2)}, u32[]{:S(2)}) collective-permute-start(bf16[128,512]{1,0:T(8,128)(2,1)S(1)} %tower.20), channel_id=1, source_target_pairs={{0,64},{64,128},{128,192},{192,0},{1,65},{65,129},{129,193},{193,1... | collective-permute-start | bytes 393224 | tf_op jit(solution)/shard_map/tower/ppermute | solution.py:24
  66.1 8.1 %collective-permute-start.17 = (bf16[128,512]{1,0:T(8,128)(2,1)S(1)}, bf16[128,512]{1,0:T(8,128)(2,1)S(1)}, u32[]{:S(2)}, u32[]{:S(2)}) collective-permute-start(bf16[128,512]{1,0:T(8,128)(2,1)S(1)} %collective-permute-done.14.rest_0_), channel_id=1, source_target_pairs={{0,6},{2,0},{4,2},{6,4},{1,7},{3,1},{5,3},{7,5},{8,14},{10,8},{12,... | collective-permute-start | bytes 393224 | tf_op jit(solution)/shard_map/tower/ppermute | solution.py:24
  69.3 6.5 %collective-permute-start.16 = (bf16[128,512]{1,0:T(8,128)(2,1)S(1)}, bf16[128,512]{1,0:T(8,128)(2,1)S(1)}, u32[]{:S(2)}, u32[]{:S(2)}) collective-permute-start(bf16[128,512]{1,0:T(8,128)(2,1)S(1)} %collective-permute-done.14.rest_0_), channel_id=1, source_target_pairs={{0,4},{2,6},{4,0},{6,2},{1,5},{3,7},{5,1},{7,3},{8,12},{10,14},{12... | collective-permute-start | bytes 393224 | tf_op jit(solution)/shard_map/tower/ppermute | solution.py:24
  69.4 6.5 %collective-permute-start.15 = (bf16[128,512]{1,0:T(8,128)(2,1)S(1)}, bf16[128,512]{1,0:T(8,128)(2,1)S(1)}, u32[]{:S(2)}, u32[]{:S(2)}) collective-permute-start(bf16[128,512]{1,0:T(8,128)(2,1)S(1)} %collective-permute-done.14.rest_0_), channel_id=1, source_target_pairs={{0,2},{2,4},{4,6},{6,0},{1,3},{3,5},{5,7},{7,1},{8,10},{10,12},{12... | collective-permute-start | bytes 393224 | tf_op jit(solution)/shard_map/tower/ppermute | solution.py:24
  75.9 2.0 %collective-permute-start.18 = (bf16[4,128,512]{2,1,0:T(8,128)(2,1)S(1)}, bf16[4,128,512]{2,1,0:T(8,128)(2,1)S(1)}, u32[]{:S(2)}, u32[]{:S(2)}) collective-permute-start(bf16[4,128,512]{2,1,0:T(8,128)(2,1)S(1)} %pad_maximum_fusion.3.near), channel_id=1, source_target_pairs={{0,1},{1,0},{2,3},{3,2},{4,5},{5,4},{6,7},{7,6},{8,9},{9,8},{10,11... | collective-permute-start | bytes 1572872 | tf_op jit(solution)/shard_map/tower/ppermute | solution.py:24
  79.0 2.7 %collective-permute-start.21 = (bf16[128,512]{1,0:T(8,128)(2,1)S(1)}, bf16[128,512]{1,0:T(8,128)(2,1)S(1)}, u32[]{:S(2)}, u32[]{:S(2)}) collective-permute-start(bf16[128,512]{1,0:T(8,128)(2,1)S(1)} %tower.23), channel_id=1, source_target_pairs={{192,128},{193,129},{194,130},{195,131},{196,132},{197,133},{198,1... | collective-permute-start | bytes 393224 | tf_op jit(solution)/shard_map/to_sections/ppermute | solution.py:317
  80.3 8.6 %collective-permute-start.19 = (bf16[128,512]{1,0:T(8,128)(2,1)S(1)}, bf16[128,512]{1,0:T(8,128)(2,1)S(1)}, u32[]{:S(2)}, u32[]{:S(2)}) collective-permute-start(bf16[128,512]{1,0:T(8,128)(2,1)S(1)} %tower.23), channel_id=1, source_target_pairs={{192,0},{193,1},{194,2},{195,3},{196,4},{197,5},{198,6},{199,7},{2... | collective-permute-start | bytes 393224 | tf_op jit(solution)/shard_map/to_sections/ppermute | solution.py:317
  89.0 8.0 %collective-permute-start.24 = (bf16[128,512]{1,0:T(8,128)(2,1)S(1)}, bf16[128,512]{1,0:T(8,128)(2,1)S(1)}, u32[]{:S(2)}, u32[]{:S(2)}) collective-permute-start(bf16[128,512]{1,0:T(8,128)(2,1)S(1)} %add_add_fusion.rest_0_), channel_id=1, source_target_pairs={{0,6},{2,0},{4,2},{6,4},{1,7},{3,1},{5,3},{7,5},{8,14},{10,8},{12,... | collective-permute-start | bytes 393224 | tf_op jit(solution)/shard_map/head/ppermute | solution.py:24
  92.0 6.5 %collective-permute-start.23 = (bf16[128,512]{1,0:T(8,128)(2,1)S(1)}, bf16[128,512]{1,0:T(8,128)(2,1)S(1)}, u32[]{:S(2)}, u32[]{:S(2)}) collective-permute-start(bf16[128,512]{1,0:T(8,128)(2,1)S(1)} %add_add_fusion.rest_0_), channel_id=1, source_target_pairs={{0,4},{2,6},{4,0},{6,2},{1,5},{3,7},{5,1},{7,3},{8,12},{10,14},{12... | collective-permute-start | bytes 393224 | tf_op jit(solution)/shard_map/head/ppermute | solution.py:24
  92.0 6.5 %collective-permute-start.22 = (bf16[128,512]{1,0:T(8,128)(2,1)S(1)}, bf16[128,512]{1,0:T(8,128)(2,1)S(1)}, u32[]{:S(2)}, u32[]{:S(2)}) collective-permute-start(bf16[128,512]{1,0:T(8,128)(2,1)S(1)} %add_add_fusion.rest_0_), channel_id=1, source_target_pairs={{0,2},{2,4},{4,6},{6,0},{1,3},{3,5},{5,7},{7,1},{8,10},{10,12},{12... | collective-permute-start | bytes 393224 | tf_op jit(solution)/shard_map/head/ppermute | solution.py:24
  98.5 2.0 %collective-permute-start.25 = (bf16[4,128,512]{2,1,0:T(8,128)(2,1)S(1)}, bf16[4,128,512]{2,1,0:T(8,128)(2,1)S(1)}, u32[]{:S(2)}, u32[]{:S(2)}) collective-permute-start(bf16[4,128,512]{2,1,0:T(8,128)(2,1)S(1)} %pad_maximum_fusion.4.near), channel_id=1, source_target_pairs={{0,1},{1,0},{2,3},{3,2},{4,5},{5,4},{6,7},{7,6},{8,9},{9,8},{10,11... | collective-permute-start | bytes 1572872 | tf_op jit(solution)/shard_map/head/ppermute | solution.py:24
  102.6 22.0 %all-to-all-start = ((bf16[8,32,640]{2,1,0:T(8,128)(2,1)}), bf16[8,32,640]{2,1,0:T(8,128)(2,1)S(1)}, u32[]{:S(2)}, u32[]{:S(2)}) async-start(bf16[8,32,640]{2,1,0:T(8,128)(2,1)} %get-tuple-element.86), calls=%async_computation | async-start | bytes 655360 | tf_op jit(solution)/shard_map/normed_home/all_to_all | solution.py:332
  111.1 76.3 %reduce-scatter.2.cloned.1.call-start = ((), (), s32[]{:S(2)}) async-start(), calls=%async_computation.7 | async-start | bytes 1179648 | tf_op jit(solution)/shard_map/passage_grads/reduce_scatter | solution.py:362
  111.1 7.2 %collective-permute-start.28 = (bf16[128,512]{1,0:T(8,128)(2,1)S(1)}, bf16[128,512]{1,0:T(8,128)(2,1)S(1)}, u32[]{:S(2)}, u32[]{:S(2)}) collective-permute-start(bf16[128,512]{1,0:T(8,128)(2,1)S(1)} %get-tuple-element.87), channel_id=1, source_target_pairs={{0,6},{2,0},{4,2},{6,4},{1,7},{3,1},{5,3},{7,5},{8,14},{10,8},{12,... | collective-permute-start | bytes 393224 | tf_op jit(solution)/shard_map/score/ppermute | solution.py:24
  114.4 6.5 %collective-permute-start.27 = (bf16[128,512]{1,0:T(8,128)(2,1)S(1)}, bf16[128,512]{1,0:T(8,128)(2,1)S(1)}, u32[]{:S(2)}, u32[]{:S(2)}) collective-permute-start(bf16[128,512]{1,0:T(8,128)(2,1)S(1)} %get-tuple-element.87), channel_id=1, source_target_pairs={{0,4},{2,6},{4,0},{6,2},{1,5},{3,7},{5,1},{7,3},{8,12},{10,14},{12... | collective-permute-start | bytes 393224 | tf_op jit(solution)/shard_map/score/ppermute | solution.py:24
  114.4 6.7 %collective-permute-start.26 = (bf16[128,512]{1,0:T(8,128)(2,1)S(1)}, bf16[128,512]{1,0:T(8,128)(2,1)S(1)}, u32[]{:S(2)}, u32[]{:S(2)}) collective-permute-start(bf16[128,512]{1,0:T(8,128)(2,1)S(1)} %get-tuple-element.87), channel_id=1, source_target_pairs={{0,2},{2,4},{4,6},{6,0},{1,3},{3,5},{5,7},{7,1},{8,10},{10,12},{12... | collective-permute-start | bytes 393224 | tf_op jit(solution)/shard_map/score/ppermute | solution.py:24
  141.8 2.2 %collective-permute-start.30 = (bf16[4,4,32,512]{3,2,1,0:T(8,128)(2,1)S(1)}, bf16[4,4,32,512]{3,2,1,0:T(8,128)(2,1)}, u32[]{:S(2)}, u32[]{:S(2)}) collective-permute-start(bf16[4,4,32,512]{3,2,1,0:T(8,128)(2,1)S(1)} %get-tuple-element.98), channel_id=1, source_target_pairs={{0,1},{1,0},{2,3},{3,2},{4,5},{5,4},{6,7},{7,6},{8,9},{9,8},{10,11... | collective-permute-start | bytes 1572872 | tf_op jit(solution)/shard_map/query_grad/ppermute | solution.py:24
  (10 other events, 219.9 us)
Sparse Core Ops, SparseCore 0:
  12.4 40.1 all-gather.1
  144.2 35.4 reduce-scatter.1
